TPU v7x, 128 devices: a whole 4x4x4 slice. The times are simulated.
128 devices in a mesh: heads: 8 (over y, core), seq: 16 (over x, z).
Axes of the slice: x: 4, y: 4, z: 4, core: 2. Of those that a mesh axis runs over, the one named last changes fastest.
Arguments:
- hidden: bfloat16 [2048, 7168], P('seq', 'heads')
- norm_gain: float32 [7168], P('heads'), may hold values from 0.5 to 1.5
- beam_src: int32 [2048], P('seq'), may hold values from 0 to 2047, as said below
- route_ids: int32 [2048, 8], P('seq'), may hold values from 0 to 255, as said below
- route_slots: int32 [2048, 8], P('seq'), may hold values from -1 to 15, as said below
- route_gates: float32 [2048, 8], P('seq'), may hold values from 0.1 to 1
- w_gate: bfloat16 [16, 7168, 2048], P('seq', None, 'heads'), may hold values from -0.0625 to 0.0625
- w_up: bfloat16 [16, 7168, 2048], P('seq', None, 'heads'), may hold values from -0.0625 to 0.0625
- w_down: bfloat16 [16, 2048, 7168], P('seq', 'heads'), may hold values from -0.1875 to 0.1875
- out_grad: bfloat16 [2048, 7168], P('seq', 'heads'), may hold values from -6 to 6
Outputs:
- moe_out: bfloat16 [2048, 7168], P('seq', 'heads')
- grad_hidden: bfloat16 [2048, 7168], P('seq', 'heads')
- grad_gates: float32 [2048, 8], P('seq')
- grad_w_gate: bfloat16 [16, 7168, 2048], P('seq', None, 'heads')
- grad_w_up: bfloat16 [16, 7168, 2048], P('seq', None, 'heads')
- grad_w_down: bfloat16 [16, 2048, 7168], P('seq', 'heads')
Inputs may be any that keep to these rules, and one draw needn't show every extreme that they name: beam_src[t] lies in the aligned group of 8 rows that holds t. `route_ids`: each row names 8 different experts of the model's 256; every expert below 16 is named in every aligned block of 128 rows. `route_slots`: in each aligned block of 128 rows, the routes that name one expert e below 16 carry the slots 0 to n - 1, each once, with n at most 16; in every draw one expert below 16 has n = 16 in every block. A route to an expert of 16 or above has slot -1.
All inputs are finite; a program needn't handle non-finite values.
Results may differ from a plain program's by a relative error of at most 0.0073.
Values may be sent and summed in bfloat16 or wider, within the bound.
No kernel may reach another device: no remote copies, remote signals or barrier semaphores. Data moves between devices by JAX's collectives and lax.ppermute only.
A program may use at most 128 MiB of HBM per device.

v0:
```python
import jax
import jax.numpy as jnp
from jax import lax
from jax.sharding import PartitionSpec as P

D = 7168
CAP = 8


epsilon = 1e-06


def feature_sum(values):
    return lax.psum(values, "heads")


def to_experts(buffer):
    seq_size = lax.axis_size("seq")
    head_count = lax.axis_size("heads")
    expert_count, capacity, feat_width = buffer.shape
    copies = jnp.broadcast_to(buffer[None], (head_count, expert_count, capacity, feat_width))
    copies = copies.reshape(head_count * expert_count, capacity, feat_width)
    received = lax.all_to_all(copies, ("heads", "seq"), split_axis=0, concat_axis=0, tiled=True)
    received = received.reshape(head_count, seq_size, capacity, feat_width).transpose(1, 2, 0, 3)
    return received.reshape(seq_size * capacity, head_count * feat_width)


def from_experts(term_rows, capacity):
    seq_size = lax.axis_size("seq")
    head_count = lax.axis_size("heads")
    feat_width = term_rows.shape[1] // head_count
    pieces = term_rows.reshape(seq_size, capacity, head_count, feat_width).transpose(2, 0, 1, 3)
    pieces = pieces.reshape(head_count * seq_size, capacity, feat_width)
    received = lax.all_to_all(pieces, ("heads", "seq"), split_axis=0, concat_axis=0, tiled=True)
    summed = jnp.sum(received.reshape(head_count, seq_size, capacity, feat_width), axis=0)
    return summed.astype(jnp.bfloat16)


def on_device(
    hidden, norm_gain, beam_src, route_ids, route_slots, route_gates, w_gate, w_up, w_down, out_grad
):
    row_count, feat_width = hidden.shape
    seq_size = lax.axis_size("seq")
    capacity = CAP
    slot_count = seq_size * capacity
    highest = lax.Precision.HIGHEST
    contract_rows = (((0,), (0,)), ((), ()))
    contract_cols = (((1,), (1,)), ((), ()))
    parent_rows = beam_src - lax.axis_index("seq") * row_count
    beam_rows = hidden[parent_rows].astype(jnp.float32)
    square_sum = feature_sum(jnp.sum(beam_rows * beam_rows, axis=1))
    inverse = lax.rsqrt(square_sum / D + epsilon)
    normed = (beam_rows * inverse[:, None] * norm_gain[None, :]).astype(jnp.bfloat16)
    in_window = (route_ids < seq_size) & (route_slots >= 0) & (route_slots < capacity)
    target = jnp.where(in_window, route_ids * capacity + route_slots, slot_count)
    one_hot = target[:, :, None] == jnp.arange(slot_count, dtype=jnp.int32)[None, None, :]
    pick_matrix = jnp.any(one_hot, axis=1).astype(jnp.bfloat16)
    mixing = jnp.sum(jnp.where(one_hot, route_gates[:, :, None], 0.0), axis=1)
    send_rows = lax.dot_general(
        pick_matrix, normed, contract_rows, preferred_element_type=jnp.float32
    )
    inputs = to_experts(send_rows.astype(jnp.bfloat16).reshape(seq_size, capacity, feat_width))
    gate_slice = w_gate[0]
    up_slice = w_up[0]
    down_slice = w_down[0]
    pre_gate = jnp.dot(inputs, gate_slice, preferred_element_type=jnp.float32)
    pre_up = jnp.dot(inputs, up_slice, preferred_element_type=jnp.float32)
    sigmoid_gate = jax.nn.sigmoid(pre_gate)
    activated = pre_gate * sigmoid_gate
    hidden_act = (activated * pre_up).astype(jnp.bfloat16)
    outputs = from_experts(
        jnp.dot(hidden_act, down_slice, preferred_element_type=jnp.float32), capacity
    )
    out_rows = outputs.reshape(slot_count, feat_width).astype(jnp.float32)
    moe_out = jnp.dot(mixing, out_rows, precision=highest).astype(jnp.bfloat16)
    cot_rows = out_grad.astype(jnp.float32)
    scores = jnp.dot(cot_rows, out_rows.T, precision=highest)
    gate_part = jnp.sum(jnp.where(one_hot, scores[:, None, :], 0.0), axis=2)
    grad_gates = feature_sum(gate_part)
    slot_grad = lax.dot_general(mixing, cot_rows, contract_rows, precision=highest).astype(
        jnp.bfloat16
    )
    out_cot = to_experts(slot_grad.reshape(seq_size, capacity, feat_width))
    hid_grad = lax.dot_general(
        out_cot, down_slice, contract_cols, preferred_element_type=jnp.float32
    )
    grad_down = lax.dot_general(
        hidden_act, out_cot, contract_rows, preferred_element_type=jnp.float32
    ).astype(jnp.bfloat16)
    grad_pre_gate = (
        hid_grad * pre_up * sigmoid_gate * (1.0 + pre_gate * (1.0 - sigmoid_gate))
    ).astype(jnp.bfloat16)
    grad_pre_up = (hid_grad * activated).astype(jnp.bfloat16)
    grad_gate_w = lax.dot_general(
        inputs, grad_pre_gate, contract_rows, preferred_element_type=jnp.float32
    ).astype(jnp.bfloat16)
    grad_up_w = lax.dot_general(
        inputs, grad_pre_up, contract_rows, preferred_element_type=jnp.float32
    ).astype(jnp.bfloat16)
    in_term = lax.dot_general(
        grad_pre_gate, gate_slice, contract_cols, preferred_element_type=jnp.float32
    ) + lax.dot_general(grad_pre_up, up_slice, contract_cols, preferred_element_type=jnp.float32)
    in_grad = from_experts(in_term, capacity)
    back_rows = jnp.dot(
        pick_matrix, in_grad.reshape(slot_count, feat_width), preferred_element_type=jnp.float32
    )
    gained = back_rows * norm_gain[None, :]
    gain_dot = feature_sum(jnp.sum(gained * beam_rows, axis=1))
    beam_grad = (
        inverse[:, None] * gained
        - beam_rows * (inverse * inverse * inverse * gain_dot / D)[:, None]
    )
    grad_hidden = jax.ops.segment_sum(beam_grad, parent_rows, num_segments=row_count).astype(
        jnp.bfloat16
    )
    return (moe_out, grad_hidden, grad_gates, grad_gate_w[None], grad_up_w[None], grad_down[None])


def solution(mesh):
    return jax.shard_map(
        on_device,
        mesh=mesh,
        in_specs=(
            P("seq", "heads"),
            P("heads"),
            P("seq"),
            P("seq", None),
            P("seq", None),
            P("seq", None),
            P("seq", None, "heads"),
            P("seq", None, "heads"),
            P("seq", "heads", None),
            P("seq", "heads"),
        ),
        out_specs=(
            P("seq", "heads"),
            P("seq", "heads"),
            P("seq", None),
            P("seq", None, "heads"),
            P("seq", None, "heads"),
            P("seq", "heads", None),
        ),
        check_vma=False,
    )
```

profile of v0, /device:TPU:0, one launch (start us, length us, event | category | flops | bytes accessed | tf_op | source)
XLA Modules:
  0.0 245.9 jit_solution(10383101270319558958)
XLA Ops:
  0.7 0.7 add_select_fusion
  2.4 2.0 gather_fusion
  4.6 14.9 %psum.21 = f32[128]{0:T(128)S(1)} all-reduce(f32[128]{0:T(128)S(1)} %fusion.15), channel_id=1, replica_groups=mesh['heads'=8,'seq'=16] {'heads'}, use_global_device_ids=true, to_apply=%region_3.4 | all-reduce | flops 128 | bytes 1024 | tf_op jit(solution)/shard_map/psum | solution.py:14
  19.5 1.0 fusion.12
  20.5 1.5 broadcast_in_dim.72
  22.0 8.4 %all-to-all-start = ((bf16[128,8,896]{2,1,0:T(8,128)(2,1)}), bf16[128,8,896]{2,1,0:T(8,128)(2,1)S(1)}, u32[]{:S(2)}, u32[]{:S(2)}) async-start(bf16[128,8,896]{2,1,0:T(8,128)(2,1)} %bitcast.109), calls=%async_computation | async-start | bytes 3670016 | tf_op jit(solution)/shard_map/all_to_all | solution.py:23
  30.4 5.9 %copy.44 = bf16[7168,256]{1,0:T(8,128)(2,1)} copy(bf16[7168,256]{0,1:T(8,128)(2,1)} %bitcast.105) | data formatting | bytes 7340032 | tf_op jit(solution)/shard_map/dot_general | solution.py:72
  36.3 21.2 %all-to-all-done = bf16[128,8,896]{2,1,0:T(8,128)(2,1)S(1)} async-done(((bf16[128,8,896]{2,1,0:T(8,128)(2,1)}), bf16[128,8,896]{2,1,0:T(8,128)(2,1)S(1)}, u32[]{:S(2)}, u32[]{:S(2)}) %all-to-all-start) | async-done | bytes 1835040 | tf_op jit(solution)/shard_map/all_to_all | solution.py:23
  57.5 1.0 copy.50
  60.2 0.8 copy-done.7
  61.7 1.3 copy-done.3
  63.1 1.3 convolution_bitcast_fusion
  64.4 2.1 copy.38
  66.5 5.9 %all-to-all-start.1 = ((f32[128,8,896]{2,1,0:T(8,128)}), f32[128,8,896]{2,1,0:T(8,128)}, u32[]{:S(2)}, u32[]{:S(2)}) async-start(f32[128,8,896]{2,1,0:T(8,128)} %bitcast.104), calls=%async_computation.1 | async-start | bytes 7340032 | tf_op jit(solution)/shard_map/all_to_all | solution.py:34
  72.5 45.8 %all-to-all-done.1 = f32[128,8,896]{2,1,0:T(8,128)} async-done(((f32[128,8,896]{2,1,0:T(8,128)}), f32[128,8,896]{2,1,0:T(8,128)}, u32[]{:S(2)}, u32[]{:S(2)}) %all-to-all-start.1) | async-done | bytes 3670048 | tf_op jit(solution)/shard_map/all_to_all | solution.py:34
  118.3 2.2 reduce_sum.56
  122.1 31.8 %all_to_all.20 = bf16[128,8,896]{2,1,0:T(8,128)(2,1)S(1)} all-to-all(bf16[128,8,896]{2,1,0:T(8,128)(2,1)S(1)} %bitcast.110), channel_id=1, replica_groups=mesh['heads'=8,'seq'=16] {'heads','seq'}, dimensions={0} | all-to-all | bytes 3670016 | tf_op jit(solution)/shard_map/all_to_all | solution.py:23
  153.9 1.0 copy.49
  155.3 1.2 copy-done.2
  156.5 1.3 multiply_convert_fusion
  158.2 1.3 fusion.8
  160.2 1.3 convolution_add_fusion
  161.5 2.1 copy.40
  163.6 5.7 %all-to-all-start.3 = ((f32[128,8,896]{2,1,0:T(8,128)}), f32[128,8,896]{2,1,0:T(8,128)}, u32[]{:S(2)}, u32[]{:S(2)}) async-start(f32[128,8,896]{2,1,0:T(8,128)} %bitcast.102), calls=%async_computation.3 | async-start | bytes 7340032 | tf_op jit(solution)/shard_map/all_to_all | solution.py:34
  169.4 1.0 convolution_convert_fusion.4
  170.4 4.5 %fusion.2 = bf16[1,256,7168]{2,1,0:T(8,128)(2,1)} fusion(bf16[128,256]{1,0:T(8,128)(2,1)S(1)} %get-tuple-element.20, bf16[128,7168]{1,0:T(8,128)(2,1)} %bitcast.101), kind=kOutput, calls=%fused_computation.7 | convolution fusion | flops 471597056 | bytes 5570560 | tf_op jit(solution)/shard_map/dot_general | solution.py:87
  174.9 3.0 %fusion = bf16[1,7168,256]{2,1,0:T(8,128)(2,1)} fusion(bf16[128,7168]{1,0:T(8,128)(2,1)S(1)} %bitcast.98, bf16[128,256]{1,0:T(8,128)(2,1)S(1)} %get-tuple-element.19), kind=kOutput, calls=%fused_computation.5 | convolution fusion | flops 471597056 | bytes 5570560 | tf_op jit(solution)/shard_map/dot_general | solution.py:94
  177.9 3.0 %fusion.1 = bf16[1,7168,256]{2,1,0:T(8,128)(2,1)} fusion(bf16[128,7168]{1,0:T(8,128)(2,1)S(1)} %bitcast.99, bf16[128,256]{1,0:T(8,128)(2,1)S(1)} %get-tuple-element.18), kind=kOutput, calls=%fused_computation.6 | convolution fusion | flops 471597056 | bytes 5570560 | tf_op jit(solution)/shard_map/dot_general | solution.py:97
  180.9 34.5 %all-to-all-done.3 = f32[128,8,896]{2,1,0:T(8,128)} async-done(((f32[128,8,896]{2,1,0:T(8,128)}), f32[128,8,896]{2,1,0:T(8,128)}, u32[]{:S(2)}, u32[]{:S(2)}) %all-to-all-start.3) | async-done | bytes 3670048 | tf_op jit(solution)/shard_map/all_to_all | solution.py:34
  215.3 2.2 reduce_sum.57
  217.9 24.8 %all-reduce = (f32[128]{0:T(128)S(1)}, f32[128,8]{1,0:T(8,128)S(1)}) all-reduce(f32[128]{0:T(128)S(1)} %get-tuple-element.22, f32[128,8]{1,0:T(8,128)S(1)} %get-tuple-element.12), channel_id=1, replica_groups=mesh['heads'=8,'seq'=16] {'heads'}, use_global_device_ids=true, to_apply=%region_7.8 | all-reduce | flops 1152 | bytes 9216 | tf_op jit(solution)/shard_map/psum | solution.py:14
  242.7 1.8 scatter_custom_fusion
  (39 shorter events, 8.2 us)
Async XLA Ops:
  0.6 119.9 %copy-start = (bf16[128,896]{1,0:T(8,128)(2,1)S(1)}, bf16[128,896]{1,0:T(8,128)(2,1)}, u32[]{:S(2)}) copy-start(bf16[128,896]{1,0:T(8,128)(2,1)} %param.19) | copy-start | bytes 688132
  22.0 35.5 %all-to-all-start = ((bf16[128,8,896]{2,1,0:T(8,128)(2,1)}), bf16[128,8,896]{2,1,0:T(8,128)(2,1)S(1)}, u32[]{:S(2)}, u32[]{:S(2)}) async-start(bf16[128,8,896]{2,1,0:T(8,128)(2,1)} %bitcast.109), calls=%async_computation | async-start | bytes 3670016 | tf_op jit(solution)/shard_map/all_to_all | solution.py:23
  57.5 2.0 copy-start.5
  58.8 2.2 copy-start.7
  61.1 2.0 copy-start.3
  66.5 5.9 %copy-start.10 = (f32[128,8]{0,1:T(8,128)S(1)}, f32[128,8]{0,1:T(8,128)}, u32[]{:S(2)}) copy-start(f32[128,8]{0,1:T(8,128)} %param.15) | copy-start | bytes 12292
  66.5 51.8 %all-to-all-start.1 = ((f32[128,8,896]{2,1,0:T(8,128)}), f32[128,8,896]{2,1,0:T(8,128)}, u32[]{:S(2)}, u32[]{:S(2)}) async-start(f32[128,8,896]{2,1,0:T(8,128)} %bitcast.104), calls=%async_computation.1 | async-start | bytes 7340032 | tf_op jit(solution)/shard_map/all_to_all | solution.py:34
  153.9 2.6 %copy-start.4 = (bf16[1,256,7168]{2,1,0:T(8,128)(2,1)S(1)}, bf16[1,256,7168]{2,1,0:T(8,128)(2,1)}, u32[]{:S(2)}) copy-start(bf16[1,256,7168]{2,1,0:T(8,128)(2,1)} %param.18) | copy-start | bytes 11010052
  155.3 1.2 copy-start.2
  155.3 2.9 %copy-start.6 = (bf16[1,7168,256]{2,1,0:T(8,128)(2,1)S(1)}, bf16[1,7168,256]{2,1,0:T(8,128)(2,1)}, u32[]{:S(2)}) copy-start(bf16[1,7168,256]{2,1,0:T(8,128)(2,1)} %param.16) | copy-start | bytes 11010052
  158.2 2.0 copy-start.8
  163.6 51.7 %all-to-all-start.3 = ((f32[128,8,896]{2,1,0:T(8,128)}), f32[128,8,896]{2,1,0:T(8,128)}, u32[]{:S(2)}, u32[]{:S(2)}) async-start(f32[128,8,896]{2,1,0:T(8,128)} %bitcast.102), calls=%async_computation.3 | async-start | bytes 7340032 | tf_op jit(solution)/shard_map/all_to_all | solution.py:34
  177.9 39.7 %copy-start.9 = (f32[896]{0:T(1024)S(1)}, f32[896]{0:T(1024)}, u32[]{:S(2)}) copy-start(f32[896]{0:T(1024)} %param.11) | copy-start | bytes 10756
  177.9 68.1 %copy-start.1 = (bf16[128,896]{1,0:T(8,128)(2,1)S(1)}, bf16[128,896]{1,0:T(8,128)(2,1)}, u32[]{:S(2)}) copy-start(bf16[128,896]{1,0:T(8,128)(2,1)} %param.19) | copy-start | bytes 688132
where the time goes:
time: 247 us; the launch traced here: 246 us
  waiting for transfers between devices  101 us (41%)
  blocking collectives  71.6 us (29%)
  local copies, waits for them, and re-layouts  22.5 us (9%)
  matrix products  20.1 us (8%)
  starting transfers between devices  20.1 us (8%)
  other arithmetic  9.34 us (4%)
    all_to_all x2, waiting for transfers between devices, from_experts(): lax.all_to_all(pieces, ('heads', 'seq'), split_axis=0, concat_axis=0, til...  80.3 us
    psum x2, blocking collectives, feature_sum(): return lax.psum(values, 'heads')  39.8 us
    all_to_all x1, blocking collectives, to_experts(): lax.all_to_all(copies, ('heads', 'seq'), split_axis=0, concat_axis=0, til...  31.8 us
    all_to_all x1, waiting for transfers between devices, to_experts(): lax.all_to_all(copies, ('heads', 'seq'), split_axis=0, concat_axis=0, til...  21.2 us
    all_to_all x2, starting transfers between devices, from_experts(): lax.all_to_all(pieces, ('heads', 'seq'), split_axis=0, concat_axis=0, til...  11.6 us
    all_to_all x1, starting transfers between devices, to_experts(): lax.all_to_all(copies, ('heads', 'seq'), split_axis=0, concat_axis=0, til...  8.43 us
    unnamed x26, local copies, waits for them, and re-layouts  6.48 us
    dot_general x1, local copies, waits for them, and re-layouts, on_device(): jnp.dot(hidden_act, down_slice, preferred_element_type=jnp.float32)  5.92 us
  transfers between devices with their start and end apart: 3, of which 3 were waited for; matrix products, arithmetic and copies ran while one was open for 7% of the time, Pallas kernels for 0%

commit v1 on v0

v1 whole, which is shorter than its diff:
```python
import jax
import jax.numpy as jnp
from jax import lax
from jax.experimental import pallas as pl
from jax.experimental.pallas import tpu as pltpu
from jax.sharding import Mesh, PartitionSpec as P

D = 7168
CAP = 8
ROWS = 128
FEAT = 896
WIDE = 1024
HID = 256
EPSILON = 1e-06
GATHERED = (0, 3, 1, 2)
HOMEWARD = (0, 1, 3, 2)

f32 = jnp.float32
bf16 = jnp.bfloat16
VMEM = pltpu.VMEM
HBM = "hbm"
RESULT = "result"


def nn(a, b):
    return lax.dot_general(a, b, (((1,), (0,)), ((), ())), preferred_element_type=f32)


def nt(a, b):
    return lax.dot_general(a, b, (((1,), (1,)), ((), ())), preferred_element_type=f32)


def tn(a, b):
    return lax.dot_general(a, b, (((0,), (0,)), ((), ())), preferred_element_type=f32)


def local_call(kernel, inputs, outputs, mib, cost, scalars=0, scratch=()):
    in_specs, args = [], []
    for i, value in enumerate(inputs):
        if i < scalars:
            in_specs.append(pl.BlockSpec(memory_space=pltpu.SMEM))
            args.append(value)
        else:
            in_specs.append(pl.BlockSpec(memory_space=VMEM))
            args.append(pltpu.with_memory_space_constraint(value, VMEM))
    out_shape, out_specs = [], []
    for shape, dtype, space in outputs:
        out_shape.append(space(shape, dtype) if space is VMEM else jax.ShapeDtypeStruct(shape, dtype))
        out_specs.append(pl.BlockSpec(memory_space=pl.ANY if space is HBM else VMEM))
    return pl.pallas_call(
        kernel,
        out_shape=out_shape,
        in_specs=in_specs,
        out_specs=out_specs,
        scratch_shapes=list(scratch),
        compiler_params=pltpu.CompilerParams(vmem_limit_bytes=mib * 2**20),
        cost_estimate=pl.CostEstimate(flops=cost[0], bytes_accessed=cost[1], transcendentals=0),
    )(*args)


def split_two(value):
    high = value.astype(bf16)
    low = (value - high.astype(f32)).astype(bf16)
    return high, low


def slot_matches(ids, slots):
    live = (ids < 16) & (slots >= 0) & (slots < CAP)
    target = jnp.where(live, ids * CAP + slots, ROWS)
    slot = lax.broadcasted_iota(jnp.int32, (ROWS, ROWS), 0)
    return live, [slot == target[k : k + 1, :] for k in range(8)]


def pick_rows(matches, parent):
    pick = matches[0]
    for match in matches[1:]:
        pick = pick | match
    pick = jnp.where(pick, 1.0, 0.0).astype(bf16)
    row = lax.broadcasted_iota(jnp.int32, (ROWS, ROWS), 0)
    from_parent = jnp.where(row == parent, 1.0, 0.0).astype(bf16)
    return pick, nt(pick, from_parent).astype(bf16)


def mix_of(matches, gates):
    mix = jnp.zeros((ROWS, ROWS), f32)
    for k, match in enumerate(matches):
        mix = mix + jnp.where(match, gates[k : k + 1, :], 0.0)
    return mix


def prepare(hidden, gain, source, ids, slots, gates, cotangent, rows_x, rows_g):
    _, matches = slot_matches(ids[...], slots[...])
    pick, select = pick_rows(matches, source[...] & (ROWS - 1))
    gate = jnp.sum(mix_of(matches, gates[...]), axis=1, keepdims=True)
    beam = nn(select, hidden[...])
    rows_x[:, :FEAT] = (beam * gain[...]).astype(bf16)
    square = jnp.sum(beam * beam, axis=1, keepdims=True) * (1.0 / D)
    high, low = split_two(square)
    lane = lax.broadcasted_iota(jnp.int32, (ROWS, WIDE - FEAT), 1)
    tail = jnp.where(lane == 0, high.astype(f32), jnp.where(lane == 1, low.astype(f32), 0.0))
    rows_x[:, FEAT:] = tail.astype(bf16)
    rows_g[...] = (nn(pick, cotangent[...]) * gate).astype(bf16)


def block_of(refs, core, i):
    near, near_other, far, far_other = refs
    if i == 0:
        return (near, near_other)[core]
    return (far[i - 1], far_other.at[i - 1])[core]


def forward(where, x0, s0, x1, x2, x3, s123, w_gate, w_up, w_down, pre_gate, pre_up, act, scale, own, other):
    y, core = where[0], where[1]
    refs = (x0, s0, (x1, x2, x3), s123)
    mean = jnp.zeros((ROWS, WIDE - FEAT), f32)
    gate = jnp.zeros((ROWS, HID), f32)
    up = jnp.zeros((ROWS, HID), f32)
    for side in range(2):
        for i, offset in enumerate(GATHERED):
            block = block_of(refs, side, i)
            head = lax.rem(y + offset, 4) * 2 + (core if side == 0 else 1 - core)
            rows = pl.ds(pl.multiple_of(head * FEAT, FEAT), FEAT)
            mean = mean + block[:, FEAT:].astype(f32)
            gate = gate + nn(block[:, :FEAT], w_gate[0, rows, :])
            up = up + nn(block[:, :FEAT], w_up[0, rows, :])
    inverse = lax.rsqrt(jnp.sum(mean, axis=1, keepdims=True) + EPSILON)
    gate = gate * inverse
    up = up * inverse
    hidden_act = (gate * jax.nn.sigmoid(gate) * up).astype(bf16)
    pre_gate[...] = gate
    pre_up[...] = up
    act[...] = hidden_act
    scale[...] = jnp.broadcast_to(inverse, (ROWS, 128))
    for side, result in ((1, other), (0, own)):
        for i, offset in enumerate(HOMEWARD):
            head = lax.rem(y + offset, 4) * 2 + (core if side == 0 else 1 - core)
            columns = pl.ds(pl.multiple_of(head * FEAT, 128), FEAT)
            result[i] = nn(hidden_act, w_down[0, :, columns]).astype(bf16)


def backward(
    where, g0, s0, g1, g2, g3, s123, w_gate, w_up, w_down, pre_gate, pre_up, act, scale, grad_gate, grad_up, own, other
):
    y, core = where[0], where[1]
    refs = (g0, s0, (g1, g2, g3), s123)
    hid = jnp.zeros((ROWS, HID), f32)
    for side in range(2):
        for i, offset in enumerate(GATHERED):
            block = block_of(refs, side, i)
            head = lax.rem(y + offset, 4) * 2 + (core if side == 0 else 1 - core)
            columns = pl.ds(pl.multiple_of(head * FEAT, 128), FEAT)
            hid = hid + nt(block[...], w_down[0, :, columns])
    gate, up = pre_gate[...], pre_up[...]
    inverse = scale[:, 0:1]
    sigmoid = jax.nn.sigmoid(gate)
    score = jnp.sum(act[...].astype(f32) * hid, axis=1, keepdims=True)
    scaled = hid * inverse
    d_gate = (scaled * up * sigmoid * (1.0 + gate * (1.0 - sigmoid))).astype(bf16)
    d_up = (scaled * gate * sigmoid).astype(bf16)
    grad_gate[...] = d_gate
    grad_up[...] = d_up
    dot = jnp.sum(d_gate.astype(f32) * gate + d_up.astype(f32) * up, axis=1, keepdims=True)
    dot = dot * inverse * (1.0 / D)
    lane = lax.broadcasted_iota(jnp.int32, (ROWS, WIDE - FEAT), 1)
    me = 2 * (y * 2 + core)
    tail = jnp.zeros((ROWS, WIDE - FEAT), f32)
    for base, value in ((0, score), (64, dot)):
        high, low = split_two(value)
        tail = jnp.where(lane == base + me, high.astype(f32), tail)
        tail = jnp.where(lane == base + me + 1, low.astype(f32), tail)
    tail = tail.astype(bf16)
    for side, result in ((1, other), (0, own)):
        for i, offset in enumerate(HOMEWARD):
            head = lax.rem(y + offset, 4) * 2 + (core if side == 0 else 1 - core)
            rows = pl.ds(pl.multiple_of(head * FEAT, FEAT), FEAT)
            term = nt(d_gate, w_gate[0, rows, :]) + nt(d_up, w_up[0, rows, :])
            result[i, :, :FEAT] = term.astype(bf16)
            result[i, :, FEAT:] = tail


def weight_grads(
    where, x0, xs0, x1, x2, x3, xs123, g0, gs0, g1, g2, g3, gs123, act, grad_gate, grad_up,
    out_gate, out_up, out_down, buf_gate, buf_up, buf_down, sems,
):
    y, core = where[0], where[1]
    x_refs = (x0, xs0, (x1, x2, x3), xs123)
    g_refs = (g0, gs0, (g1, g2, g3), gs123)
    act_t = act[...].T
    pending = {}
    for n in range(8):
        side, i = divmod(n, 4)
        slot = n % 2
        head = lax.rem(y + GATHERED[i], 4) * 2 + (core if side == 0 else 1 - core)
        rows = pl.ds(pl.multiple_of(head * FEAT, FEAT), FEAT)
        columns = pl.ds(pl.multiple_of(head * FEAT, 128), FEAT)
        if slot in pending:
            for copy in pending[slot]:
                copy.wait()
        x_t = block_of(x_refs, side, i)[:, :FEAT].T
        buf_gate[slot] = nn(x_t, grad_gate[...]).astype(bf16)
        buf_up[slot] = nn(x_t, grad_up[...]).astype(bf16)
        buf_down[slot] = nn(act_t, block_of(g_refs, side, i)[...]).astype(bf16)
        pending[slot] = [
            pltpu.make_async_copy(buf_gate.at[slot], out_gate.at[0, rows, :], sems.at[slot, 0]),
            pltpu.make_async_copy(buf_up.at[slot], out_up.at[0, rows, :], sems.at[slot, 1]),
            pltpu.make_async_copy(buf_down.at[slot], out_down.at[0, :, columns], sems.at[slot, 2]),
        ]
        for copy in pending[slot]:
            copy.start()
    for copies in pending.values():
        for copy in copies:
            copy.wait()


def finish(out_rows, in_rows, hidden, gain, source, ids, slots, gates, moe, grad_hidden, grad_gates):
    live, matches = slot_matches(ids[...], slots[...])
    _, select = pick_rows(matches, source[...] & (ROWS - 1))
    mix = mix_of(matches, gates[...])
    first = mix.astype(bf16)
    rest = mix - first.astype(f32)
    second = rest.astype(bf16)
    third = (rest - second.astype(f32)).astype(bf16)
    rows = out_rows[...]
    moe[...] = (tn(first, rows) + (tn(second, rows) + tn(third, rows))).astype(bf16)
    tail = in_rows[:, FEAT:].astype(f32)
    lane = lax.broadcasted_iota(jnp.int32, tail.shape, 1)
    score = jnp.sum(jnp.where(lane < 64, tail, 0.0), axis=1, keepdims=True)
    dot = jnp.sum(jnp.where(lane < 64, 0.0, tail), axis=1, keepdims=True)
    found = [jnp.sum(jnp.where(match, score, 0.0), axis=0, keepdims=True) for match in matches]
    found = jnp.concatenate(found, axis=0)
    grad_gates[...] = jnp.where(live, found / gates[...], 0.0)
    back = tn(select, in_rows[:, :FEAT]) * gain[...]
    dots = jnp.where(select.astype(f32) > 0, dot, 0.0)
    per_parent = jnp.sum(dots.T, axis=1, keepdims=True)
    grad_hidden[...] = (back - hidden[...].astype(f32) * per_parent).astype(bf16)


def to_y(values, step):
    return lax.ppermute(values, "y", [(i, (i + step) % 4) for i in range(4)])


def to_sibling(values):
    return lax.ppermute(values, "core", [(0, 1), (1, 0)])


def gather(block):
    sibling = to_sibling(block)
    far = [to_y(block, 1), to_y(block, 3), to_y(block, 2)]
    return (block, sibling, *far, to_sibling(jnp.stack(far)))


def send_home(own, other):
    received = to_sibling(other)
    total = (own.astype(f32) + received.astype(f32)).astype(bf16)
    parts = [to_y(total[1], 1), to_y(total[2], 3), to_y(total[3], 2)]
    summed = total[0].astype(f32)
    for part in parts:
        summed = summed + part.astype(f32)
    return summed.astype(bf16)


def exchange(rows):
    width = rows.shape[1]
    pieces = rows.reshape(16, CAP, width)
    return lax.all_to_all(pieces, ("x", "z"), 0, 0, tiled=True).reshape(ROWS, width)


def on_device(
    hidden, norm_gain, beam_src, route_ids, route_slots, route_gates, w_gate, w_up, w_down, out_grad
):
    where = jnp.stack([lax.axis_index("y"), lax.axis_index("core")]).astype(jnp.int32)
    gain = norm_gain.reshape(1, FEAT)
    source = beam_src.reshape(1, ROWS)
    ids, slots, gates = route_ids.T, route_slots.T, route_gates.T
    rows_x, rows_g = local_call(
        prepare,
        (hidden, gain, source, ids, slots, gates, out_grad),
        [((ROWS, WIDE), bf16, VMEM), ((ROWS, FEAT), bf16, VMEM)],
        8,
        (10**8, 10**6),
    )
    sent = exchange(jnp.concatenate([rows_x, rows_g], axis=1))
    x_blocks = gather(sent[:, :WIDE])
    g_blocks = gather(sent[:, WIDE:])
    pre_gate, pre_up, act, scale, out_own, out_other = local_call(
        forward,
        (where, *x_blocks, w_gate, w_up, w_down),
        [
            ((ROWS, HID), f32, VMEM),
            ((ROWS, HID), f32, VMEM),
            ((ROWS, HID), bf16, VMEM),
            ((ROWS, 128), f32, VMEM),
            ((4, ROWS, FEAT), bf16, VMEM),
            ((4, ROWS, FEAT), bf16, VMEM),
        ],
        8,
        (3 * 2 * ROWS * D * HID, 10**6),
        scalars=1,
    )
    out_rows = send_home(out_own, out_other)
    d_gate, d_up, in_own, in_other = local_call(
        backward,
        (where, *g_blocks, w_gate, w_up, w_down, pre_gate, pre_up, act, scale),
        [
            ((ROWS, HID), bf16, VMEM),
            ((ROWS, HID), bf16, VMEM),
            ((4, ROWS, WIDE), bf16, VMEM),
            ((4, ROWS, WIDE), bf16, VMEM),
        ],
        8,
        (3 * 2 * ROWS * D * HID, 10**6),
        scalars=1,
    )
    in_rows = send_home(in_own, in_other)
    grads = local_call(
        weight_grads,
        (where, *x_blocks, *g_blocks, act, d_gate, d_up),
        [((1, D, HID), bf16, HBM), ((1, D, HID), bf16, HBM), ((1, HID, D), bf16, HBM)],
        16,
        (2 * 3 * 2 * ROWS * D * HID, 11 * 10**6),
        scalars=1,
        scratch=(
            VMEM((2, FEAT, HID), bf16),
            VMEM((2, FEAT, HID), bf16),
            VMEM((2, HID, FEAT), bf16),
            pltpu.SemaphoreType.DMA((2, 3)),
        ),
    )
    home = exchange(jnp.concatenate([out_rows, in_rows], axis=1))
    moe, grad_hidden, grad_gates = local_call(
        finish,
        (home[:, :FEAT], home[:, FEAT:], hidden, gain, source, ids, slots, gates),
        [((ROWS, FEAT), bf16, RESULT), ((ROWS, FEAT), bf16, RESULT), ((8, ROWS), f32, RESULT)],
        8,
        (10**8, 10**6),
    )
    return (moe, grad_hidden, grad_gates.T, *grads)


def solution(mesh):
    split = Mesh(mesh.devices.reshape(4, 2, 4, 4), ("y", "core", "x", "z"))
    heads, seq = ("y", "core"), ("x", "z")
    return jax.shard_map(
        on_device,
        mesh=split,
        in_specs=(
            P(seq, heads),
            P(heads),
            P(seq),
            P(seq, None),
            P(seq, None),
            P(seq, None),
            P(seq, None, heads),
            P(seq, None, heads),
            P(seq, heads, None),
            P(seq, heads),
        ),
        out_specs=(
            P(seq, heads),
            P(seq, heads),
            P(seq, None),
            P(seq, None, heads),
            P(seq, None, heads),
            P(seq, heads, None),
        ),
        check_vma=False,
    )
```

time: 247 us -> 124 us (0.50)
  waiting for transfers between devices: 101 us -> 39.7 us
  blocking collectives: 71.6 us -> 18.9 us
  matrix products: 20.1 us -> 0 us
  Pallas kernels: 0 us -> 18.4 us
  local copies, waits for them, and re-layouts: 22.5 us -> 16.5 us
  other arithmetic: 9.34 us -> 3.77 us
  starting transfers between devices: 20.1 us -> 25.3 us
    all_to_all x3 -> x1, waiting for transfers between devices: 101 us -> 1.05 us  [exchange(): lax.all_to_all(pieces, ('x', 'z'), 0, 0, tiled=True).reshape(ROWS, width)]
    psum x2 -> x0, blocking collectives: 39.8 us -> none  [feature_sum(): return lax.psum(values, 'heads')]
    ppermute x0 -> x18, waiting for transfers between devices: none -> 38.6 us  [the longest x12 34.8 us: to_y(): return lax.ppermute(values, 'y', [(i, (i + step) % 4) for i in range(4)])]
    ppermute x0 -> x18, starting transfers between devices: none -> 21 us  [the longest x12 19.5 us: to_y(): return lax.ppermute(values, 'y', [(i, (i + step) % 4) for i in range(4)])]
    dot_general x14 -> x0, matrix products: 20.1 us -> none  [the longest x1 4.48 us: on_device(): lax.dot_general(hidden_act, out_cot, contract_rows, preferred_element_typ...]
    pallas_call x0 -> x5, Pallas kernels: none -> 18.4 us  [local_call(): pl.pallas_call(kernel, out_shape=out_shape, in_specs=in_specs, out_specs=...]
    all_to_all x3 -> x1, starting transfers between devices: 20.1 us -> 4.22 us  [exchange(): lax.all_to_all(pieces, ('x', 'z'), 0, 0, tiled=True).reshape(ROWS, width)]
    all_to_all x1, blocking collectives: 31.8 us -> 18.9 us  [exchange(): lax.all_to_all(pieces, ('x', 'z'), 0, 0, tiled=True).reshape(ROWS, width)]
  transfers between devices with their start and end apart: 3 -> 19, of which waited for: 3 -> 11; matrix products, arithmetic and copies ran while one was open for 7% -> 2% of each run, Pallas kernels for 0% -> 13%
where the time goes in v1:
time: 124 us; the launch traced here: 123 us
  waiting for transfers between devices  39.7 us (32%)
  starting transfers between devices  25.3 us (20%)
  blocking collectives  18.9 us (15%)
  Pallas kernels  18.4 us (15%)
  local copies, waits for them, and re-layouts  16.5 us (13%)
  other arithmetic  3.77 us (3%)
    ppermute x12, waiting for transfers between devices, to_y(): return lax.ppermute(values, 'y', [(i, (i + step) % 4) for i in range(4)])  34.8 us
    ppermute x12, starting transfers between devices, to_y(): return lax.ppermute(values, 'y', [(i, (i + step) % 4) for i in range(4)])  19.5 us
    all_to_all x1, blocking collectives, exchange(): lax.all_to_all(pieces, ('x', 'z'), 0, 0, tiled=True).reshape(ROWS, width)  18.9 us
    pallas_call x5, Pallas kernels, local_call(): pl.pallas_call(kernel, out_shape=out_shape, in_specs=in_specs, out_specs=...  18.4 us
    unnamed x46, local copies, waits for them, and re-layouts  13.7 us
    all_to_all x1, starting transfers between devices, exchange(): lax.all_to_all(pieces, ('x', 'z'), 0, 0, tiled=True).reshape(ROWS, width)  4.22 us
    ppermute x6, waiting for transfers between devices, to_sibling(): return lax.ppermute(values, 'core', [(0, 1), (1, 0)])  3.87 us
  transfers between devices with their start and end apart: 19, of which 11 were waited for; matrix products, arithmetic and copies ran while one was open for 2% of the time, Pallas kernels for 13%

profile of v1, /device:TPU:0, one launch (start us, length us, event | category | flops | bytes accessed | tf_op | source)
XLA Modules:
  0.0 123.3 jit_solution(1664118236970899500)
XLA Ops:
  6.4 18.9 %all_to_all.10 = bf16[16,8,1920]{2,1,0:T(8,128)(2,1)S(1)} all-to-all(bf16[16,8,1920]{2,1,0:T(8,128)(2,1)S(1)} %maximum_bitcast_fusion), channel_id=1, replica_groups=mesh['y'=4,'core'=2,'x'=4,'z'=4] {'x','z'}, dimensions={0} | all-to-all | bytes 983040 | tf_op jit(solution)/shard_map/all_to_all | solution.py:265
  25.4 3.3 %collective-permute-start.3 = (bf16[128,1024]{1,0:T(8,128)(2,1)S(1)}, bf16[128,1024]{1,0:T(8,128)(2,1)S(1)}, u32[]{:S(2)}, u32[]{:S(2)}) collective-permute-start(bf16[128,1024]{1,0:T(8,128)(2,1)S(1)} %slice.48.x0), channel_id=1, source_target_pairs={{0,64},{32,96},{64,0},{96,32},{1,65},{33,97},{65,1},{97,33},{2,66}... | collective-permute-start | bytes 786440 | tf_op jit(solution)/shard_map/ppermute | solution.py:239
  28.6 1.1 collective-permute-start.2
  29.7 1.0 collective-permute-start.1
  30.7 5.5 %collective-permute-done.3.x3 = bf16[128,1024]{1,0:T(8,128)(2,1)S(1)} collective-permute-done((bf16[128,1024]{1,0:T(8,128)(2,1)S(1)}, bf16[128,1024]{1,0:T(8,128)(2,1)S(1)}, u32[]{:S(2)}, u32[]{:S(2)}) %collective-permute-start.3) | collective-permute-done | bytes 262176 | tf_op jit(solution)/shard_map/ppermute | solution.py:239
  36.2 3.4 %collective-permute-done.2.x2 = bf16[128,1024]{1,0:T(8,128)(2,1)S(1)} collective-permute-done((bf16[128,1024]{1,0:T(8,128)(2,1)S(1)}, bf16[128,1024]{1,0:T(8,128)(2,1)S(1)}, u32[]{:S(2)}, u32[]{:S(2)}) %collective-permute-start.2) | collective-permute-done | bytes 262176 | tf_op jit(solution)/shard_map/ppermute | solution.py:239
  39.5 1.0 pad_maximum_fusion
  40.5 2.9 %collective-permute-start.12 = (bf16[128,896]{1,0:T(8,128)(2,1)S(1)}, bf16[128,896]{1,0:T(8,128)(2,1)S(1)}, u32[]{:S(2)}, u32[]{:S(2)}) collective-permute-start(bf16[128,896]{1,0:T(8,128)(2,1)S(1)} %slice.53.g0), channel_id=1, source_target_pairs={{0,64},{32,96},{64,0},{96,32},{1,65},{33,97},{65,1},{97,33},{2,66}... | collective-permute-start | bytes 688136 | tf_op jit(solution)/shard_map/ppermute | solution.py:239
  43.4 1.2 collective-permute-start.11
  45.5 5.1 %collective-permute-done.12.g3 = bf16[128,896]{1,0:T(8,128)(2,1)S(1)} collective-permute-done((bf16[128,896]{1,0:T(8,128)(2,1)S(1)}, bf16[128,896]{1,0:T(8,128)(2,1)S(1)}, u32[]{:S(2)}, u32[]{:S(2)}) %collective-permute-start.12) | collective-permute-done | bytes 229408 | tf_op jit(solution)/shard_map/ppermute | solution.py:239
  50.5 4.5 %collective-permute-done.11.g2 = bf16[128,896]{1,0:T(8,128)(2,1)S(1)} collective-permute-done((bf16[128,896]{1,0:T(8,128)(2,1)S(1)}, bf16[128,896]{1,0:T(8,128)(2,1)S(1)}, u32[]{:S(2)}, u32[]{:S(2)}) %collective-permute-start.11) | collective-permute-done | bytes 229408 | tf_op jit(solution)/shard_map/ppermute | solution.py:239
  56.6 1.6 %collective-permute-done.s0.xs0 = bf16[128,1024]{1,0:T(8,128)(2,1)S(1)} collective-permute-done((bf16[128,1024]{1,0:T(8,128)(2,1)S(1)}, bf16[128,1024]{1,0:T(8,128)(2,1)S(1)}, u32[]{:S(2)}, u32[]{:S(2)}) %collective-permute-start) | collective-permute-done | bytes 262176 | tf_op jit(solution)/shard_map/ppermute | solution.py:243
  58.2 2.0 %copy-done = bf16[1,7168,256]{2,1,0:T(8,128)(2,1)S(1)} copy-done((bf16[1,7168,256]{2,1,0:T(8,128)(2,1)S(1)}, bf16[1,7168,256]{2,1,0:T(8,128)(2,1)}, u32[]{:S(2)}) %copy-start) | copy-done | bytes 3670040
  60.2 2.0 %copy-done.2 = bf16[1,7168,256]{2,1,0:T(8,128)(2,1)S(1)} copy-done((bf16[1,7168,256]{2,1,0:T(8,128)(2,1)S(1)}, bf16[1,7168,256]{2,1,0:T(8,128)(2,1)}, u32[]{:S(2)}) %copy-start.2) | copy-done | bytes 3670040
  62.2 2.0 %copy-done.4 = bf16[1,256,7168]{2,1,0:T(8,128)(2,1)S(1)} copy-done((bf16[1,256,7168]{2,1,0:T(8,128)(2,1)S(1)}, bf16[1,256,7168]{2,1,0:T(8,128)(2,1)}, u32[]{:S(2)}) %copy-start.4) | copy-done | bytes 3670040
  64.3 2.6 %shard_map.146 = (f32[128,256]{1,0:T(8,128)S(1)}, f32[128,256]{1,0:T(8,128)S(1)}, bf16[128,256]{1,0:T(8,128)(2,1)S(1)}, f32[128,128]{1,0:T(8,128)S(1)}, bf16[4,1...) custom-call(s32[2]{0:T(128)S(1)} %pad_add_fusion.where, bf16[128,1024]{1,0:T(8,128)(2,1)S(1)} %slice.48.x0, ...), custom_call_target="tpu_custom_call" | custom-call | flops 1409286144 | bytes 1000000 | tf_op jit(solution)/shard_map/pallas_call | solution.py:50
  67.4 2.3 %collective-permute-done.9.s0.gs0 = bf16[128,896]{1,0:T(8,128)(2,1)S(1)} collective-permute-done((bf16[128,896]{1,0:T(8,128)(2,1)S(1)}, bf16[128,896]{1,0:T(8,128)(2,1)S(1)}, u32[]{:S(2)}, u32[]{:S(2)}) %collective-permute-start.9) | collective-permute-done | bytes 229408 | tf_op jit(solution)/shard_map/ppermute | solution.py:243
  69.8 6.4 %shard_map.147 = (bf16[128,256]{1,0:T(8,128)(2,1)S(1)}, bf16[128,256]{1,0:T(8,128)(2,1)S(1)}, bf16[4,128,1024]{2,1,0:T(8,128)(2,1)S(1)}, bf16[4,128,1024]{2,1,0:T(8,128)(2,1)S(1)}) custom-call(s32[2]{0:T(128)S(1)} %pad_add_fusion.where, bf16[128,896]{1,0:T(8,128)(2,1)S(1)} %slice.53.g0, bf16[128,896]{1,0:T(8,128)(2,1)S(1)} %collective-permute-done.9.s0.gs0, ...), custom_call_target="tpu_custom_call" | custom-call | flops 1409286144 | bytes 1000000 | tf_op jit(solution)/shard_map/pallas_call | solution.py:50
  76.9 1.4 %collective-permute-start.6 = (bf16[128,896]{1,0:T(8,128)(2,1)S(1)}, bf16[128,896]{1,0:T(8,128)(2,1)S(1)}, u32[]{:S(2)}, u32[]{:S(2)}) collective-permute-start(bf16[128,896]{1,0:T(8,128)(2,1)S(1)} %get-tuple-element.45), channel_id=1, source_target_pairs={{0,32},{32,64},{64,96},{96,0},{1,33},{33,65},{65,97},{97,1},{2,34}... | collective-permute-start | bytes 688136 | tf_op jit(solution)/shard_map/ppermute | solution.py:239
  78.3 2.7 %collective-permute-start.8 = (bf16[128,896]{1,0:T(8,128)(2,1)S(1)}, bf16[128,896]{1,0:T(8,128)(2,1)S(1)}, u32[]{:S(2)}, u32[]{:S(2)}) collective-permute-start(bf16[128,896]{1,0:T(8,128)(2,1)S(1)} %get-tuple-element.46), channel_id=1, source_target_pairs={{0,64},{32,96},{64,0},{96,32},{1,65},{33,97},{65,1},{97,33},{2,66}... | collective-permute-start | bytes 688136 | tf_op jit(solution)/shard_map/ppermute | solution.py:239
  81.1 1.3 %collective-permute-start.7 = (bf16[128,896]{1,0:T(8,128)(2,1)S(1)}, bf16[128,896]{1,0:T(8,128)(2,1)S(1)}, u32[]{:S(2)}, u32[]{:S(2)}) collective-permute-start(bf16[128,896]{1,0:T(8,128)(2,1)S(1)} %get-tuple-element.47), channel_id=1, source_target_pairs={{0,96},{32,0},{64,32},{96,64},{1,97},{33,1},{65,33},{97,65},{2,98}... | collective-permute-start | bytes 688136 | tf_op jit(solution)/shard_map/ppermute | solution.py:239
  84.5 1.4 %collective-permute-done.6 = bf16[128,896]{1,0:T(8,128)(2,1)S(1)} collective-permute-done((bf16[128,896]{1,0:T(8,128)(2,1)S(1)}, bf16[128,896]{1,0:T(8,128)(2,1)S(1)}, u32[]{:S(2)}, u32[]{:S(2)}) %collective-permute-start.6) | collective-permute-done | bytes 229408 | tf_op jit(solution)/shard_map/ppermute | solution.py:239
  85.8 2.2 %collective-permute-start.16 = (bf16[128,1024]{1,0:T(8,128)(2,1)S(1)}, bf16[128,1024]{1,0:T(8,128)(2,1)S(1)}, u32[]{:S(2)}, u32[]{:S(2)}) collective-permute-start(bf16[128,1024]{1,0:T(8,128)(2,1)S(1)} %get-tuple-element.44), channel_id=1, source_target_pairs={{0,96},{32,0},{64,32},{96,64},{1,97},{33,1},{65,33},{97,65},{2,98}... | collective-permute-start | bytes 786440 | tf_op jit(solution)/shard_map/ppermute | solution.py:239
  88.0 4.4 %collective-permute-done.8 = bf16[128,896]{1,0:T(8,128)(2,1)S(1)} collective-permute-done((bf16[128,896]{1,0:T(8,128)(2,1)S(1)}, bf16[128,896]{1,0:T(8,128)(2,1)S(1)}, u32[]{:S(2)}, u32[]{:S(2)}) %collective-permute-start.8) | collective-permute-done | bytes 229408 | tf_op jit(solution)/shard_map/ppermute | solution.py:239
  92.6 4.0 %collective-permute-done.15 = bf16[128,1024]{1,0:T(8,128)(2,1)S(1)} collective-permute-done((bf16[128,1024]{1,0:T(8,128)(2,1)S(1)}, bf16[128,1024]{1,0:T(8,128)(2,1)S(1)}, u32[]{:S(2)}, u32[]{:S(2)}) %collective-permute-start.15) | collective-permute-done | bytes 262176 | tf_op jit(solution)/shard_map/ppermute | solution.py:239
  96.6 6.5 %collective-permute-done.17 = bf16[128,1024]{1,0:T(8,128)(2,1)S(1)} collective-permute-done((bf16[128,1024]{1,0:T(8,128)(2,1)S(1)}, bf16[128,1024]{1,0:T(8,128)(2,1)S(1)}, u32[]{:S(2)}, u32[]{:S(2)}) %collective-permute-start.17) | collective-permute-done | bytes 262176 | tf_op jit(solution)/shard_map/ppermute | solution.py:239
  104.1 4.2 %all-to-all-start.1 = ((bf16[16,8,1920]{2,1,0:T(8,128)(2,1)}), bf16[16,8,1920]{2,1,0:T(8,128)(2,1)}, u32[]{:S(2)}, u32[]{:S(2)}) async-start(bf16[16,8,1920]{2,1,0:T(8,128)(2,1)} %maximum_bitcast_fusion.1), calls=%async_computation.1 | async-start | bytes 983040 | tf_op jit(solution)/shard_map/all_to_all | solution.py:265
  110.7 7.7 %shard_map.149 = (bf16[1,7168,256]{2,1,0:T(8,128)(2,1)}, bf16[1,7168,256]{2,1,0:T(8,128)(2,1)}, bf16[1,256,7168]{2,1,0:T(8,128)(2,1)}) custom-call(s32[2]{0:T(128)S(1)} %copy-done.16, bf16[128,1024]{1,0:T(8,128)(2,1)S(1)} %slice.48.x0, bf16[128,1024]{1,0:T(8,128)(2,1)S(1)} %collective-permute-done.s0.xs0, bf16[128,1024]{1,0:T(8,128)(2,1)S(1)} %collective-permute-done.1.x1, ...), custom_call_target="tpu_custom_call" | custom-call | flops 2818572288 | bytes 11000000 | tf_op jit(solution)/shard_map/pallas_call | solution.py:50
  118.4 1.0 all-to-all-done.1
  119.4 1.0 slice.58.out_rows
  120.4 1.0 slice.59.in_rows
  122.0 1.3 %shard_map.148 = (bf16[128,896]{1,0:T(8,128)(2,1)}, bf16[128,896]{1,0:T(8,128)(2,1)}, f32[8,128]{1,0:T(8,128)}) custom-call(bf16[128,896]{1,0:T(8,128)(2,1)S(1)} %slice.58.out_rows, bf16[128,1024]{1,0:T(8,128)(2,1)S(1)} %slice.59.in_rows, bf16[128,896]{1,0:T(8,128)(2,1)S(1)} %copy-done.7, f32[1,896]{1,0:T(1,128)S(1)} %reshape.34.gain, ...), custom_call_target="tpu_custom_call" | custom-call | flops 100000000 | bytes 1000000 | tf_op jit(solution)/shard_map/pallas_call | solution.py:50
  (74 shorter events, 15.7 us)
Async XLA Ops:
  25.4 10.8 %collective-permute-start.3 = (bf16[128,1024]{1,0:T(8,128)(2,1)S(1)}, bf16[128,1024]{1,0:T(8,128)(2,1)S(1)}, u32[]{:S(2)}, u32[]{:S(2)}) collective-permute-start(bf16[128,1024]{1,0:T(8,128)(2,1)S(1)} %slice.48.x0), channel_id=1, source_target_pairs={{0,64},{32,96},{64,0},{96,32},{1,65},{33,97},{65,1},{97,33},{2,66}... | collective-permute-start | bytes 786440 | tf_op jit(solution)/shard_map/ppermute | solution.py:239
  28.6 10.9 %collective-permute-start.2 = (bf16[128,1024]{1,0:T(8,128)(2,1)S(1)}, bf16[128,1024]{1,0:T(8,128)(2,1)S(1)}, u32[]{:S(2)}, u32[]{:S(2)}) collective-permute-start(bf16[128,1024]{1,0:T(8,128)(2,1)S(1)} %slice.48.x0), channel_id=1, source_target_pairs={{0,96},{32,0},{64,32},{96,64},{1,97},{33,1},{65,33},{97,65},{2,98}... | collective-permute-start | bytes 786440 | tf_op jit(solution)/shard_map/ppermute | solution.py:239
  29.7 9.9 %collective-permute-start.1 = (bf16[128,1024]{1,0:T(8,128)(2,1)S(1)}, bf16[128,1024]{1,0:T(8,128)(2,1)S(1)}, u32[]{:S(2)}, u32[]{:S(2)}) collective-permute-start(bf16[128,1024]{1,0:T(8,128)(2,1)S(1)} %slice.48.x0), channel_id=1, source_target_pairs={{0,32},{32,64},{64,96},{96,0},{1,33},{33,65},{65,97},{97,1},{2,34}... | collective-permute-start | bytes 786440 | tf_op jit(solution)/shard_map/ppermute | solution.py:239
  40.5 17.6 %collective-permute-start.4 = (bf16[3,128,1024]{2,1,0:T(8,128)(2,1)}, bf16[3,128,1024]{2,1,0:T(8,128)(2,1)S(1)}, u32[]{:S(2)}, u32[]{:S(2)}) collective-permute-start(bf16[3,128,1024]{2,1,0:T(8,128)(2,1)} %pad_maximum_fusion), channel_id=1, source_target_pairs={{0,16},{16,0},{1,17},{17,1},{2,18},{18,2},{3,19},{19,3},{4,20},{20... | collective-permute-start | bytes 2359304 | tf_op jit(solution)/shard_map/ppermute | solution.py:243
  40.5 10.0 %collective-permute-start.12 = (bf16[128,896]{1,0:T(8,128)(2,1)S(1)}, bf16[128,896]{1,0:T(8,128)(2,1)S(1)}, u32[]{:S(2)}, u32[]{:S(2)}) collective-permute-start(bf16[128,896]{1,0:T(8,128)(2,1)S(1)} %slice.53.g0), channel_id=1, source_target_pairs={{0,64},{32,96},{64,0},{96,32},{1,65},{33,97},{65,1},{97,33},{2,66}... | collective-permute-start | bytes 688136 | tf_op jit(solution)/shard_map/ppermute | solution.py:239
  43.4 11.6 %collective-permute-start.11 = (bf16[128,896]{1,0:T(8,128)(2,1)S(1)}, bf16[128,896]{1,0:T(8,128)(2,1)S(1)}, u32[]{:S(2)}, u32[]{:S(2)}) collective-permute-start(bf16[128,896]{1,0:T(8,128)(2,1)S(1)} %slice.53.g0), channel_id=1, source_target_pairs={{0,96},{32,0},{64,32},{96,64},{1,97},{33,1},{65,33},{97,65},{2,98}... | collective-permute-start | bytes 688136 | tf_op jit(solution)/shard_map/ppermute | solution.py:239
  44.6 10.4 %collective-permute-start.10 = (bf16[128,896]{1,0:T(8,128)(2,1)S(1)}, bf16[128,896]{1,0:T(8,128)(2,1)S(1)}, u32[]{:S(2)}, u32[]{:S(2)}) collective-permute-start(bf16[128,896]{1,0:T(8,128)(2,1)S(1)} %slice.53.g0), channel_id=1, source_target_pairs={{0,32},{32,64},{64,96},{96,0},{1,33},{33,65},{65,97},{97,1},{2,34}... | collective-permute-start | bytes 688136 | tf_op jit(solution)/shard_map/ppermute | solution.py:239
  56.0 13.7 %collective-permute-start.13 = (bf16[3,128,896]{2,1,0:T(8,128)(2,1)}, bf16[3,128,896]{2,1,0:T(8,128)(2,1)}, u32[]{:S(2)}, u32[]{:S(2)}) collective-permute-start(bf16[3,128,896]{2,1,0:T(8,128)(2,1)} %pad_maximum_fusion.1), channel_id=1, source_target_pairs={{0,16},{16,0},{1,17},{17,1},{2,18},{18,2},{3,19},{19,3},{4,20},{20... | collective-permute-start | bytes 2064392 | tf_op jit(solution)/shard_map/ppermute | solution.py:243
  56.0 2.1 %collective-permute-start = (bf16[128,1024]{1,0:T(8,128)(2,1)S(1)}, bf16[128,1024]{1,0:T(8,128)(2,1)S(1)}, u32[]{:S(2)}, u32[]{:S(2)}) collective-permute-start(bf16[128,1024]{1,0:T(8,128)(2,1)S(1)} %slice.48.x0), channel_id=1, source_target_pairs={{0,16},{16,0},{1,17},{17,1},{2,18},{18,2},{3,19},{19,3},{4,20},{20... | collective-permute-start | bytes 786440 | tf_op jit(solution)/shard_map/ppermute | solution.py:243
  56.6 13.1 %copy-start.15 = (s32[2]{0:T(128)}, s32[2]{0:T(128)S(1)}, u32[]{:S(2)}) copy-start(s32[2]{0:T(128)S(1)} %pad_add_fusion.where) | copy-start | bytes 28
  58.2 2.0 %copy-start = (bf16[1,7168,256]{2,1,0:T(8,128)(2,1)S(1)}, bf16[1,7168,256]{2,1,0:T(8,128)(2,1)}, u32[]{:S(2)}) copy-start(bf16[1,7168,256]{2,1,0:T(8,128)(2,1)} %w_gate.3) | copy-start | bytes 11010052
  60.2 2.0 %copy-start.2 = (bf16[1,7168,256]{2,1,0:T(8,128)(2,1)S(1)}, bf16[1,7168,256]{2,1,0:T(8,128)(2,1)}, u32[]{:S(2)}) copy-start(bf16[1,7168,256]{2,1,0:T(8,128)(2,1)} %w_up.3) | copy-start | bytes 11010052
  62.2 2.0 %copy-start.4 = (bf16[1,256,7168]{2,1,0:T(8,128)(2,1)S(1)}, bf16[1,256,7168]{2,1,0:T(8,128)(2,1)}, u32[]{:S(2)}) copy-start(bf16[1,256,7168]{2,1,0:T(8,128)(2,1)} %w_down.3) | copy-start | bytes 11010052
  64.3 5.5 %copy-start.1 = (bf16[1,7168,256]{2,1,0:T(8,128)(2,1)S(1)}, bf16[1,7168,256]{2,1,0:T(8,128)(2,1)}, u32[]{:S(2)}) copy-start(bf16[1,7168,256]{2,1,0:T(8,128)(2,1)} %w_gate.3) | copy-start | bytes 11010052
  64.3 5.5 %copy-start.3 = (bf16[1,7168,256]{2,1,0:T(8,128)(2,1)S(1)}, bf16[1,7168,256]{2,1,0:T(8,128)(2,1)}, u32[]{:S(2)}) copy-start(bf16[1,7168,256]{2,1,0:T(8,128)(2,1)} %w_up.3) | copy-start | bytes 11010052
  64.3 5.5 %copy-start.5 = (bf16[1,256,7168]{2,1,0:T(8,128)(2,1)S(1)}, bf16[1,256,7168]{2,1,0:T(8,128)(2,1)}, u32[]{:S(2)}) copy-start(bf16[1,256,7168]{2,1,0:T(8,128)(2,1)} %w_down.3) | copy-start | bytes 11010052
  66.8 9.8 %collective-permute-start.5 = (bf16[4,128,896]{2,1,0:T(8,128)(2,1)S(1)}, bf16[4,128,896]{2,1,0:T(8,128)(2,1)S(1)}, u32[]{:S(2)}, u32[]{:S(2)}) collective-permute-start(bf16[4,128,896]{2,1,0:T(8,128)(2,1)S(1)} %get-tuple-element.27), channel_id=1, source_target_pairs={{0,16},{16,0},{1,17},{17,1},{2,18},{18,2},{3,19},{19,3},{4,20},{20... | collective-permute-start | bytes 2752520 | tf_op jit(solution)/shard_map/ppermute | solution.py:243
  67.3 2.4 %collective-permute-start.9 = (bf16[128,896]{1,0:T(8,128)(2,1)S(1)}, bf16[128,896]{1,0:T(8,128)(2,1)S(1)}, u32[]{:S(2)}, u32[]{:S(2)}) collective-permute-start(bf16[128,896]{1,0:T(8,128)(2,1)S(1)} %slice.53.g0), channel_id=1, source_target_pairs={{0,16},{16,0},{1,17},{17,1},{2,18},{18,2},{3,19},{19,3},{4,20},{20... | collective-permute-start | bytes 688136 | tf_op jit(solution)/shard_map/ppermute | solution.py:243
  76.1 6.7 %copy-start.19 = (bf16[128,256]{1,0:T(8,128)(2,1)}, bf16[128,256]{1,0:T(8,128)(2,1)S(1)}, u32[]{:S(2)}) copy-start(bf16[128,256]{1,0:T(8,128)(2,1)S(1)} %get-tuple-element.37.grad_gate) | copy-start | bytes 196612
  76.1 6.7 %copy-start.21 = (bf16[128,256]{1,0:T(8,128)(2,1)}, bf16[128,256]{1,0:T(8,128)(2,1)S(1)}, u32[]{:S(2)}) copy-start(bf16[128,256]{1,0:T(8,128)(2,1)S(1)} %get-tuple-element.38.grad_up) | copy-start | bytes 196612
  76.2 6.2 %collective-permute-start.14 = (bf16[4,128,1024]{2,1,0:T(8,128)(2,1)S(1)}, bf16[4,128,1024]{2,1,0:T(8,128)(2,1)S(1)}, u32[]{:S(2)}, u32[]{:S(2)}) collective-permute-start(bf16[4,128,1024]{2,1,0:T(8,128)(2,1)S(1)} %get-tuple-element.33), channel_id=1, source_target_pairs={{0,16},{16,0},{1,17},{17,1},{2,18},{18,2},{3,19},{19,3},{4,20},{20... | collective-permute-start | bytes 3145736 | tf_op jit(solution)/shard_map/ppermute | solution.py:243
  76.9 8.9 %collective-permute-start.6 = (bf16[128,896]{1,0:T(8,128)(2,1)S(1)}, bf16[128,896]{1,0:T(8,128)(2,1)S(1)}, u32[]{:S(2)}, u32[]{:S(2)}) collective-permute-start(bf16[128,896]{1,0:T(8,128)(2,1)S(1)} %get-tuple-element.45), channel_id=1, source_target_pairs={{0,32},{32,64},{64,96},{96,0},{1,33},{33,65},{65,97},{97,1},{2,34}... | collective-permute-start | bytes 688136 | tf_op jit(solution)/shard_map/ppermute | solution.py:239
  78.3 14.1 %collective-permute-start.8 = (bf16[128,896]{1,0:T(8,128)(2,1)S(1)}, bf16[128,896]{1,0:T(8,128)(2,1)S(1)}, u32[]{:S(2)}, u32[]{:S(2)}) collective-permute-start(bf16[128,896]{1,0:T(8,128)(2,1)S(1)} %get-tuple-element.46), channel_id=1, source_target_pairs={{0,64},{32,96},{64,0},{96,32},{1,65},{33,97},{65,1},{97,33},{2,66}... | collective-permute-start | bytes 688136 | tf_op jit(solution)/shard_map/ppermute | solution.py:239
  81.1 11.4 %collective-permute-start.7 = (bf16[128,896]{1,0:T(8,128)(2,1)S(1)}, bf16[128,896]{1,0:T(8,128)(2,1)S(1)}, u32[]{:S(2)}, u32[]{:S(2)}) collective-permute-start(bf16[128,896]{1,0:T(8,128)(2,1)S(1)} %get-tuple-element.47), channel_id=1, source_target_pairs={{0,96},{32,0},{64,32},{96,64},{1,97},{33,1},{65,33},{97,65},{2,98}... | collective-permute-start | bytes 688136 | tf_op jit(solution)/shard_map/ppermute | solution.py:239
  82.9 13.7 %collective-permute-start.15 = (bf16[128,1024]{1,0:T(8,128)(2,1)S(1)}, bf16[128,1024]{1,0:T(8,128)(2,1)S(1)}, u32[]{:S(2)}, u32[]{:S(2)}) collective-permute-start(bf16[128,1024]{1,0:T(8,128)(2,1)S(1)} %get-tuple-element.42), channel_id=1, source_target_pairs={{0,32},{32,64},{64,96},{96,0},{1,33},{33,65},{65,97},{97,1},{2,34}... | collective-permute-start | bytes 786440 | tf_op jit(solution)/shard_map/ppermute | solution.py:239
  83.7 19.4 %collective-permute-start.17 = (bf16[128,1024]{1,0:T(8,128)(2,1)S(1)}, bf16[128,1024]{1,0:T(8,128)(2,1)S(1)}, u32[]{:S(2)}, u32[]{:S(2)}) collective-permute-start(bf16[128,1024]{1,0:T(8,128)(2,1)S(1)} %get-tuple-element.43), channel_id=1, source_target_pairs={{0,64},{32,96},{64,0},{96,32},{1,65},{33,97},{65,1},{97,33},{2,66}... | collective-permute-start | bytes 786440 | tf_op jit(solution)/shard_map/ppermute | solution.py:239
  85.8 17.2 %collective-permute-start.16 = (bf16[128,1024]{1,0:T(8,128)(2,1)S(1)}, bf16[128,1024]{1,0:T(8,128)(2,1)S(1)}, u32[]{:S(2)}, u32[]{:S(2)}) collective-permute-start(bf16[128,1024]{1,0:T(8,128)(2,1)S(1)} %get-tuple-element.44), channel_id=1, source_target_pairs={{0,96},{32,0},{64,32},{96,64},{1,97},{33,1},{65,33},{97,65},{2,98}... | collective-permute-start | bytes 786440 | tf_op jit(solution)/shard_map/ppermute | solution.py:239
  104.1 15.3 %all-to-all-start.1 = ((bf16[16,8,1920]{2,1,0:T(8,128)(2,1)}), bf16[16,8,1920]{2,1,0:T(8,128)(2,1)}, u32[]{:S(2)}, u32[]{:S(2)}) async-start(bf16[16,8,1920]{2,1,0:T(8,128)(2,1)} %maximum_bitcast_fusion.1), calls=%async_computation.1 | async-start | bytes 983040 | tf_op jit(solution)/shard_map/all_to_all | solution.py:265
  110.7 10.7 %copy-start.7 = (bf16[128,896]{1,0:T(8,128)(2,1)S(1)}, bf16[128,896]{1,0:T(8,128)(2,1)}, u32[]{:S(2)}) copy-start(bf16[128,896]{1,0:T(8,128)(2,1)} %hidden.3) | copy-start | bytes 688132
  110.7 10.7 %copy-start.10 = (s32[128,8]{0,1:T(8,128)S(1)}, s32[128,8]{0,1:T(8,128)}, u32[]{:S(2)}) copy-start(s32[128,8]{0,1:T(8,128)} %param.13) | copy-start | bytes 12292
  110.7 10.7 %copy-start.12 = (s32[128,8]{0,1:T(8,128)S(1)}, s32[128,8]{0,1:T(8,128)}, u32[]{:S(2)}) copy-start(s32[128,8]{0,1:T(8,128)} %param.14) | copy-start | bytes 12292
  110.7 10.7 %copy-start.14 = (f32[128,8]{0,1:T(8,128)S(1)}, f32[128,8]{0,1:T(8,128)}, u32[]{:S(2)}) copy-start(f32[128,8]{0,1:T(8,128)} %param.15) | copy-start | bytes 12292
  (10 other events, 7.6 us)

commit v2 on v1

v2 whole, which is shorter than its diff:
```python
import jax
import jax.numpy as jnp
from jax import lax
from jax.experimental import pallas as pl
from jax.experimental.pallas import tpu as pltpu
from jax.sharding import Mesh, PartitionSpec as P

D = 7168
CAP = 8
ROWS = 128
FEAT = 896
WIDE = 1024
HID = 256
EPSILON = 1e-06
GATHERED = (0, 3, 1, 2)
HOMEWARD = (0, 1, 3, 2)

f32 = jnp.float32
bf16 = jnp.bfloat16
SMEM, VMEM, COPY, HBM = "smem", "vmem", "copy", "hbm"


def nn(a, b):
    return lax.dot_general(a, b, (((1,), (0,)), ((), ())), preferred_element_type=f32)


def nt(a, b):
    return lax.dot_general(a, b, (((1,), (1,)), ((), ())), preferred_element_type=f32)


def tn(a, b):
    return lax.dot_general(a, b, (((0,), (0,)), ((), ())), preferred_element_type=f32)


def local_call(kernel, inputs, outputs, mib, cost, scratch=()):
    in_specs, args = [], []
    for kind, value in inputs:
        space = {SMEM: pltpu.SMEM, HBM: pl.ANY}.get(kind, pltpu.VMEM)
        in_specs.append(pl.BlockSpec(memory_space=space))
        if kind != SMEM:
            value = pltpu.with_memory_space_constraint(value, pltpu.VMEM if kind == VMEM else pltpu.HBM)
        args.append(value)
    out_shape, out_specs = [], []
    for kind, shape, dtype in outputs:
        space = {VMEM: pltpu.VMEM, HBM: pltpu.HBM}.get(kind, jax.ShapeDtypeStruct)
        out_shape.append(space(shape, dtype))
        out_specs.append(pl.BlockSpec(memory_space=pl.ANY if kind == HBM else pltpu.VMEM))
    return pl.pallas_call(
        kernel,
        out_shape=out_shape,
        in_specs=in_specs,
        out_specs=out_specs,
        scratch_shapes=list(scratch),
        compiler_params=pltpu.CompilerParams(vmem_limit_bytes=mib * 2**20),
        cost_estimate=pl.CostEstimate(flops=cost[0], bytes_accessed=cost[1], transcendentals=0),
    )(*args)


def held(*values):
    return [(VMEM, value) for value in values]


def fetched(*values):
    return [(COPY, value) for value in values]


def split_two(value):
    high = value.astype(bf16)
    low = (value - high.astype(f32)).astype(bf16)
    return high, low


def slot_matches(ids, slots):
    live = (ids < 16) & (slots >= 0) & (slots < CAP)
    target = jnp.where(live, ids * CAP + slots, ROWS)
    slot = lax.broadcasted_iota(jnp.int32, (ROWS, ROWS), 0)
    return live, [slot == target[k : k + 1, :] for k in range(8)]


def pick_rows(matches, parent):
    pick = matches[0]
    for match in matches[1:]:
        pick = pick | match
    pick = jnp.where(pick, 1.0, 0.0).astype(bf16)
    row = lax.broadcasted_iota(jnp.int32, (ROWS, ROWS), 0)
    from_parent = jnp.where(row == parent, 1.0, 0.0).astype(bf16)
    return pick, nt(pick, from_parent).astype(bf16)


def mix_of(matches, gates):
    mix = jnp.zeros((ROWS, ROWS), f32)
    for k, match in enumerate(matches):
        mix = mix + jnp.where(match, gates[k : k + 1, :], 0.0)
    return mix


def prepare(hidden, gain, source, ids, slots, gates, cotangent, rows, kept):
    _, matches = slot_matches(ids[...], slots[...])
    pick, select = pick_rows(matches, source[...] & (ROWS - 1))
    gate = jnp.sum(mix_of(matches, gates[...]), axis=1, keepdims=True)
    beam = nn(select, hidden[...])
    rows[:, :FEAT] = (beam * gain[...][None, :]).astype(bf16)
    square = jnp.sum(beam * beam, axis=1, keepdims=True) * (1.0 / D)
    high, low = split_two(square)
    lane = lax.broadcasted_iota(jnp.int32, (ROWS, WIDE - FEAT), 1)
    tail = jnp.where(lane == 0, high.astype(f32), jnp.where(lane == 1, low.astype(f32), 0.0))
    rows[:, FEAT:WIDE] = tail.astype(bf16)
    rows[:, WIDE:] = (nn(pick, cotangent[...]) * gate).astype(bf16)
    kept[...] = hidden[...]


def turn_weights(gate, up, down, gate_t, up_t, down_t, wide, tall, wide_t, tall_t, sems):
    loads = [
        pltpu.make_async_copy(down, tall, sems.at[0]),
        pltpu.make_async_copy(gate, wide.at[0], sems.at[1]),
        pltpu.make_async_copy(up, wide.at[1], sems.at[2]),
    ]
    stores = [
        pltpu.make_async_copy(tall_t, down_t, sems.at[3]),
        pltpu.make_async_copy(wide_t.at[0], gate_t, sems.at[4]),
        pltpu.make_async_copy(wide_t.at[1], up_t, sems.at[5]),
    ]
    for load in loads:
        load.start()
    loads[0].wait()
    for head in range(8):
        part = slice(head * FEAT, (head + 1) * FEAT)
        tall_t[part, :] = tall[0, :, part].T
    stores[0].start()
    for i in range(2):
        loads[1 + i].wait()
        for head in range(8):
            part = slice(head * FEAT, (head + 1) * FEAT)
            wide_t[i, :, part] = wide[i, 0, part, :].T
        stores[1 + i].start()
    for store in stores:
        store.wait()


def head_at(where, offset, side):
    core = where[1] if side == 0 else 1 - where[1]
    return lax.rem(where[0] + offset, 4) * 2 + core


def row_part(head):
    return pl.ds(pl.multiple_of(head * FEAT, FEAT), FEAT)


def column_part(head):
    return pl.ds(pl.multiple_of(head * FEAT, 128), FEAT)


def forward(where, *refs):
    blocks, weights, (pre_gate, pre_up, act, scale) = refs[:8], refs[8:11], refs[11:15]
    own, other, (w_gate, w_up, w_down, sems) = refs[15:19], refs[19:23], refs[23:]
    loads = [
        pltpu.make_async_copy(source, target, sems.at[i])
        for i, (source, target) in enumerate(zip(weights, (w_gate, w_up, w_down)))
    ]
    for load in loads:
        load.start()
    mean = jnp.zeros((ROWS, WIDE - FEAT), f32)
    for block in blocks:
        mean = mean + block[:, FEAT:WIDE].astype(f32)
    pre = []
    for load, weight in zip(loads, (w_gate, w_up)):
        load.wait()
        total = jnp.zeros((ROWS, HID), f32)
        for n, block in enumerate(blocks):
            rows = row_part(head_at(where, GATHERED[n % 4], n // 4))
            total = total + nn(block[:, :FEAT], weight[0, rows, :])
        pre.append(total)
    gate, up = pre
    inverse = lax.rsqrt(jnp.sum(mean, axis=1, keepdims=True) + EPSILON)
    gate = gate * inverse
    up = up * inverse
    hidden_act = (gate * jax.nn.sigmoid(gate) * up).astype(bf16)
    pre_gate[...] = gate
    pre_up[...] = up
    act[...] = hidden_act
    scale[...] = jnp.broadcast_to(inverse, (ROWS, 128))
    loads[2].wait()
    for side, result in ((1, other), (0, own)):
        for i, offset in enumerate(HOMEWARD):
            columns = column_part(head_at(where, offset, side))
            result[i][...] = nn(hidden_act, w_down[0, :, columns]).astype(bf16)


def backward(where, *refs):
    blocks = refs[:8]
    gate_t, up_t, down_t, pre_gate, pre_up, act, scale, grad_gate, grad_up = refs[8:17]
    own, other = refs[17:21], refs[21:25]
    hid = jnp.zeros((ROWS, HID), f32)
    for n, block in enumerate(blocks):
        hid = hid + nn(g_part(block)[...], down_t[row_part(head_at(where, GATHERED[n % 4], n // 4)), :])
    gate, up = pre_gate[...], pre_up[...]
    inverse = scale[:, 0:1]
    sigmoid = jax.nn.sigmoid(gate)
    score = jnp.sum(act[...].astype(f32) * hid, axis=1, keepdims=True)
    scaled = hid * inverse
    d_gate = (scaled * up * sigmoid * (1.0 + gate * (1.0 - sigmoid))).astype(bf16)
    d_up = (scaled * gate * sigmoid).astype(bf16)
    grad_gate[...] = d_gate
    grad_up[...] = d_up
    dot = jnp.sum(d_gate.astype(f32) * gate + d_up.astype(f32) * up, axis=1, keepdims=True)
    dot = dot * inverse * (1.0 / D)
    lane = lax.broadcasted_iota(jnp.int32, (ROWS, WIDE - FEAT), 1)
    me = 2 * head_at(where, 0, 0)
    tail = jnp.zeros((ROWS, WIDE - FEAT), f32)
    for base, value in ((0, score), (64, dot)):
        high, low = split_two(value)
        tail = jnp.where(lane == base + me, high.astype(f32), tail)
        tail = jnp.where(lane == base + me + 1, low.astype(f32), tail)
    tail = tail.astype(bf16)
    for side, result in ((1, other), (0, own)):
        for i, offset in enumerate(HOMEWARD):
            columns = column_part(head_at(where, offset, side))
            term = nn(d_gate, gate_t[:, columns]) + nn(d_up, up_t[:, columns])
            result[i][:, :FEAT] = term.astype(bf16)
            result[i][:, FEAT:] = tail


def weight_grads(where, *refs):
    x_blocks = refs[:8]
    g_blocks = (refs[0], *refs[8:11], refs[4], *refs[11:14])
    act, grad_gate, grad_up, out_gate, out_up, out_down, buf_gate, buf_up, buf_down, sems = refs[14:]
    act_t = act[...].T
    pending = {}
    for n in range(8):
        slot = n % 2
        head = head_at(where, GATHERED[n % 4], n // 4)
        for copy in pending.get(slot, ()):
            copy.wait()
        x_t = x_blocks[n][:, :FEAT].T
        buf_gate[slot] = nn(x_t, grad_gate[...]).astype(bf16)
        buf_up[slot] = nn(x_t, grad_up[...]).astype(bf16)
        buf_down[slot] = nn(act_t, g_part(g_blocks[n])[...]).astype(bf16)
        pending[slot] = [
            pltpu.make_async_copy(buf_gate.at[slot], out_gate.at[0, row_part(head), :], sems.at[slot, 0]),
            pltpu.make_async_copy(buf_up.at[slot], out_up.at[0, row_part(head), :], sems.at[slot, 1]),
            pltpu.make_async_copy(buf_down.at[slot], out_down.at[0, :, column_part(head)], sems.at[slot, 2]),
        ]
        for copy in pending[slot]:
            copy.start()
    for copies in pending.values():
        for copy in copies:
            copy.wait()


def finish(home, hidden, gain, source, ids, slots, gates, moe, grad_hidden, grad_gates):
    live, matches = slot_matches(ids[...], slots[...])
    _, select = pick_rows(matches, source[...] & (ROWS - 1))
    mix = mix_of(matches, gates[...])
    first = mix.astype(bf16)
    rest = mix - first.astype(f32)
    second = rest.astype(bf16)
    third = (rest - second.astype(f32)).astype(bf16)
    rows = home[:, :FEAT]
    moe[...] = (tn(first, rows) + (tn(second, rows) + tn(third, rows))).astype(bf16)
    tail = home[:, FEAT + FEAT :].astype(f32)
    lane = lax.broadcasted_iota(jnp.int32, tail.shape, 1)
    score = jnp.sum(jnp.where(lane < 64, tail, 0.0), axis=1, keepdims=True)
    dot = jnp.sum(jnp.where(lane < 64, 0.0, tail), axis=1, keepdims=True)
    found = [jnp.sum(jnp.where(match, score, 0.0), axis=0, keepdims=True) for match in matches]
    found = jnp.concatenate(found, axis=0)
    grad_gates[...] = jnp.where(live, found / gates[...], 0.0)
    back = tn(select, home[:, FEAT : FEAT + FEAT]) * gain[...][None, :]
    dots = jnp.where(select.astype(f32) > 0, dot, 0.0)
    per_parent = jnp.sum(dots.T, axis=1, keepdims=True)
    grad_hidden[...] = (back - hidden[...].astype(f32) * per_parent).astype(bf16)


def to_y(values, step):
    return lax.ppermute(values, "y", [(i, (i + step) % 4) for i in range(4)])


def to_sibling(values):
    return lax.ppermute(values, "core", [(0, 1), (1, 0)])


def gather(sent, sibling, part):
    block = sent[:, part]
    far = [to_y(block, 1), to_y(block, 3), to_y(block, 2)]
    return [sent, *far, sibling, *[to_sibling(value) for value in far]]


def g_part(block):
    return block if block.shape[1] == FEAT else block.at[:, WIDE:]


def chip_sums(own, other):
    return [(mine.astype(f32) + to_sibling(theirs).astype(f32)).astype(bf16) for mine, theirs in zip(own, other)]


def sent_home(sums):
    return [to_y(sums[1], 1), to_y(sums[2], 3), to_y(sums[3], 2)]


def row_sum(mine, parts):
    total = mine.astype(f32)
    for part in parts:
        total = total + part.astype(f32)
    return total.astype(bf16)


def exchange(rows):
    width = rows.shape[1]
    pieces = rows.reshape(16, CAP, width)
    return lax.all_to_all(pieces, ("x", "z"), 0, 0, tiled=True).reshape(ROWS, width)


def on_device(
    hidden, norm_gain, beam_src, route_ids, route_slots, route_gates, w_gate, w_up, w_down, out_grad
):
    where = (SMEM, jnp.stack([lax.axis_index("y"), lax.axis_index("core")]).astype(jnp.int32))
    gain = norm_gain
    source = beam_src.reshape(1, ROWS)
    ids, slots, gates = route_ids.T, route_slots.T, route_gates.T
    rows, kept = local_call(
        prepare,
        fetched(hidden, gain, source, ids, slots, gates, out_grad),
        [(VMEM, (ROWS, WIDE + FEAT), bf16), (VMEM, (ROWS, FEAT), bf16)],
        8,
        (0, 1000),
    )
    turned = local_call(
        turn_weights,
        [(HBM, w_gate), (HBM, w_up), (HBM, w_down)],
        [(HBM, (HID, D), bf16), (HBM, (HID, D), bf16), (HBM, (D, HID), bf16)],
        24,
        (0, 60 * 10**6),
        scratch=(
            pltpu.VMEM((2, 1, D, HID), bf16),
            pltpu.VMEM((1, HID, D), bf16),
            pltpu.VMEM((2, HID, D), bf16),
            pltpu.VMEM((D, HID), bf16),
            pltpu.SemaphoreType.DMA((6,)),
        ),
    )
    sent = exchange(rows)
    sent, *turned = lax.optimization_barrier((sent, *turned))
    sibling = to_sibling(sent)
    x_blocks = gather(sent, sibling, slice(None, WIDE))
    g_blocks = gather(sent, sibling, slice(WIDE, None))
    pre_gate, pre_up, act, scale, *out_terms = local_call(
        forward,
        [where, *held(*x_blocks), (HBM, w_gate), (HBM, w_up), (HBM, w_down)],
        [
            (VMEM, (ROWS, HID), f32),
            (VMEM, (ROWS, HID), f32),
            (VMEM, (ROWS, HID), bf16),
            (VMEM, (ROWS, 128), f32),
            *[(VMEM, (ROWS, FEAT), bf16)] * 8,
        ],
        16,
        (10**10, 1000),
        scratch=(
            pltpu.VMEM((1, D, HID), bf16),
            pltpu.VMEM((1, D, HID), bf16),
            pltpu.VMEM((1, HID, D), bf16),
            pltpu.SemaphoreType.DMA((3,)),
        ),
    )
    out_sums = chip_sums(out_terms[:4], out_terms[4:])
    out_parts = sent_home(out_sums)
    d_gate, d_up, *in_terms = local_call(
        backward,
        [where, *held(*g_blocks, *turned, pre_gate, pre_up, act, scale)],
        [
            (VMEM, (ROWS, HID), bf16),
            (VMEM, (ROWS, HID), bf16),
            *[(VMEM, (ROWS, WIDE), bf16)] * 8,
        ],
        4,
        (10**10, 1000),
    )
    in_terms, out_parts = lax.optimization_barrier((in_terms, out_parts))
    in_sums = chip_sums(in_terms[:4], in_terms[4:])
    out_rows = row_sum(out_sums[0], out_parts)
    in_rows = row_sum(in_sums[0], sent_home(in_sums))
    grads = local_call(
        weight_grads,
        [where, *fetched(*x_blocks, *g_blocks[1:4], *g_blocks[5:], act, d_gate, d_up)],
        [(HBM, (1, D, HID), bf16), (HBM, (1, D, HID), bf16), (HBM, (1, HID, D), bf16)],
        12,
        (2 * 3 * 2 * ROWS * D * HID, 22 * 10**6),
        scratch=(
            pltpu.VMEM((2, FEAT, HID), bf16),
            pltpu.VMEM((2, FEAT, HID), bf16),
            pltpu.VMEM((2, HID, FEAT), bf16),
            pltpu.SemaphoreType.DMA((2, 3)),
        ),
    )
    home = exchange(jnp.concatenate([out_rows, in_rows], axis=1))
    moe, grad_hidden, grad_gates = local_call(
        finish,
        held(home, kept) + fetched(gain, source, ids, slots, gates),
        [(COPY, (ROWS, FEAT), bf16), (COPY, (ROWS, FEAT), bf16), (COPY, (8, ROWS), f32)],
        8,
        (0, 1000),
    )
    return (moe, grad_hidden, grad_gates.T, *grads)


def solution(mesh):
    split = Mesh(mesh.devices.reshape(4, 2, 4, 4), ("y", "core", "x", "z"))
    heads, seq = ("y", "core"), ("x", "z")
    return jax.shard_map(
        on_device,
        mesh=split,
        in_specs=(
            P(seq, heads),
            P(heads),
            P(seq),
            P(seq, None),
            P(seq, None),
            P(seq, None),
            P(seq, None, heads),
            P(seq, None, heads),
            P(seq, heads, None),
            P(seq, heads),
        ),
        out_specs=(
            P(seq, heads),
            P(seq, heads),
            P(seq, None),
            P(seq, None, heads),
            P(seq, None, heads),
            P(seq, heads, None),
        ),
        check_vma=False,
    )
```

time: 124 us -> 104 us (0.84)
  blocking collectives: 18.9 us -> 0 us
  local copies, waits for them, and re-layouts: 16.5 us -> 0.13 us
  Pallas kernels: 18.4 us -> 30.1 us
  starting transfers between devices: 25.3 us -> 34 us
  waiting for transfers between devices: 39.7 us -> 36.6 us
  other arithmetic: 3.77 us -> 1.68 us
    all_to_all x1 -> x0, blocking collectives: 18.9 us -> none  [exchange(): lax.all_to_all(pieces, ('x', 'z'), 0, 0, tiled=True).reshape(ROWS, width)]
    unnamed x46 -> x40, local copies, waits for them, and re-layouts: 13.7 us -> 0.09 us
    pallas_call x5 -> x6, Pallas kernels: 18.4 us -> 30.1 us  [local_call(): pl.pallas_call(kernel, out_shape=out_shape, in_specs=in_specs, out_specs=...]
    all_to_all x1 -> x2, starting transfers between devices: 4.22 us -> 12.5 us  [exchange(): lax.all_to_all(pieces, ('x', 'z'), 0, 0, tiled=True).reshape(ROWS, width)]
    ppermute x12, waiting for transfers between devices: 34.8 us -> 29.4 us  [to_y(): return lax.ppermute(values, 'y', [(i, (i + step) % 4) for i in range(4)])]
    all_to_all x1 -> x2, waiting for transfers between devices: 1.05 us -> 5.58 us  [exchange(): lax.all_to_all(pieces, ('x', 'z'), 0, 0, tiled=True).reshape(ROWS, width)]
    ppermute x6 -> x15, waiting for transfers between devices: 3.87 us -> 1.59 us  [to_sibling(): return lax.ppermute(values, 'core', [(0, 1), (1, 0)])]
    slice x4 -> x2, local copies, waits for them, and re-layouts: 1.96 us -> 0.04 us  [gather(): block = sent[:, part]]
  transfers between devices with their start and end apart: 19 -> 29, of which waited for: 11 -> 13; matrix products, arithmetic and copies ran while one was open for 2% -> 1% of each run, Pallas kernels for 13% -> 25%
where the time goes in v2:
time: 104 us
  waiting for transfers between devices  36.6 us (35%)
  starting transfers between devices  34 us (33%)
  Pallas kernels  30.1 us (29%)
  other arithmetic  1.68 us (2%)
  between operations  1.06 us (1%)
    pallas_call x6, Pallas kernels, local_call(): pl.pallas_call(kernel, out_shape=out_shape, in_specs=in_specs, out_specs=...  30.1 us
    ppermute x12, waiting for transfers between devices, to_y(): return lax.ppermute(values, 'y', [(i, (i + step) % 4) for i in range(4)])  29.4 us
    ppermute x12, starting transfers between devices, to_y(): return lax.ppermute(values, 'y', [(i, (i + step) % 4) for i in range(4)])  18.4 us
    all_to_all x2, starting transfers between devices, exchange(): lax.all_to_all(pieces, ('x', 'z'), 0, 0, tiled=True).reshape(ROWS, width)  12.5 us
    all_to_all x2, waiting for transfers between devices, exchange(): lax.all_to_all(pieces, ('x', 'z'), 0, 0, tiled=True).reshape(ROWS, width)  5.58 us
    ppermute x15, starting transfers between devices, to_sibling(): return lax.ppermute(values, 'core', [(0, 1), (1, 0)])  3.1 us
  transfers between devices with their start and end apart: 29, of which 13 were waited for; matrix products, arithmetic and copies ran while one was open for 1% of the time, Pallas kernels for 25%

profile of v2, /device:TPU:0, one launch (start us, length us, event | category | flops | bytes accessed | tf_op | source)
XLA Modules:
  0.0 103.5 jit_solution(18364606118704845425)
XLA Ops:
  0.6 2.4 %shard_map.145 = (bf16[128,1920]{1,0:T(8,128)(2,1)}, bf16[128,896]{1,0:T(8,128)(2,1)S(1)}) custom-call(bf16[128,896]{1,0:T(8,128)(2,1)} %hidden.1, f32[896]{0:T(1024)} %gain.3, s32[1,128]{1,0:T(1,128)} %bitcast.25, s32[8,128]{1,0:T(8,128)} %bitcast.19, s32[8,128]{1,0:T(8,128)} %bitcast.21, f32[8,128]{1,0:T(8,128)} %bitcast.23, bf16[128,896]{1,0:T(8,128)(2,1)} %cotangent.1), custom_call_target="tpu_custom_call" | custom-call | bytes 1000 | tf_op jit(solution)/shard_map/pallas_call | solution.py:48
  3.0 8.0 %all-to-all-start = ((bf16[16,8,1920]{2,1,0:T(8,128)(2,1)}), bf16[16,8,1920]{2,1,0:T(8,128)(2,1)S(1)}, u32[]{:S(2)}, u32[]{:S(2)}) async-start(bf16[16,8,1920]{2,1,0:T(8,128)(2,1)} %bitcast.6), calls=%async_computation | async-start | bytes 983040 | tf_op jit(solution)/shard_map/all_to_all | solution.py:309
  11.0 7.5 %shard_map.146 = (bf16[256,7168]{1,0:T(8,128)(2,1)}, bf16[256,7168]{1,0:T(8,128)(2,1)}, bf16[7168,256]{1,0:T(8,128)(2,1)}) custom-call(bf16[1,7168,256]{2,1,0:T(8,128)(2,1)} %refs_8_.1, bf16[1,7168,256]{2,1,0:T(8,128)(2,1)} %refs_9_.1, bf16[1,256,7168]{2,1,0:T(8,128)(2,1)} %refs_10_.1), custom_call_target="tpu_custom_call" | custom-call | bytes 60000000 | tf_op jit(solution)/shard_map/pallas_call | solution.py:48
  18.5 3.6 %all-to-all-done = bf16[16,8,1920]{2,1,0:T(8,128)(2,1)S(1)} async-done(((bf16[16,8,1920]{2,1,0:T(8,128)(2,1)}), bf16[16,8,1920]{2,1,0:T(8,128)(2,1)S(1)}, u32[]{:S(2)}, u32[]{:S(2)}) %all-to-all-start) | async-done | bytes 491552 | tf_op jit(solution)/shard_map/all_to_all | solution.py:309
  22.2 3.3 %collective-permute-start.2 = (bf16[128,1024]{1,0:T(8,128)(2,1)S(1)}, bf16[128,1024]{1,0:T(8,128)(2,1)S(1)}, u32[]{:S(2)}, u32[]{:S(2)}) collective-permute-start(bf16[128,1024]{1,0:T(8,128)(2,1)S(1)} %slice.6), channel_id=1, source_target_pairs={{0,64},{32,96},{64,0},{96,32},{1,65},{33,97},{65,1},{97,33},{2,66}... | collective-permute-start | bytes 786440 | tf_op jit(solution)/shard_map/ppermute | solution.py:274
  25.4 1.1 %collective-permute-start.1 = (bf16[128,1024]{1,0:T(8,128)(2,1)S(1)}, bf16[128,1024]{1,0:T(8,128)(2,1)S(1)}, u32[]{:S(2)}, u32[]{:S(2)}) collective-permute-start(bf16[128,1024]{1,0:T(8,128)(2,1)S(1)} %slice.6), channel_id=1, source_target_pairs={{0,96},{32,0},{64,32},{96,64},{1,97},{33,1},{65,33},{97,65},{2,98}... | collective-permute-start | bytes 786440 | tf_op jit(solution)/shard_map/ppermute | solution.py:274
  26.5 1.0 collective-permute-start
  27.5 5.5 %collective-permute-done.2.refs_3_ = bf16[128,1024]{1,0:T(8,128)(2,1)S(1)} collective-permute-done((bf16[128,1024]{1,0:T(8,128)(2,1)S(1)}, bf16[128,1024]{1,0:T(8,128)(2,1)S(1)}, u32[]{:S(2)}, u32[]{:S(2)}) %collective-permute-start.2) | collective-permute-done | bytes 262176 | tf_op jit(solution)/shard_map/ppermute | solution.py:274
  33.0 3.3 %collective-permute-done.1.refs_2_ = bf16[128,1024]{1,0:T(8,128)(2,1)S(1)} collective-permute-done((bf16[128,1024]{1,0:T(8,128)(2,1)S(1)}, bf16[128,1024]{1,0:T(8,128)(2,1)S(1)}, u32[]{:S(2)}, u32[]{:S(2)}) %collective-permute-start.1) | collective-permute-done | bytes 262176 | tf_op jit(solution)/shard_map/ppermute | solution.py:274
  37.0 2.4 %collective-permute-start.10 = (bf16[128,896]{1,0:T(8,128)(2,1)S(1)}, bf16[128,896]{1,0:T(8,128)(2,1)S(1)}, u32[]{:S(2)}, u32[]{:S(2)}) collective-permute-start(bf16[128,896]{1,0:T(8,128)(2,1)S(1)} %slice.7), channel_id=1, source_target_pairs={{0,64},{32,96},{64,0},{96,32},{1,65},{33,97},{65,1},{97,33},{2,66}... | collective-permute-start | bytes 688136 | tf_op jit(solution)/shard_map/ppermute | solution.py:274
  39.4 1.6 %collective-permute-start.9 = (bf16[128,896]{1,0:T(8,128)(2,1)S(1)}, bf16[128,896]{1,0:T(8,128)(2,1)S(1)}, u32[]{:S(2)}, u32[]{:S(2)}) collective-permute-start(bf16[128,896]{1,0:T(8,128)(2,1)S(1)} %slice.7), channel_id=1, source_target_pairs={{0,96},{32,0},{64,32},{96,64},{1,97},{33,1},{65,33},{97,65},{2,98}... | collective-permute-start | bytes 688136 | tf_op jit(solution)/shard_map/ppermute | solution.py:274
  41.4 5.8 %shard_map.147 = (f32[128,256]{1,0:T(8,128)S(1)}, f32[128,256]{1,0:T(8,128)S(1)}, bf16[128,256]{1,0:T(8,128)(2,1)S(1)}, f32[128,128]{1,0:T(8,128)S(1)}, bf16[128...) custom-call(s32[2]{0:T(128)S(1)} %pad_add_fusion.where, ...), custom_call_target="tpu_custom_call" | custom-call | flops 10000000000 | bytes 1000 | tf_op jit(solution)/shard_map/pallas_call | solution.py:48
  47.9 3.2 %collective-permute-done.9.refs_2_.refs_9_ = bf16[128,896]{1,0:T(8,128)(2,1)S(1)} collective-permute-done((bf16[128,896]{1,0:T(8,128)(2,1)S(1)}, bf16[128,896]{1,0:T(8,128)(2,1)S(1)}, u32[]{:S(2)}, u32[]{:S(2)}) %collective-permute-start.9) | collective-permute-done | bytes 229408 | tf_op jit(solution)/shard_map/ppermute | solution.py:274
  52.2 1.0 %collective-permute-done.16 = bf16[128,896]{1,0:T(8,128)(2,1)S(1)} collective-permute-done((bf16[128,896]{1,0:T(8,128)(2,1)S(1)}, bf16[128,896]{1,0:T(8,128)(2,1)S(1)}, u32[]{:S(2)}, u32[]{:S(2)}) %collective-permute-start.16) | collective-permute-done | bytes 229408 | tf_op jit(solution)/shard_map/ppermute | solution.py:278
  53.3 1.2 %collective-permute-start.15 = (bf16[128,896]{1,0:T(8,128)(2,1)S(1)}, bf16[128,896]{1,0:T(8,128)(2,1)S(1)}, u32[]{:S(2)}, u32[]{:S(2)}) collective-permute-start(bf16[128,896]{1,0:T(8,128)(2,1)S(1)} %add_convert_fusion.8), channel_id=1, source_target_pairs={{0,32},{32,64},{64,96},{96,0},{1,33},{33,65},{65,97},{97,1},{2,34}... | collective-permute-start | bytes 688136 | tf_op jit(solution)/shard_map/ppermute | solution.py:274
  54.6 2.1 %collective-permute-start.17 = (bf16[128,896]{1,0:T(8,128)(2,1)S(1)}, bf16[128,896]{1,0:T(8,128)(2,1)S(1)}, u32[]{:S(2)}, u32[]{:S(2)}) collective-permute-start(bf16[128,896]{1,0:T(8,128)(2,1)S(1)} %add_convert_fusion.7), channel_id=1, source_target_pairs={{0,96},{32,0},{64,32},{96,64},{1,97},{33,1},{65,33},{97,65},{2,98}... | collective-permute-start | bytes 688136 | tf_op jit(solution)/shard_map/ppermute | solution.py:274
  56.7 1.4 %collective-permute-start.19 = (bf16[128,896]{1,0:T(8,128)(2,1)S(1)}, bf16[128,896]{1,0:T(8,128)(2,1)S(1)}, u32[]{:S(2)}, u32[]{:S(2)}) collective-permute-start(bf16[128,896]{1,0:T(8,128)(2,1)S(1)} %add_convert_fusion.6), channel_id=1, source_target_pairs={{0,64},{32,96},{64,0},{96,32},{1,65},{33,97},{65,1},{97,33},{2,66}... | collective-permute-start | bytes 688136 | tf_op jit(solution)/shard_map/ppermute | solution.py:274
  58.2 3.7 %shard_map.148 = (bf16[128,256]{1,0:T(8,128)(2,1)S(1)}, bf16[128,256]{1,0:T(8,128)(2,1)S(1)}, bf16[128,1024]{1,0:T(8,128)(2,1)S(1)}, bf16[128,1024]{1,0:T(8,128)...) custom-call(s32[2]{0:T(128)S(1)} %pad_add_fusion.where, ...), custom_call_target="tpu_custom_call" | custom-call | flops 10000000000 | bytes 1000 | tf_op jit(solution)/shard_map/pallas_call | solution.py:48
  62.2 4.4 %collective-permute-done.17 = bf16[128,896]{1,0:T(8,128)(2,1)S(1)} collective-permute-done((bf16[128,896]{1,0:T(8,128)(2,1)S(1)}, bf16[128,896]{1,0:T(8,128)(2,1)S(1)}, u32[]{:S(2)}, u32[]{:S(2)}) %collective-permute-start.17) | collective-permute-done | bytes 229408 | tf_op jit(solution)/shard_map/ppermute | solution.py:274
  66.5 1.4 %collective-permute-done.19 = bf16[128,896]{1,0:T(8,128)(2,1)S(1)} collective-permute-done((bf16[128,896]{1,0:T(8,128)(2,1)S(1)}, bf16[128,896]{1,0:T(8,128)(2,1)S(1)}, u32[]{:S(2)}, u32[]{:S(2)}) %collective-permute-start.19) | collective-permute-done | bytes 229408 | tf_op jit(solution)/shard_map/ppermute | solution.py:274
  69.0 0.5 collective-permute-done.21
  69.5 1.4 %collective-permute-start.22 = (bf16[128,1024]{1,0:T(8,128)(2,1)S(1)}, bf16[128,1024]{1,0:T(8,128)(2,1)S(1)}, u32[]{:S(2)}, u32[]{:S(2)}) collective-permute-start(bf16[128,1024]{1,0:T(8,128)(2,1)S(1)} %add_convert_fusion.3), channel_id=1, source_target_pairs={{0,32},{32,64},{64,96},{96,0},{1,33},{33,65},{65,97},{97,1},{2,34}... | collective-permute-start | bytes 786440 | tf_op jit(solution)/shard_map/ppermute | solution.py:274
  71.0 2.0 %collective-permute-start.24 = (bf16[128,1024]{1,0:T(8,128)(2,1)S(1)}, bf16[128,1024]{1,0:T(8,128)(2,1)S(1)}, u32[]{:S(2)}, u32[]{:S(2)}) collective-permute-start(bf16[128,1024]{1,0:T(8,128)(2,1)S(1)} %add_convert_fusion.2), channel_id=1, source_target_pairs={{0,96},{32,0},{64,32},{96,64},{1,97},{33,1},{65,33},{97,65},{2,98}... | collective-permute-start | bytes 786440 | tf_op jit(solution)/shard_map/ppermute | solution.py:274
  73.1 0.6 collective-permute-start.26
  73.8 5.7 %collective-permute-done.22 = bf16[128,1024]{1,0:T(8,128)(2,1)S(1)} collective-permute-done((bf16[128,1024]{1,0:T(8,128)(2,1)S(1)}, bf16[128,1024]{1,0:T(8,128)(2,1)S(1)}, u32[]{:S(2)}, u32[]{:S(2)}) %collective-permute-start.22) | collective-permute-done | bytes 262176 | tf_op jit(solution)/shard_map/ppermute | solution.py:274
  79.5 4.7 %collective-permute-done.24 = bf16[128,1024]{1,0:T(8,128)(2,1)S(1)} collective-permute-done((bf16[128,1024]{1,0:T(8,128)(2,1)S(1)}, bf16[128,1024]{1,0:T(8,128)(2,1)S(1)}, u32[]{:S(2)}, u32[]{:S(2)}) %collective-permute-start.24) | collective-permute-done | bytes 262176 | tf_op jit(solution)/shard_map/ppermute | solution.py:274
  84.2 1.0 %collective-permute-done.26 = bf16[128,1024]{1,0:T(8,128)(2,1)S(1)} collective-permute-done((bf16[128,1024]{1,0:T(8,128)(2,1)S(1)}, bf16[128,1024]{1,0:T(8,128)(2,1)S(1)}, u32[]{:S(2)}, u32[]{:S(2)}) %collective-permute-start.26) | collective-permute-done | bytes 262176 | tf_op jit(solution)/shard_map/ppermute | solution.py:274
  85.5 0.8 maximum_bitcast_fusion
  86.3 4.5 %all-to-all-start.1 = ((bf16[16,8,1920]{2,1,0:T(8,128)(2,1)}), bf16[16,8,1920]{2,1,0:T(8,128)(2,1)S(1)}, u32[]{:S(2)}, u32[]{:S(2)}) async-start(bf16[16,8,1920]{2,1,0:T(8,128)(2,1)} %maximum_bitcast_fusion), calls=%async_computation.1 | async-start | bytes 983040 | tf_op jit(solution)/shard_map/all_to_all | solution.py:309
  90.9 8.6 %shard_map.150 = (bf16[1,7168,256]{2,1,0:T(8,128)(2,1)}, bf16[1,7168,256]{2,1,0:T(8,128)(2,1)}, bf16[1,256,7168]{2,1,0:T(8,128)(2,1)}) custom-call(s32[2]{0:T(128)S(1)} %pad_add_fusion.where, bf16[128,1920]{1,0:T(8,128)(2,1)} %bitcast.18, bf16[128,1024]{1,0:T(8,128)(2,1)} %copy-done.7, bf16[128,1024]{1,0:T(8,128)(2,1)} %copy-done.6, ...), custom_call_target="tpu_custom_call" | custom-call | flops 2818572288 | bytes 22000000 | tf_op jit(solution)/shard_map/pallas_call | solution.py:48
  99.5 2.0 %all-to-all-done.1 = bf16[16,8,1920]{2,1,0:T(8,128)(2,1)S(1)} async-done(((bf16[16,8,1920]{2,1,0:T(8,128)(2,1)}), bf16[16,8,1920]{2,1,0:T(8,128)(2,1)S(1)}, u32[]{:S(2)}, u32[]{:S(2)}) %all-to-all-start.1) | async-done | bytes 491552 | tf_op jit(solution)/shard_map/all_to_all | solution.py:309
  101.5 2.0 %shard_map.149 = (bf16[128,896]{1,0:T(8,128)(2,1)}, bf16[128,896]{1,0:T(8,128)(2,1)}, f32[8,128]{1,0:T(8,128)}) custom-call(bf16[128,1920]{1,0:T(8,128)(2,1)S(1)} %bitcast.12, bf16[128,896]{1,0:T(8,128)(2,1)S(1)} %get-tuple-element.93.hidden, f32[896]{0:T(1024)} %gain.3, s32[1,128]{1,0:T(1,128)} %bitcast.26, s32[8,128]{1,0:T(8,128)} %bitcast.20, ...), custom_call_target="tpu_custom_call" | custom-call | bytes 1000 | tf_op jit(solution)/shard_map/pallas_call | solution.py:48
  (84 shorter events, 4.8 us)
Async XLA Ops:
  3.0 19.1 %all-to-all-start = ((bf16[16,8,1920]{2,1,0:T(8,128)(2,1)}), bf16[16,8,1920]{2,1,0:T(8,128)(2,1)S(1)}, u32[]{:S(2)}, u32[]{:S(2)}) async-start(bf16[16,8,1920]{2,1,0:T(8,128)(2,1)} %bitcast.6), calls=%async_computation | async-start | bytes 983040 | tf_op jit(solution)/shard_map/all_to_all | solution.py:309
  22.1 36.0 %copy-start = (bf16[16,8,1920]{2,1,0:T(8,128)(2,1)}, bf16[16,8,1920]{2,1,0:T(8,128)(2,1)S(1)}, u32[]{:S(2)}) copy-start(bf16[16,8,1920]{2,1,0:T(8,128)(2,1)S(1)} %all-to-all-done) | copy-start | bytes 1474564
  22.2 10.8 %collective-permute-start.2 = (bf16[128,1024]{1,0:T(8,128)(2,1)S(1)}, bf16[128,1024]{1,0:T(8,128)(2,1)S(1)}, u32[]{:S(2)}, u32[]{:S(2)}) collective-permute-start(bf16[128,1024]{1,0:T(8,128)(2,1)S(1)} %slice.6), channel_id=1, source_target_pairs={{0,64},{32,96},{64,0},{96,32},{1,65},{33,97},{65,1},{97,33},{2,66}... | collective-permute-start | bytes 786440 | tf_op jit(solution)/shard_map/ppermute | solution.py:274
  25.4 10.9 %collective-permute-start.1 = (bf16[128,1024]{1,0:T(8,128)(2,1)S(1)}, bf16[128,1024]{1,0:T(8,128)(2,1)S(1)}, u32[]{:S(2)}, u32[]{:S(2)}) collective-permute-start(bf16[128,1024]{1,0:T(8,128)(2,1)S(1)} %slice.6), channel_id=1, source_target_pairs={{0,96},{32,0},{64,32},{96,64},{1,97},{33,1},{65,33},{97,65},{2,98}... | collective-permute-start | bytes 786440 | tf_op jit(solution)/shard_map/ppermute | solution.py:274
  26.5 9.9 %collective-permute-start = (bf16[128,1024]{1,0:T(8,128)(2,1)S(1)}, bf16[128,1024]{1,0:T(8,128)(2,1)S(1)}, u32[]{:S(2)}, u32[]{:S(2)}) collective-permute-start(bf16[128,1024]{1,0:T(8,128)(2,1)S(1)} %slice.6), channel_id=1, source_target_pairs={{0,32},{32,64},{64,96},{96,0},{1,33},{33,65},{65,97},{97,1},{2,34}... | collective-permute-start | bytes 786440 | tf_op jit(solution)/shard_map/ppermute | solution.py:274
  27.5 11.9 %collective-permute-start.3 = (bf16[128,1920]{1,0:T(8,128)(2,1)S(1)}, bf16[128,1920]{1,0:T(8,128)(2,1)S(1)}, u32[]{:S(2)}, u32[]{:S(2)}) collective-permute-start(bf16[128,1920]{1,0:T(8,128)(2,1)S(1)} %bitcast.14), channel_id=1, source_target_pairs={{0,16},{16,0},{1,17},{17,1},{2,18},{18,2},{3,19},{19,3},{4,20},{20... | collective-permute-start | bytes 1474568 | tf_op jit(solution)/shard_map/ppermute | solution.py:278
  33.0 7.9 %collective-permute-start.6 = (bf16[128,1024]{1,0:T(8,128)(2,1)S(1)}, bf16[128,1024]{1,0:T(8,128)(2,1)S(1)}, u32[]{:S(2)}, u32[]{:S(2)}) collective-permute-start(bf16[128,1024]{1,0:T(8,128)(2,1)S(1)} %collective-permute-done.2.refs_3_), channel_id=1, source_target_pairs={{0,16},{16,0},{1,17},{17,1},{2,18},{18,2},{3,19},{19,3},{4,20},{20... | collective-permute-start | bytes 786440 | tf_op jit(solution)/shard_map/ppermute | solution.py:278
  36.4 5.1 %collective-permute-start.5 = (bf16[128,1024]{1,0:T(8,128)(2,1)S(1)}, bf16[128,1024]{1,0:T(8,128)(2,1)S(1)}, u32[]{:S(2)}, u32[]{:S(2)}) collective-permute-start(bf16[128,1024]{1,0:T(8,128)(2,1)S(1)} %collective-permute-done.1.refs_2_), channel_id=1, source_target_pairs={{0,16},{16,0},{1,17},{17,1},{2,18},{18,2},{3,19},{19,3},{4,20},{20... | collective-permute-start | bytes 786440 | tf_op jit(solution)/shard_map/ppermute | solution.py:278
  36.4 5.1 %collective-permute-start.4 = (bf16[128,1024]{1,0:T(8,128)(2,1)S(1)}, bf16[128,1024]{1,0:T(8,128)(2,1)S(1)}, u32[]{:S(2)}, u32[]{:S(2)}) collective-permute-start(bf16[128,1024]{1,0:T(8,128)(2,1)S(1)} %collective-permute-done.refs_1_), channel_id=1, source_target_pairs={{0,16},{16,0},{1,17},{17,1},{2,18},{18,2},{3,19},{19,3},{4,20},{20... | collective-permute-start | bytes 786440 | tf_op jit(solution)/shard_map/ppermute | solution.py:278
  37.0 10.4 %collective-permute-start.10 = (bf16[128,896]{1,0:T(8,128)(2,1)S(1)}, bf16[128,896]{1,0:T(8,128)(2,1)S(1)}, u32[]{:S(2)}, u32[]{:S(2)}) collective-permute-start(bf16[128,896]{1,0:T(8,128)(2,1)S(1)} %slice.7), channel_id=1, source_target_pairs={{0,64},{32,96},{64,0},{96,32},{1,65},{33,97},{65,1},{97,33},{2,66}... | collective-permute-start | bytes 688136 | tf_op jit(solution)/shard_map/ppermute | solution.py:274
  39.4 11.7 %collective-permute-start.9 = (bf16[128,896]{1,0:T(8,128)(2,1)S(1)}, bf16[128,896]{1,0:T(8,128)(2,1)S(1)}, u32[]{:S(2)}, u32[]{:S(2)}) collective-permute-start(bf16[128,896]{1,0:T(8,128)(2,1)S(1)} %slice.7), channel_id=1, source_target_pairs={{0,96},{32,0},{64,32},{96,64},{1,97},{33,1},{65,33},{97,65},{2,98}... | collective-permute-start | bytes 688136 | tf_op jit(solution)/shard_map/ppermute | solution.py:274
  40.9 10.2 %collective-permute-start.8 = (bf16[128,896]{1,0:T(8,128)(2,1)S(1)}, bf16[128,896]{1,0:T(8,128)(2,1)S(1)}, u32[]{:S(2)}, u32[]{:S(2)}) collective-permute-start(bf16[128,896]{1,0:T(8,128)(2,1)S(1)} %slice.7), channel_id=1, source_target_pairs={{0,32},{32,64},{64,96},{96,0},{1,33},{33,65},{65,97},{97,1},{2,34}... | collective-permute-start | bytes 688136 | tf_op jit(solution)/shard_map/ppermute | solution.py:274
  47.3 4.4 %collective-permute-start.14 = (bf16[128,896]{1,0:T(8,128)(2,1)S(1)}, bf16[128,896]{1,0:T(8,128)(2,1)S(1)}, u32[]{:S(2)}, u32[]{:S(2)}) collective-permute-start(bf16[128,896]{1,0:T(8,128)(2,1)S(1)} %get-tuple-element.77), channel_id=1, source_target_pairs={{0,16},{16,0},{1,17},{17,1},{2,18},{18,2},{3,19},{19,3},{4,20},{20... | collective-permute-start | bytes 688136 | tf_op jit(solution)/shard_map/ppermute | solution.py:278
  47.5 9.3 %collective-permute-start.13 = (bf16[128,896]{1,0:T(8,128)(2,1)S(1)}, bf16[128,896]{1,0:T(8,128)(2,1)S(1)}, u32[]{:S(2)}, u32[]{:S(2)}) collective-permute-start(bf16[128,896]{1,0:T(8,128)(2,1)S(1)} %collective-permute-done.10.refs_3_.refs_10_), channel_id=1, source_target_pairs={{0,16},{16,0},{1,17},{17,1},{2,18},{18,2},{3,19},{19,3},{4,20},{20... | collective-permute-start | bytes 688136 | tf_op jit(solution)/shard_map/ppermute | solution.py:278
  51.1 7.1 %collective-permute-start.12 = (bf16[128,896]{1,0:T(8,128)(2,1)S(1)}, bf16[128,896]{1,0:T(8,128)(2,1)S(1)}, u32[]{:S(2)}, u32[]{:S(2)}) collective-permute-start(bf16[128,896]{1,0:T(8,128)(2,1)S(1)} %collective-permute-done.9.refs_2_.refs_9_), channel_id=1, source_target_pairs={{0,16},{16,0},{1,17},{17,1},{2,18},{18,2},{3,19},{19,3},{4,20},{20... | collective-permute-start | bytes 688136 | tf_op jit(solution)/shard_map/ppermute | solution.py:278
  51.1 7.0 %collective-permute-start.11 = (bf16[128,896]{1,0:T(8,128)(2,1)S(1)}, bf16[128,896]{1,0:T(8,128)(2,1)S(1)}, u32[]{:S(2)}, u32[]{:S(2)}) collective-permute-start(bf16[128,896]{1,0:T(8,128)(2,1)S(1)} %collective-permute-done.8.refs_1_.refs_8_), channel_id=1, source_target_pairs={{0,16},{16,0},{1,17},{17,1},{2,18},{18,2},{3,19},{19,3},{4,20},{20... | collective-permute-start | bytes 688136 | tf_op jit(solution)/shard_map/ppermute | solution.py:278
  51.6 1.6 %collective-permute-start.16 = (bf16[128,896]{1,0:T(8,128)(2,1)S(1)}, bf16[128,896]{1,0:T(8,128)(2,1)S(1)}, u32[]{:S(2)}, u32[]{:S(2)}) collective-permute-start(bf16[128,896]{1,0:T(8,128)(2,1)S(1)} %get-tuple-element.79), channel_id=1, source_target_pairs={{0,16},{16,0},{1,17},{17,1},{2,18},{18,2},{3,19},{19,3},{4,20},{20... | collective-permute-start | bytes 688136 | tf_op jit(solution)/shard_map/ppermute | solution.py:278
  51.7 2.9 %collective-permute-start.18 = (bf16[128,896]{1,0:T(8,128)(2,1)S(1)}, bf16[128,896]{1,0:T(8,128)(2,1)S(1)}, u32[]{:S(2)}, u32[]{:S(2)}) collective-permute-start(bf16[128,896]{1,0:T(8,128)(2,1)S(1)} %get-tuple-element.81), channel_id=1, source_target_pairs={{0,16},{16,0},{1,17},{17,1},{2,18},{18,2},{3,19},{19,3},{4,20},{20... | collective-permute-start | bytes 688136 | tf_op jit(solution)/shard_map/ppermute | solution.py:278
  53.3 8.9 %collective-permute-start.15 = (bf16[128,896]{1,0:T(8,128)(2,1)S(1)}, bf16[128,896]{1,0:T(8,128)(2,1)S(1)}, u32[]{:S(2)}, u32[]{:S(2)}) collective-permute-start(bf16[128,896]{1,0:T(8,128)(2,1)S(1)} %add_convert_fusion.8), channel_id=1, source_target_pairs={{0,32},{32,64},{64,96},{96,0},{1,33},{33,65},{65,97},{97,1},{2,34}... | collective-permute-start | bytes 688136 | tf_op jit(solution)/shard_map/ppermute | solution.py:274
  54.6 11.9 %collective-permute-start.17 = (bf16[128,896]{1,0:T(8,128)(2,1)S(1)}, bf16[128,896]{1,0:T(8,128)(2,1)S(1)}, u32[]{:S(2)}, u32[]{:S(2)}) collective-permute-start(bf16[128,896]{1,0:T(8,128)(2,1)S(1)} %add_convert_fusion.7), channel_id=1, source_target_pairs={{0,96},{32,0},{64,32},{96,64},{1,97},{33,1},{65,33},{97,65},{2,98}... | collective-permute-start | bytes 688136 | tf_op jit(solution)/shard_map/ppermute | solution.py:274
  56.7 11.2 %collective-permute-start.19 = (bf16[128,896]{1,0:T(8,128)(2,1)S(1)}, bf16[128,896]{1,0:T(8,128)(2,1)S(1)}, u32[]{:S(2)}, u32[]{:S(2)}) collective-permute-start(bf16[128,896]{1,0:T(8,128)(2,1)S(1)} %add_convert_fusion.6), channel_id=1, source_target_pairs={{0,64},{32,96},{64,0},{96,32},{1,65},{33,97},{65,1},{97,33},{2,66}... | collective-permute-start | bytes 688136 | tf_op jit(solution)/shard_map/ppermute | solution.py:274
  62.0 23.5 %copy-start.18 = (bf16[128,256]{1,0:T(8,128)(2,1)}, bf16[128,256]{1,0:T(8,128)(2,1)S(1)}, u32[]{:S(2)}) copy-start(bf16[128,256]{1,0:T(8,128)(2,1)S(1)} %get-tuple-element.97.refs_15_) | copy-start | bytes 196612
  62.0 23.5 %copy-start.19 = (bf16[128,256]{1,0:T(8,128)(2,1)}, bf16[128,256]{1,0:T(8,128)(2,1)S(1)}, u32[]{:S(2)}) copy-start(bf16[128,256]{1,0:T(8,128)(2,1)S(1)} %get-tuple-element.98.refs_16_) | copy-start | bytes 196612
  67.9 1.5 %collective-permute-start.21 = (bf16[128,1024]{1,0:T(8,128)(2,1)S(1)}, bf16[128,1024]{1,0:T(8,128)(2,1)S(1)}, u32[]{:S(2)}, u32[]{:S(2)}) collective-permute-start(bf16[128,1024]{1,0:T(8,128)(2,1)S(1)} %get-tuple-element.88), channel_id=1, source_target_pairs={{0,16},{16,0},{1,17},{17,1},{2,18},{18,2},{3,19},{19,3},{4,20},{20... | collective-permute-start | bytes 786440 | tf_op jit(solution)/shard_map/ppermute | solution.py:278
  67.9 3.0 %collective-permute-start.23 = (bf16[128,1024]{1,0:T(8,128)(2,1)S(1)}, bf16[128,1024]{1,0:T(8,128)(2,1)S(1)}, u32[]{:S(2)}, u32[]{:S(2)}) collective-permute-start(bf16[128,1024]{1,0:T(8,128)(2,1)S(1)} %get-tuple-element.90), channel_id=1, source_target_pairs={{0,16},{16,0},{1,17},{17,1},{2,18},{18,2},{3,19},{19,3},{4,20},{20... | collective-permute-start | bytes 786440 | tf_op jit(solution)/shard_map/ppermute | solution.py:278
  68.4 5.2 %collective-permute-start.7 = (bf16[128,896]{1,0:T(8,128)(2,1)S(1)}, bf16[128,896]{1,0:T(8,128)(2,1)S(1)}, u32[]{:S(2)}, u32[]{:S(2)}) collective-permute-start(bf16[128,896]{1,0:T(8,128)(2,1)S(1)} %get-tuple-element.60), channel_id=1, source_target_pairs={{0,16},{16,0},{1,17},{17,1},{2,18},{18,2},{3,19},{19,3},{4,20},{20... | collective-permute-start | bytes 688136 | tf_op jit(solution)/shard_map/ppermute | solution.py:278
  68.4 5.4 %collective-permute-start.20 = (bf16[128,1024]{1,0:T(8,128)(2,1)S(1)}, bf16[128,1024]{1,0:T(8,128)(2,1)S(1)}, u32[]{:S(2)}, u32[]{:S(2)}) collective-permute-start(bf16[128,1024]{1,0:T(8,128)(2,1)S(1)} %get-tuple-element.86), channel_id=1, source_target_pairs={{0,16},{16,0},{1,17},{17,1},{2,18},{18,2},{3,19},{19,3},{4,20},{20... | collective-permute-start | bytes 786440 | tf_op jit(solution)/shard_map/ppermute | solution.py:278
  69.0 4.0 %collective-permute-start.25 = (bf16[128,1024]{1,0:T(8,128)(2,1)S(1)}, bf16[128,1024]{1,0:T(8,128)(2,1)S(1)}, u32[]{:S(2)}, u32[]{:S(2)}) collective-permute-start(bf16[128,1024]{1,0:T(8,128)(2,1)S(1)} %get-tuple-element.92), channel_id=1, source_target_pairs={{0,16},{16,0},{1,17},{17,1},{2,18},{18,2},{3,19},{19,3},{4,20},{20... | collective-permute-start | bytes 786440 | tf_op jit(solution)/shard_map/ppermute | solution.py:278
  69.5 9.9 %collective-permute-start.22 = (bf16[128,1024]{1,0:T(8,128)(2,1)S(1)}, bf16[128,1024]{1,0:T(8,128)(2,1)S(1)}, u32[]{:S(2)}, u32[]{:S(2)}) collective-permute-start(bf16[128,1024]{1,0:T(8,128)(2,1)S(1)} %add_convert_fusion.3), channel_id=1, source_target_pairs={{0,32},{32,64},{64,96},{96,0},{1,33},{33,65},{65,97},{97,1},{2,34}... | collective-permute-start | bytes 786440 | tf_op jit(solution)/shard_map/ppermute | solution.py:274
  71.0 13.3 %collective-permute-start.24 = (bf16[128,1024]{1,0:T(8,128)(2,1)S(1)}, bf16[128,1024]{1,0:T(8,128)(2,1)S(1)}, u32[]{:S(2)}, u32[]{:S(2)}) collective-permute-start(bf16[128,1024]{1,0:T(8,128)(2,1)S(1)} %add_convert_fusion.2), channel_id=1, source_target_pairs={{0,96},{32,0},{64,32},{96,64},{1,97},{33,1},{65,33},{97,65},{2,98}... | collective-permute-start | bytes 786440 | tf_op jit(solution)/shard_map/ppermute | solution.py:274
  73.1 12.2 %collective-permute-start.26 = (bf16[128,1024]{1,0:T(8,128)(2,1)S(1)}, bf16[128,1024]{1,0:T(8,128)(2,1)S(1)}, u32[]{:S(2)}, u32[]{:S(2)}) collective-permute-start(bf16[128,1024]{1,0:T(8,128)(2,1)S(1)} %add_convert_fusion.1), channel_id=1, source_target_pairs={{0,64},{32,96},{64,0},{96,32},{1,65},{33,97},{65,1},{97,33},{2,66}... | collective-permute-start | bytes 786440 | tf_op jit(solution)/shard_map/ppermute | solution.py:274
  86.3 15.1 %all-to-all-start.1 = ((bf16[16,8,1920]{2,1,0:T(8,128)(2,1)}), bf16[16,8,1920]{2,1,0:T(8,128)(2,1)S(1)}, u32[]{:S(2)}, u32[]{:S(2)}) async-start(bf16[16,8,1920]{2,1,0:T(8,128)(2,1)} %maximum_bitcast_fusion), calls=%async_computation.1 | async-start | bytes 983040 | tf_op jit(solution)/shard_map/all_to_all | solution.py:309
  (17 other events, 200.3 us)

commit v3 on v2

--- a/solution.py
+++ b/solution.py
@@ -10,10 +10,11 @@
 ROWS = 128
 FEAT = 896
 WIDE = 1024
+BOTH = WIDE + FEAT
 HID = 256
 EPSILON = 1e-06
-GATHERED = (0, 3, 1, 2)
-HOMEWARD = (0, 1, 3, 2)
+OFFSETS = (0, 1, 3, 2)
+HALF = ROWS // 2
 
 f32 = jnp.float32
 bf16 = jnp.bfloat16
@@ -150,56 +151,72 @@
     return pl.ds(pl.multiple_of(head * FEAT, 128), FEAT)
 
 
-def forward(where, *refs):
-    blocks, weights, (pre_gate, pre_up, act, scale) = refs[:8], refs[8:11], refs[11:15]
-    own, other, (w_gate, w_up, w_down, sems) = refs[15:19], refs[19:23], refs[23:]
-    loads = [
-        pltpu.make_async_copy(source, target, sems.at[i])
-        for i, (source, target) in enumerate(zip(weights, (w_gate, w_up, w_down)))
-    ]
-    for load in loads:
-        load.start()
-    mean = jnp.zeros((ROWS, WIDE - FEAT), f32)
-    for block in blocks:
-        mean = mean + block[:, FEAT:WIDE].astype(f32)
-    pre = []
-    for load, weight in zip(loads, (w_gate, w_up)):
-        load.wait()
-        total = jnp.zeros((ROWS, HID), f32)
-        for n, block in enumerate(blocks):
-            rows = row_part(head_at(where, GATHERED[n % 4], n // 4))
-            total = total + nn(block[:, :FEAT], weight[0, rows, :])
-        pre.append(total)
-    gate, up = pre
-    inverse = lax.rsqrt(jnp.sum(mean, axis=1, keepdims=True) + EPSILON)
+def first_blocks(where, *refs):
+    blocks, (w_gate, w_up, w_down_t) = refs[:6], refs[6:9]
+    gate, up, hid, mean, late_gate, late_up, late_down = refs[9:16]
+    rows_gate, rows_up, rows_down, sems = refs[16:]
+    loads, late = [], []
+    for n in range(8):
+        side, i = divmod(n, 4)
+        head = head_at(where, OFFSETS[i], side)
+        part = row_part(head)
+        for j, (source, early, later) in enumerate(
+            (
+                (w_gate.at[0], rows_gate, late_gate),
+                (w_up.at[0], rows_up, late_up),
+                (w_down_t, rows_down, late_down),
+            )
+        ):
+            target = later.at[side] if i == 3 else early.at[3 * side + i]
+            copy = pltpu.make_async_copy(source.at[part, :], target, sems.at[n, j])
+            (late if i == 3 else loads).append(copy)
+    for copy in loads + late:
+        copy.start()
+    totals = [jnp.zeros((ROWS, HID), f32) for _ in range(3)]
+    squares = jnp.zeros((ROWS, WIDE - FEAT), f32)
+    for n, block in enumerate(blocks):
+        squares = squares + block[:, FEAT:WIDE].astype(f32)
+        for j, weight in enumerate((rows_gate, rows_up, rows_down)):
+            loads[3 * n + j].wait()
+            columns = slice(0, FEAT) if j < 2 else slice(WIDE, BOTH)
+            totals[j] = totals[j] + nn(block[:, columns], weight[n])
+    for copy in late:
+        copy.wait()
+    gate[...], up[...], hid[...] = totals
+    mean[...] = squares
+
+
+def expert_terms(where, act, d_gate, d_up, w_down, gate_t, up_t, side, results, tail):
+    for i in (3, 1, 2, 0):
+        columns = column_part(head_at(where, OFFSETS[i], side))
+        results[i][:, :FEAT] = nn(act, w_down[0, :, columns]).astype(bf16)
+        term = nn(d_gate, gate_t[:, columns]) + nn(d_up, up_t[:, columns])
+        results[i][:, FEAT : FEAT + FEAT] = term.astype(bf16)
+        results[i][:, FEAT + FEAT :] = tail
+
+
+def last_blocks(where, *refs):
+    halves, (late_gate, late_up, late_down) = refs[:4], refs[4:7]
+    first_gate, first_up, first_hid, mean, w_down, gate_t, up_t = refs[7:14]
+    act, grad_gate, grad_up, tail_out, *other = refs[14:]
+    gate, up, hid = first_gate[...], first_up[...], first_hid[...]
+    squares = mean[...]
+    for side in range(2):
+        block = jnp.concatenate([halves[2 * side][...], halves[2 * side + 1][...]], axis=0)
+        squares = squares + block[:, FEAT:WIDE].astype(f32)
+        gate = gate + nn(block[:, :FEAT], late_gate[side])
+        up = up + nn(block[:, :FEAT], late_up[side])
+        hid = hid + nn(block[:, WIDE:], late_down[side])
+    inverse = lax.rsqrt(jnp.sum(squares, axis=1, keepdims=True) + EPSILON)
     gate = gate * inverse
     up = up * inverse
-    hidden_act = (gate * jax.nn.sigmoid(gate) * up).astype(bf16)
-    pre_gate[...] = gate
-    pre_up[...] = up
-    act[...] = hidden_act
-    scale[...] = jnp.broadcast_to(inverse, (ROWS, 128))
-    loads[2].wait()
-    for side, result in ((1, other), (0, own)):
-        for i, offset in enumerate(HOMEWARD):
-            columns = column_part(head_at(where, offset, side))
-            result[i][...] = nn(hidden_act, w_down[0, :, columns]).astype(bf16)
-
-
-def backward(where, *refs):
-    blocks = refs[:8]
-    gate_t, up_t, down_t, pre_gate, pre_up, act, scale, grad_gate, grad_up = refs[8:17]
-    own, other = refs[17:21], refs[21:25]
-    hid = jnp.zeros((ROWS, HID), f32)
-    for n, block in enumerate(blocks):
-        hid = hid + nn(g_part(block)[...], down_t[row_part(head_at(where, GATHERED[n % 4], n // 4)), :])
-    gate, up = pre_gate[...], pre_up[...]
-    inverse = scale[:, 0:1]
     sigmoid = jax.nn.sigmoid(gate)
-    score = jnp.sum(act[...].astype(f32) * hid, axis=1, keepdims=True)
+    hidden_act = (gate * sigmoid * up).astype(bf16)
+    score = jnp.sum(hidden_act.astype(f32) * hid, axis=1, keepdims=True)
     scaled = hid * inverse
     d_gate = (scaled * up * sigmoid * (1.0 + gate * (1.0 - sigmoid))).astype(bf16)
     d_up = (scaled * gate * sigmoid).astype(bf16)
+    act[...] = hidden_act
     grad_gate[...] = d_gate
     grad_up[...] = d_up
     dot = jnp.sum(d_gate.astype(f32) * gate + d_up.astype(f32) * up, axis=1, keepdims=True)
@@ -212,29 +229,33 @@
         tail = jnp.where(lane == base + me, high.astype(f32), tail)
         tail = jnp.where(lane == base + me + 1, low.astype(f32), tail)
     tail = tail.astype(bf16)
-    for side, result in ((1, other), (0, own)):
-        for i, offset in enumerate(HOMEWARD):
-            columns = column_part(head_at(where, offset, side))
-            term = nn(d_gate, gate_t[:, columns]) + nn(d_up, up_t[:, columns])
-            result[i][:, :FEAT] = term.astype(bf16)
-            result[i][:, FEAT:] = tail
+    tail_out[...] = tail
+    expert_terms(where, hidden_act, d_gate, d_up, w_down, gate_t, up_t, 1, other, tail)
+
+
+def own_terms(where, act, grad_gate, grad_up, tail, w_down, gate_t, up_t, *own):
+    expert_terms(where, act[...], grad_gate[...], grad_up[...], w_down, gate_t, up_t, 0, own, tail[...])
 
 
 def weight_grads(where, *refs):
-    x_blocks = refs[:8]
-    g_blocks = (refs[0], *refs[8:11], refs[4], *refs[11:14])
-    act, grad_gate, grad_up, out_gate, out_up, out_down, buf_gate, buf_up, buf_down, sems = refs[14:]
+    blocks = refs[:3], refs[3:5], refs[5:8], refs[8:10]
+    act, grad_gate, grad_up, out_gate, out_up, out_down, buf_gate, buf_up, buf_down, sems = refs[10:]
     act_t = act[...].T
     pending = {}
     for n in range(8):
+        side, i = divmod(n, 4)
         slot = n % 2
-        head = head_at(where, GATHERED[n % 4], n // 4)
+        head = head_at(where, OFFSETS[i], side)
         for copy in pending.get(slot, ()):
             copy.wait()
-        x_t = x_blocks[n][:, :FEAT].T
-        buf_gate[slot] = nn(x_t, grad_gate[...]).astype(bf16)
-        buf_up[slot] = nn(x_t, grad_up[...]).astype(bf16)
-        buf_down[slot] = nn(act_t, g_part(g_blocks[n])[...]).astype(bf16)
+        if i < 3:
+            block = blocks[2 * side][i][...]
+        else:
+            block = jnp.concatenate([half[...] for half in blocks[2 * side + 1]], axis=0)
+        beam_t = block[:, :FEAT].T
+        buf_gate[slot] = nn(beam_t, grad_gate[...]).astype(bf16)
+        buf_up[slot] = nn(beam_t, grad_up[...]).astype(bf16)
+        buf_down[slot] = nn(act_t, block[:, WIDE:]).astype(bf16)
         pending[slot] = [
             pltpu.make_async_copy(buf_gate.at[slot], out_gate.at[0, row_part(head), :], sems.at[slot, 0]),
             pltpu.make_async_copy(buf_up.at[slot], out_up.at[0, row_part(head), :], sems.at[slot, 1]),
@@ -278,27 +299,17 @@
     return lax.ppermute(values, "core", [(0, 1), (1, 0)])
 
 
-def gather(sent, sibling, part):
-    block = sent[:, part]
-    far = [to_y(block, 1), to_y(block, 3), to_y(block, 2)]
-    return [sent, *far, sibling, *[to_sibling(value) for value in far]]
-
-
-def g_part(block):
-    return block if block.shape[1] == FEAT else block.at[:, WIDE:]
-
-
-def chip_sums(own, other):
-    return [(mine.astype(f32) + to_sibling(theirs).astype(f32)).astype(bf16) for mine, theirs in zip(own, other)]
-
-
 def sent_home(sums):
-    return [to_y(sums[1], 1), to_y(sums[2], 3), to_y(sums[3], 2)]
-
-
-def row_sum(mine, parts):
-    total = mine.astype(f32)
-    for part in parts:
+    mine, above, below, across = sums
+    for_above, for_below = to_y(across[:HALF], 1), to_y(across[HALF:], 3)
+    above = joined(above, jnp.pad(for_above, ((0, HALF), (0, 0))))
+    below = joined(below, jnp.pad(for_below, ((HALF, 0), (0, 0))))
+    return joined(mine, to_y(above, 1), to_y(below, 3))
+
+
+def joined(*parts):
+    total = parts[0].astype(f32)
+    for part in parts[1:]:
         total = total + part.astype(f32)
     return total.astype(bf16)
 
@@ -338,49 +349,47 @@
         ),
     )
     sent = exchange(rows)
-    sent, *turned = lax.optimization_barrier((sent, *turned))
-    sibling = to_sibling(sent)
-    x_blocks = gather(sent, sibling, slice(None, WIDE))
-    g_blocks = gather(sent, sibling, slice(WIDE, None))
-    pre_gate, pre_up, act, scale, *out_terms = local_call(
-        forward,
-        [where, *held(*x_blocks), (HBM, w_gate), (HBM, w_up), (HBM, w_down)],
+    above, below = to_y(sent, 3), to_y(sent, 1)
+    above, below, gate_t, up_t, down_t = lax.optimization_barrier((above, below, *turned))
+    across = [to_y(below[:HALF], 1), to_y(above[HALF:], 3)]
+    near = [sent, above, below]
+    near_sibling = [to_sibling(value) for value in near]
+    gate, up, hid, mean, *late = local_call(
+        first_blocks,
+        [where, *held(*near, *near_sibling), (HBM, w_gate), (HBM, w_up), (HBM, down_t)],
         [
-            (VMEM, (ROWS, HID), f32),
-            (VMEM, (ROWS, HID), f32),
-            (VMEM, (ROWS, HID), bf16),
-            (VMEM, (ROWS, 128), f32),
-            *[(VMEM, (ROWS, FEAT), bf16)] * 8,
+            *[(VMEM, (ROWS, HID), f32)] * 3,
+            (VMEM, (ROWS, WIDE - FEAT), f32),
+            *[(VMEM, (2, FEAT, HID), bf16)] * 3,
         ],
         16,
         (10**10, 1000),
-        scratch=(
-            pltpu.VMEM((1, D, HID), bf16),
-            pltpu.VMEM((1, D, HID), bf16),
-            pltpu.VMEM((1, HID, D), bf16),
-            pltpu.SemaphoreType.DMA((3,)),
-        ),
-    )
-    out_sums = chip_sums(out_terms[:4], out_terms[4:])
-    out_parts = sent_home(out_sums)
-    d_gate, d_up, *in_terms = local_call(
-        backward,
-        [where, *held(*g_blocks, *turned, pre_gate, pre_up, act, scale)],
+        scratch=(*[pltpu.VMEM((6, FEAT, HID), bf16)] * 3, pltpu.SemaphoreType.DMA((8, 3))),
+    )
+    across, mean = lax.optimization_barrier((across, mean))
+    across_sibling = [to_sibling(value) for value in across]
+    act, d_gate, d_up, tail, *other = local_call(
+        last_blocks,
+        [where, *held(*across, *across_sibling, *late, gate, up, hid, mean, w_down, gate_t, up_t)],
         [
-            (VMEM, (ROWS, HID), bf16),
-            (VMEM, (ROWS, HID), bf16),
-            *[(VMEM, (ROWS, WIDE), bf16)] * 8,
+            *[(VMEM, (ROWS, HID), bf16)] * 3,
+            (VMEM, (ROWS, WIDE - FEAT), bf16),
+            *[(VMEM, (ROWS, BOTH), bf16)] * 4,
         ],
         4,
-        (10**10, 1000),
-    )
-    in_terms, out_parts = lax.optimization_barrier((in_terms, out_parts))
-    in_sums = chip_sums(in_terms[:4], in_terms[4:])
-    out_rows = row_sum(out_sums[0], out_parts)
-    in_rows = row_sum(in_sums[0], sent_home(in_sums))
+        (10**9, 1000),
+    )
+    theirs = [to_sibling(value) for value in other]
+    own = local_call(
+        own_terms,
+        [where, *held(act, d_gate, d_up, tail, w_down, gate_t, up_t)],
+        [(VMEM, (ROWS, BOTH), bf16)] * 4,
+        4,
+        (2 * 10**9, 1000),
+    )
     grads = local_call(
         weight_grads,
-        [where, *fetched(*x_blocks, *g_blocks[1:4], *g_blocks[5:], act, d_gate, d_up)],
+        [where, *fetched(*near, *across, *near_sibling, *across_sibling, act, d_gate, d_up)],
         [(HBM, (1, D, HID), bf16), (HBM, (1, D, HID), bf16), (HBM, (1, HID, D), bf16)],
         12,
         (2 * 3 * 2 * ROWS * D * HID, 22 * 10**6),
@@ -391,7 +400,9 @@
             pltpu.SemaphoreType.DMA((2, 3)),
         ),
     )
-    home = exchange(jnp.concatenate([out_rows, in_rows], axis=1))
+    home_sums = sent_home([joined(mine, term) for mine, term in zip(own, theirs)])
+    home_sums, *grads = lax.optimization_barrier((home_sums, *grads))
+    home = exchange(home_sums)
     moe, grad_hidden, grad_gates = local_call(
         finish,
         held(home, kept) + fetched(gain, source, ids, slots, gates),

time: 104 us -> 92.8 us (0.89)
  blocking collectives: 0 us -> 32.4 us
  waiting for transfers between devices: 36.6 us -> 13.1 us
  starting transfers between devices: 34 us -> 15.4 us
    all_to_all x0 -> x2, blocking collectives: none -> 32.4 us  [exchange(): lax.all_to_all(pieces, ('x', 'z'), 0, 0, tiled=True).reshape(ROWS, width)]
    ppermute x12 -> x8, waiting for transfers between devices: 29.4 us -> 11.7 us  [to_y(): return lax.ppermute(values, 'y', [(i, (i + step) % 4) for i in range(4)])]
    all_to_all x2 -> x0, starting transfers between devices: 12.5 us -> none  [exchange(): lax.all_to_all(pieces, ('x', 'z'), 0, 0, tiled=True).reshape(ROWS, width)]
    all_to_all x2 -> x0, waiting for transfers between devices: 5.58 us -> none  [exchange(): lax.all_to_all(pieces, ('x', 'z'), 0, 0, tiled=True).reshape(ROWS, width)]
    ppermute x12 -> x8, starting transfers between devices: 18.4 us -> 13.1 us  [to_y(): return lax.ppermute(values, 'y', [(i, (i + step) % 4) for i in range(4)])]
    ppermute x15 -> x9, starting transfers between devices: 3.1 us -> 2.32 us  [to_sibling(): return lax.ppermute(values, 'core', [(0, 1), (1, 0)])]
    pallas_call x6 -> x7, Pallas kernels: 30.1 us -> 29.5 us  [local_call(): pl.pallas_call(kernel, out_shape=out_shape, in_specs=in_specs, out_specs=...]
  transfers between devices with their start and end apart: 29 -> 17, of which waited for: 13 -> 6; matrix products, arithmetic and copies ran while one was open for 1% -> 1% of each run, Pallas kernels for 25% -> 25%
where the time goes in v3:
time: 92.8 us; the launch traced here: 92.2 us
  blocking collectives  32.4 us (35%)
  Pallas kernels  29.5 us (32%)
  starting transfers between devices  15.4 us (17%)
  waiting for transfers between devices  13.1 us (14%)
  between operations  1 us (1%)
    all_to_all x2, blocking collectives, exchange(): lax.all_to_all(pieces, ('x', 'z'), 0, 0, tiled=True).reshape(ROWS, width)  32.4 us
    pallas_call x7, Pallas kernels, local_call(): pl.pallas_call(kernel, out_shape=out_shape, in_specs=in_specs, out_specs=...  29.5 us
    ppermute x8, starting transfers between devices, to_y(): return lax.ppermute(values, 'y', [(i, (i + step) % 4) for i in range(4)])  13.1 us
    ppermute x8, waiting for transfers between devices, to_y(): return lax.ppermute(values, 'y', [(i, (i + step) % 4) for i in range(4)])  11.7 us
    ppermute x9, starting transfers between devices, to_sibling(): return lax.ppermute(values, 'core', [(0, 1), (1, 0)])  2.32 us
  transfers between devices with their start and end apart: 17, of which 6 were waited for; matrix products, arithmetic and copies ran while one was open for 1% of the time, Pallas kernels for 25%

profile of v3, /device:TPU:0, one launch (start us, length us, event | category | flops | bytes accessed | tf_op | source)
XLA Modules:
  0.0 92.2 jit_solution(13482111295822414368)
XLA Ops:
  0.6 1.6 %shard_map.145 = (bf16[128,1920]{1,0:T(8,128)(2,1)S(1)}, bf16[128,896]{1,0:T(8,128)(2,1)S(1)}) custom-call(bf16[128,896]{1,0:T(8,128)(2,1)} %hidden.1, f32[896]{0:T(1024)} %gain.3, s32[1,128]{1,0:T(1,128)} %bitcast.25, s32[8,128]{1,0:T(8,128)} %bitcast.19, s32[8,128]{1,0:T(8,128)} %bitcast.21, f32[8,128]{1,0:T(8,128)} %bitcast.23, bf16[128,896]{1,0:T(8,128)(2,1)} %cotangent.1), custom_call_target="tpu_custom_call" | custom-call | bytes 1000 | tf_op jit(solution)/shard_map/pallas_call | solution.py:49
  2.2 18.9 %all_to_all.10 = bf16[16,8,1920]{2,1,0:T(8,128)(2,1)S(1)} all-to-all(bf16[16,8,1920]{2,1,0:T(8,128)(2,1)S(1)} %bitcast.17), channel_id=1, replica_groups=mesh['y'=4,'core'=2,'x'=4,'z'=4] {'x','z'}, dimensions={0} | all-to-all | bytes 983040 | tf_op jit(solution)/shard_map/all_to_all | solution.py:320
  21.1 1.6 %collective-permute-start.1 = (bf16[128,1920]{1,0:T(8,128)(2,1)S(1)}, bf16[128,1920]{1,0:T(8,128)(2,1)S(1)}, u32[]{:S(2)}, u32[]{:S(2)}) collective-permute-start(bf16[128,1920]{1,0:T(8,128)(2,1)S(1)} %bitcast.12), channel_id=1, source_target_pairs={{0,32},{32,64},{64,96},{96,0},{1,33},{33,65},{65,97},{97,1},{2,34}... | collective-permute-start | bytes 1474568 | tf_op jit(solution)/shard_map/ppermute | solution.py:295
  22.7 1.7 %collective-permute-start = (bf16[128,1920]{1,0:T(8,128)(2,1)S(1)}, bf16[128,1920]{1,0:T(8,128)(2,1)S(1)}, u32[]{:S(2)}, u32[]{:S(2)}) collective-permute-start(bf16[128,1920]{1,0:T(8,128)(2,1)S(1)} %bitcast.13), channel_id=1, source_target_pairs={{0,96},{32,0},{64,32},{96,64},{1,97},{33,1},{65,33},{97,65},{2,98}... | collective-permute-start | bytes 1474568 | tf_op jit(solution)/shard_map/ppermute | solution.py:295
  24.4 7.5 %shard_map.146 = (bf16[256,7168]{1,0:T(8,128)(2,1)}, bf16[256,7168]{1,0:T(8,128)(2,1)}, bf16[7168,256]{1,0:T(8,128)(2,1)}) custom-call(bf16[1,7168,256]{2,1,0:T(8,128)(2,1)} %refs_6_.1, bf16[1,7168,256]{2,1,0:T(8,128)(2,1)} %refs_7_.1, bf16[1,256,7168]{2,1,0:T(8,128)(2,1)} %w_down.1), custom_call_target="tpu_custom_call" | custom-call | bytes 60000000 | tf_op jit(solution)/shard_map/pallas_call | solution.py:49
  31.9 0.1 collective-permute-start.4
  32.0 1.9 %collective-permute-done.1.refs_2_ = bf16[128,1920]{1,0:T(8,128)(2,1)S(1)} collective-permute-done((bf16[128,1920]{1,0:T(8,128)(2,1)S(1)}, bf16[128,1920]{1,0:T(8,128)(2,1)S(1)}, u32[]{:S(2)}, u32[]{:S(2)}) %collective-permute-start.1) | collective-permute-done | bytes 491552 | tf_op jit(solution)/shard_map/ppermute | solution.py:295
  34.0 0.5 collective-permute-start.5
  34.7 2.9 %collective-permute-start.3 = (bf16[64,1920]{1,0:T(8,128)(2,1)S(1)}, bf16[64,1920]{1,0:T(8,128)(2,1)S(1)}, u32[]{:S(2)}, u32[]{:S(2)}) collective-permute-start(bf16[64,1920]{1,0:T(8,128)(2,1)S(1)} %slice.13), channel_id=1, source_target_pairs={{0,96},{32,0},{64,32},{96,64},{1,97},{33,1},{65,33},{97,65},{2,98}... | collective-permute-start | bytes 737288 | tf_op jit(solution)/shard_map/ppermute | solution.py:295
  37.7 5.7 %shard_map.147 = (f32[128,256]{1,0:T(8,128)S(1)}, f32[128,256]{1,0:T(8,128)S(1)}, f32[128,256]{1,0:T(8,128)S(1)}, f32[128,128]{1,0:T(8,128)S(1)}, bf16[2,896,256...) custom-call(s32[2]{0:T(128)S(1)} %pad_add_fusion.where, ...), custom_call_target="tpu_custom_call" | custom-call | flops 10000000000 | bytes 1000 | tf_op jit(solution)/shard_map/pallas_call | solution.py:49
  43.5 2.9 %collective-permute-done.2.refs_0_.refs_3_ = bf16[64,1920]{1,0:T(8,128)(2,1)S(1)} collective-permute-done((bf16[64,1920]{1,0:T(8,128)(2,1)S(1)}, bf16[64,1920]{1,0:T(8,128)(2,1)S(1)}, u32[]{:S(2)}, u32[]{:S(2)}) %collective-permute-start.2) | collective-permute-done | bytes 245792 | tf_op jit(solution)/shard_map/ppermute | solution.py:295
  46.4 0.5 collective-permute-start.8
  46.9 1.0 %collective-permute-done.7.refs_2_.refs_8_ = bf16[64,1920]{1,0:T(8,128)(2,1)S(1)} collective-permute-done((bf16[64,1920]{1,0:T(8,128)(2,1)S(1)}, bf16[64,1920]{1,0:T(8,128)(2,1)S(1)}, u32[]{:S(2)}, u32[]{:S(2)}) %collective-permute-start.7) | collective-permute-done | bytes 245792 | tf_op jit(solution)/shard_map/ppermute | solution.py:299
  47.9 0.3 collective-permute-done.8.refs_3_.refs_9_
  48.3 2.3 %shard_map.148 = (bf16[128,256]{1,0:T(8,128)(2,1)S(1)}, bf16[128,256]{1,0:T(8,128)(2,1)S(1)}, bf16[128,256]{1,0:T(8,128)(2,1)S(1)}, bf16[128,128]{1,0:T(8,128)(2...) custom-call(s32[2]{0:T(128)S(1)} %pad_add_fusion.where, ...), custom_call_target="tpu_custom_call" | custom-call | flops 1000000000 | bytes 1000 | tf_op jit(solution)/shard_map/pallas_call | solution.py:49
  50.7 0.2 collective-permute-start.11
  50.9 0.4 collective-permute-start.10
  51.3 1.6 %shard_map.149 = (bf16[128,1920]{1,0:T(8,128)(2,1)S(1)}, bf16[128,1920]{1,0:T(8,128)(2,1)S(1)}, bf16[128,1920]{1,0:T(8,128)(2,1)S(1)}, bf16[128,1920]{1,0:T(8,128)(2,1)S(1)}) custom-call(s32[2]{0:T(128)S(1)} %pad_add_fusion.where, bf16[128,256]{1,0:T(8,128)(2,1)S(1)} %get-tuple-element.67.act.refs_10_, ...), custom_call_target="tpu_custom_call" | custom-call | flops 2000000000 | bytes 1000 | tf_op jit(solution)/shard_map/pallas_call | solution.py:49
  52.9 0.1 add_convert_fusion.4
  53.1 0.3 collective-permute-start.12
  53.4 0.2 collective-permute-start.14
  53.6 0.4 collective-permute-start.9
  53.9 3.1 %collective-permute-start.15 = (bf16[64,1920]{1,0:T(8,128)(2,1)S(1)}, bf16[64,1920]{1,0:T(8,128)(2,1)S(1)}, u32[]{:S(2)}, u32[]{:S(2)}) collective-permute-start(bf16[64,1920]{1,0:T(8,128)(2,1)S(1)} %get-tuple-element.91), channel_id=1, source_target_pairs={{0,96},{32,0},{64,32},{96,64},{1,97},{33,1},{65,33},{97,65},{2,98}... | collective-permute-start | bytes 737288 | tf_op jit(solution)/shard_map/ppermute | solution.py:295
  57.1 5.5 %collective-permute-done.12 = bf16[64,1920]{1,0:T(8,128)(2,1)S(1)} collective-permute-done((bf16[64,1920]{1,0:T(8,128)(2,1)S(1)}, bf16[64,1920]{1,0:T(8,128)(2,1)S(1)}, u32[]{:S(2)}, u32[]{:S(2)}) %collective-permute-start.12) | collective-permute-done | bytes 245792 | tf_op jit(solution)/shard_map/ppermute | solution.py:295
  62.6 0.1 add_convert_fusion.3
  62.8 0.1 add_convert_fusion.1
  63.0 3.4 %collective-permute-start.16 = (bf16[128,1920]{1,0:T(8,128)(2,1)S(1)}, bf16[128,1920]{1,0:T(8,128)(2,1)S(1)}, u32[]{:S(2)}, u32[]{:S(2)}) collective-permute-start(bf16[128,1920]{1,0:T(8,128)(2,1)S(1)} %add_convert_fusion.1), channel_id=1, source_target_pairs={{0,96},{32,0},{64,32},{96,64},{1,97},{33,1},{65,33},{97,65},{2,98}... | collective-permute-start | bytes 1474568 | tf_op jit(solution)/shard_map/ppermute | solution.py:295
  66.4 8.6 %shard_map.150 = (bf16[1,7168,256]{2,1,0:T(8,128)(2,1)}, bf16[1,7168,256]{2,1,0:T(8,128)(2,1)}, bf16[1,256,7168]{2,1,0:T(8,128)(2,1)}) custom-call(s32[2]{0:T(128)S(1)} %pad_add_fusion.where, bf16[128,1920]{1,0:T(8,128)(2,1)} %bitcast.16, bf16[128,1920]{1,0:T(8,128)(2,1)} %copy-done.9, bf16[128,1920]{1,0:T(8,128)(2,1)} %copy-done.8, ...), custom_call_target="tpu_custom_call" | custom-call | flops 2818572288 | bytes 22000000 | tf_op jit(solution)/shard_map/pallas_call | solution.py:49
  75.1 1.4 %collective-permute-done.13 = bf16[128,1920]{1,0:T(8,128)(2,1)S(1)} collective-permute-done((bf16[128,1920]{1,0:T(8,128)(2,1)S(1)}, bf16[128,1920]{1,0:T(8,128)(2,1)S(1)}, u32[]{:S(2)}, u32[]{:S(2)}) %collective-permute-start.13) | collective-permute-done | bytes 491552 | tf_op jit(solution)/shard_map/ppermute | solution.py:295
  76.4 0.3 add_convert_fusion
  76.7 13.5 %all_to_all.11 = bf16[16,8,1920]{2,1,0:T(8,128)(2,1)S(1)} all-to-all(bf16[16,8,1920]{2,1,0:T(8,128)(2,1)S(1)} %bitcast.18), channel_id=1, replica_groups=mesh['y'=4,'core'=2,'x'=4,'z'=4] {'x','z'}, dimensions={0} | all-to-all | bytes 983040 | tf_op jit(solution)/shard_map/all_to_all | solution.py:320
  90.2 2.1 %shard_map.151 = (bf16[128,896]{1,0:T(8,128)(2,1)}, bf16[128,896]{1,0:T(8,128)(2,1)}, f32[8,128]{1,0:T(8,128)}) custom-call(bf16[128,1920]{1,0:T(8,128)(2,1)S(1)} %bitcast.11, bf16[128,896]{1,0:T(8,128)(2,1)S(1)} %get-tuple-element.83.hidden, f32[896]{0:T(1024)} %gain.3, s32[1,128]{1,0:T(1,128)} %bitcast.26, s32[8,128]{1,0:T(8,128)} %bitcast.20, ...), custom_call_target="tpu_custom_call" | custom-call | bytes 1000 | tf_op jit(solution)/shard_map/pallas_call | solution.py:49
  (51 shorter events, 0.4 us)
Async XLA Ops:
  21.1 16.5 %copy-start.3 = (bf16[16,8,1920]{2,1,0:T(8,128)(2,1)}, bf16[16,8,1920]{2,1,0:T(8,128)(2,1)S(1)}, u32[]{:S(2)}) copy-start(bf16[16,8,1920]{2,1,0:T(8,128)(2,1)S(1)} %all_to_all.10) | copy-start | bytes 1474564
  21.1 12.8 %collective-permute-start.1 = (bf16[128,1920]{1,0:T(8,128)(2,1)S(1)}, bf16[128,1920]{1,0:T(8,128)(2,1)S(1)}, u32[]{:S(2)}, u32[]{:S(2)}) collective-permute-start(bf16[128,1920]{1,0:T(8,128)(2,1)S(1)} %bitcast.12), channel_id=1, source_target_pairs={{0,32},{32,64},{64,96},{96,0},{1,33},{33,65},{65,97},{97,1},{2,34}... | collective-permute-start | bytes 1474568 | tf_op jit(solution)/shard_map/ppermute | solution.py:295
  22.7 11.2 %collective-permute-start = (bf16[128,1920]{1,0:T(8,128)(2,1)S(1)}, bf16[128,1920]{1,0:T(8,128)(2,1)S(1)}, u32[]{:S(2)}, u32[]{:S(2)}) collective-permute-start(bf16[128,1920]{1,0:T(8,128)(2,1)S(1)} %bitcast.13), channel_id=1, source_target_pairs={{0,96},{32,0},{64,32},{96,64},{1,97},{33,1},{65,33},{97,65},{2,98}... | collective-permute-start | bytes 1474568 | tf_op jit(solution)/shard_map/ppermute | solution.py:295
  31.9 5.7 %collective-permute-start.4 = (bf16[128,1920]{1,0:T(8,128)(2,1)S(1)}, bf16[128,1920]{1,0:T(8,128)(2,1)S(1)}, u32[]{:S(2)}, u32[]{:S(2)}) collective-permute-start(bf16[128,1920]{1,0:T(8,128)(2,1)S(1)} %bitcast.14), channel_id=1, source_target_pairs={{0,16},{16,0},{1,17},{17,1},{2,18},{18,2},{3,19},{19,3},{4,20},{20... | collective-permute-start | bytes 1474568 | tf_op jit(solution)/shard_map/ppermute | solution.py:299
  33.9 9.5 %copy-start.8 = (bf16[128,1920]{1,0:T(8,128)(2,1)}, bf16[128,1920]{1,0:T(8,128)(2,1)S(1)}, u32[]{:S(2)}) copy-start(bf16[128,1920]{1,0:T(8,128)(2,1)S(1)} %collective-permute-done.1.refs_2_) | copy-start | bytes 1474564
  34.0 9.5 %copy-start.9 = (bf16[128,1920]{1,0:T(8,128)(2,1)}, bf16[128,1920]{1,0:T(8,128)(2,1)S(1)}, u32[]{:S(2)}) copy-start(bf16[128,1920]{1,0:T(8,128)(2,1)S(1)} %collective-permute-done.refs_1_) | copy-start | bytes 1474564
  34.0 3.7 %collective-permute-start.6 = (bf16[128,1920]{1,0:T(8,128)(2,1)S(1)}, bf16[128,1920]{1,0:T(8,128)(2,1)S(1)}, u32[]{:S(2)}, u32[]{:S(2)}) collective-permute-start(bf16[128,1920]{1,0:T(8,128)(2,1)S(1)} %collective-permute-done.1.refs_2_), channel_id=1, source_target_pairs={{0,16},{16,0},{1,17},{17,1},{2,18},{18,2},{3,19},{19,3},{4,20},{20... | collective-permute-start | bytes 1474568 | tf_op jit(solution)/shard_map/ppermute | solution.py:299
  34.0 3.6 %collective-permute-start.5 = (bf16[128,1920]{1,0:T(8,128)(2,1)S(1)}, bf16[128,1920]{1,0:T(8,128)(2,1)S(1)}, u32[]{:S(2)}, u32[]{:S(2)}) collective-permute-start(bf16[128,1920]{1,0:T(8,128)(2,1)S(1)} %collective-permute-done.refs_1_), channel_id=1, source_target_pairs={{0,16},{16,0},{1,17},{17,1},{2,18},{18,2},{3,19},{19,3},{4,20},{20... | collective-permute-start | bytes 1474568 | tf_op jit(solution)/shard_map/ppermute | solution.py:299
  34.6 13.6 %copy-start = (bf16[1,256,7168]{2,1,0:T(8,128)(2,1)S(1)}, bf16[1,256,7168]{2,1,0:T(8,128)(2,1)}, u32[]{:S(2)}) copy-start(bf16[1,256,7168]{2,1,0:T(8,128)(2,1)} %w_down.1) | copy-start | bytes 11010052
  34.6 13.6 %copy-start.1 = (bf16[256,7168]{1,0:T(8,128)(2,1)S(1)}, bf16[256,7168]{1,0:T(8,128)(2,1)}, u32[]{:S(2)}) copy-start(bf16[256,7168]{1,0:T(8,128)(2,1)} %get-tuple-element.65.refs_12_.gate_t) | copy-start | bytes 11010052
  34.7 13.6 %copy-start.2 = (bf16[256,7168]{1,0:T(8,128)(2,1)S(1)}, bf16[256,7168]{1,0:T(8,128)(2,1)}, u32[]{:S(2)}) copy-start(bf16[256,7168]{1,0:T(8,128)(2,1)} %get-tuple-element.66.refs_13_.up_t) | copy-start | bytes 11010052
  34.7 8.8 %collective-permute-start.3 = (bf16[64,1920]{1,0:T(8,128)(2,1)S(1)}, bf16[64,1920]{1,0:T(8,128)(2,1)S(1)}, u32[]{:S(2)}, u32[]{:S(2)}) collective-permute-start(bf16[64,1920]{1,0:T(8,128)(2,1)S(1)} %slice.13), channel_id=1, source_target_pairs={{0,96},{32,0},{64,32},{96,64},{1,97},{33,1},{65,33},{97,65},{2,98}... | collective-permute-start | bytes 737288 | tf_op jit(solution)/shard_map/ppermute | solution.py:295
  37.6 8.8 %collective-permute-start.2 = (bf16[64,1920]{1,0:T(8,128)(2,1)S(1)}, bf16[64,1920]{1,0:T(8,128)(2,1)S(1)}, u32[]{:S(2)}, u32[]{:S(2)}) collective-permute-start(bf16[64,1920]{1,0:T(8,128)(2,1)S(1)} %slice.12), channel_id=1, source_target_pairs={{0,32},{32,64},{64,96},{96,0},{1,33},{33,65},{65,97},{97,1},{2,34}... | collective-permute-start | bytes 737288 | tf_op jit(solution)/shard_map/ppermute | solution.py:295
  37.6 5.8 %copy-start.13 = (bf16[128,1920]{1,0:T(8,128)(2,1)}, bf16[128,1920]{1,0:T(8,128)(2,1)S(1)}, u32[]{:S(2)}) copy-start(bf16[128,1920]{1,0:T(8,128)(2,1)S(1)} %collective-permute-done.4.refs_3_.refs_5_) | copy-start | bytes 1474564
  37.6 5.8 %copy-start.14 = (bf16[128,1920]{1,0:T(8,128)(2,1)}, bf16[128,1920]{1,0:T(8,128)(2,1)S(1)}, u32[]{:S(2)}) copy-start(bf16[128,1920]{1,0:T(8,128)(2,1)S(1)} %collective-permute-done.6.refs_5_.refs_7_) | copy-start | bytes 1474564
  37.7 5.8 %copy-start.15 = (bf16[128,1920]{1,0:T(8,128)(2,1)}, bf16[128,1920]{1,0:T(8,128)(2,1)S(1)}, u32[]{:S(2)}) copy-start(bf16[128,1920]{1,0:T(8,128)(2,1)S(1)} %collective-permute-done.5.refs_4_.refs_6_) | copy-start | bytes 1474564
  43.5 7.1 %copy-start.4 = (bf16[64,1920]{1,0:T(8,128)(2,1)}, bf16[64,1920]{1,0:T(8,128)(2,1)S(1)}, u32[]{:S(2)}) copy-start(bf16[64,1920]{1,0:T(8,128)(2,1)S(1)} %collective-permute-done.3.refs_1_.refs_4_) | copy-start | bytes 737284
  46.4 4.2 %copy-start.5 = (bf16[64,1920]{1,0:T(8,128)(2,1)}, bf16[64,1920]{1,0:T(8,128)(2,1)S(1)}, u32[]{:S(2)}) copy-start(bf16[64,1920]{1,0:T(8,128)(2,1)S(1)} %collective-permute-done.2.refs_0_.refs_3_) | copy-start | bytes 737284
  46.4 1.5 %collective-permute-start.7 = (bf16[64,1920]{1,0:T(8,128)(2,1)S(1)}, bf16[64,1920]{1,0:T(8,128)(2,1)S(1)}, u32[]{:S(2)}, u32[]{:S(2)}) collective-permute-start(bf16[64,1920]{1,0:T(8,128)(2,1)S(1)} %collective-permute-done.2.refs_0_.refs_3_), channel_id=1, source_target_pairs={{0,16},{16,0},{1,17},{17,1},{2,18},{18,2},{3,19},{19,3},{4,20},{20... | collective-permute-start | bytes 737288 | tf_op jit(solution)/shard_map/ppermute | solution.py:299
  46.4 1.9 %collective-permute-start.8 = (bf16[64,1920]{1,0:T(8,128)(2,1)S(1)}, bf16[64,1920]{1,0:T(8,128)(2,1)S(1)}, u32[]{:S(2)}, u32[]{:S(2)}) collective-permute-start(bf16[64,1920]{1,0:T(8,128)(2,1)S(1)} %collective-permute-done.3.refs_1_.refs_4_), channel_id=1, source_target_pairs={{0,16},{16,0},{1,17},{17,1},{2,18},{18,2},{3,19},{19,3},{4,20},{20... | collective-permute-start | bytes 737288 | tf_op jit(solution)/shard_map/ppermute | solution.py:299
  47.9 2.7 %copy-start.6 = (bf16[64,1920]{1,0:T(8,128)(2,1)}, bf16[64,1920]{1,0:T(8,128)(2,1)S(1)}, u32[]{:S(2)}) copy-start(bf16[64,1920]{1,0:T(8,128)(2,1)S(1)} %collective-permute-done.7.refs_2_.refs_8_) | copy-start | bytes 737284
  48.3 2.4 %copy-start.7 = (bf16[64,1920]{1,0:T(8,128)(2,1)}, bf16[64,1920]{1,0:T(8,128)(2,1)S(1)}, u32[]{:S(2)}) copy-start(bf16[64,1920]{1,0:T(8,128)(2,1)S(1)} %collective-permute-done.8.refs_3_.refs_9_) | copy-start | bytes 737284
  50.6 2.2 %copy-start.10 = (bf16[128,256]{1,0:T(8,128)(2,1)}, bf16[128,256]{1,0:T(8,128)(2,1)S(1)}, u32[]{:S(2)}) copy-start(bf16[128,256]{1,0:T(8,128)(2,1)S(1)} %get-tuple-element.67.act.refs_10_) | copy-start | bytes 196612
  50.7 2.2 %copy-start.11 = (bf16[128,256]{1,0:T(8,128)(2,1)}, bf16[128,256]{1,0:T(8,128)(2,1)S(1)}, u32[]{:S(2)}) copy-start(bf16[128,256]{1,0:T(8,128)(2,1)S(1)} %get-tuple-element.68.grad_gate.refs_11_) | copy-start | bytes 196612
  50.7 2.2 %collective-permute-start.11 = (bf16[128,1920]{1,0:T(8,128)(2,1)S(1)}, bf16[128,1920]{1,0:T(8,128)(2,1)S(1)}, u32[]{:S(2)}, u32[]{:S(2)}) collective-permute-start(bf16[128,1920]{1,0:T(8,128)(2,1)S(1)} %get-tuple-element.76), channel_id=1, source_target_pairs={{0,16},{16,0},{1,17},{17,1},{2,18},{18,2},{3,19},{19,3},{4,20},{20... | collective-permute-start | bytes 1474568 | tf_op jit(solution)/shard_map/ppermute | solution.py:299
  50.9 6.2 %collective-permute-start.10 = (bf16[128,1920]{1,0:T(8,128)(2,1)S(1)}, bf16[128,1920]{1,0:T(8,128)(2,1)S(1)}, u32[]{:S(2)}, u32[]{:S(2)}) collective-permute-start(bf16[128,1920]{1,0:T(8,128)(2,1)S(1)} %get-tuple-element.74), channel_id=1, source_target_pairs={{0,16},{16,0},{1,17},{17,1},{2,18},{18,2},{3,19},{19,3},{4,20},{20... | collective-permute-start | bytes 1474568 | tf_op jit(solution)/shard_map/ppermute | solution.py:299
  53.1 9.5 %collective-permute-start.12 = (bf16[64,1920]{1,0:T(8,128)(2,1)S(1)}, bf16[64,1920]{1,0:T(8,128)(2,1)S(1)}, u32[]{:S(2)}, u32[]{:S(2)}) collective-permute-start(bf16[64,1920]{1,0:T(8,128)(2,1)S(1)} %get-tuple-element.90), channel_id=1, source_target_pairs={{0,32},{32,64},{64,96},{96,0},{1,33},{33,65},{65,97},{97,1},{2,34}... | collective-permute-start | bytes 737288 | tf_op jit(solution)/shard_map/ppermute | solution.py:295
  53.4 9.4 %collective-permute-start.14 = (bf16[128,1920]{1,0:T(8,128)(2,1)S(1)}, bf16[128,1920]{1,0:T(8,128)(2,1)S(1)}, u32[]{:S(2)}, u32[]{:S(2)}) collective-permute-start(bf16[128,1920]{1,0:T(8,128)(2,1)S(1)} %get-tuple-element.78), channel_id=1, source_target_pairs={{0,16},{16,0},{1,17},{17,1},{2,18},{18,2},{3,19},{19,3},{4,20},{20... | collective-permute-start | bytes 1474568 | tf_op jit(solution)/shard_map/ppermute | solution.py:299
  53.6 21.5 %collective-permute-start.9 = (bf16[128,1920]{1,0:T(8,128)(2,1)S(1)}, bf16[128,1920]{1,0:T(8,128)(2,1)S(1)}, u32[]{:S(2)}, u32[]{:S(2)}) collective-permute-start(bf16[128,1920]{1,0:T(8,128)(2,1)S(1)} %get-tuple-element.72), channel_id=1, source_target_pairs={{0,16},{16,0},{1,17},{17,1},{2,18},{18,2},{3,19},{19,3},{4,20},{20... | collective-permute-start | bytes 1474568 | tf_op jit(solution)/shard_map/ppermute | solution.py:299
  53.9 8.9 %collective-permute-start.15 = (bf16[64,1920]{1,0:T(8,128)(2,1)S(1)}, bf16[64,1920]{1,0:T(8,128)(2,1)S(1)}, u32[]{:S(2)}, u32[]{:S(2)}) collective-permute-start(bf16[64,1920]{1,0:T(8,128)(2,1)S(1)} %get-tuple-element.91), channel_id=1, source_target_pairs={{0,96},{32,0},{64,32},{96,64},{1,97},{33,1},{65,33},{97,65},{2,98}... | collective-permute-start | bytes 737288 | tf_op jit(solution)/shard_map/ppermute | solution.py:295
  62.7 13.7 %collective-permute-start.13 = (bf16[128,1920]{1,0:T(8,128)(2,1)S(1)}, bf16[128,1920]{1,0:T(8,128)(2,1)S(1)}, u32[]{:S(2)}, u32[]{:S(2)}) collective-permute-start(bf16[128,1920]{1,0:T(8,128)(2,1)S(1)} %add_convert_fusion.3), channel_id=1, source_target_pairs={{0,32},{32,64},{64,96},{96,0},{1,33},{33,65},{65,97},{97,1},{2,34}... | collective-permute-start | bytes 1474568 | tf_op jit(solution)/shard_map/ppermute | solution.py:295
  63.0 13.5 %collective-permute-start.16 = (bf16[128,1920]{1,0:T(8,128)(2,1)S(1)}, bf16[128,1920]{1,0:T(8,128)(2,1)S(1)}, u32[]{:S(2)}, u32[]{:S(2)}) collective-permute-start(bf16[128,1920]{1,0:T(8,128)(2,1)S(1)} %add_convert_fusion.1), channel_id=1, source_target_pairs={{0,96},{32,0},{64,32},{96,64},{1,97},{33,1},{65,33},{97,65},{2,98}... | collective-permute-start | bytes 1474568 | tf_op jit(solution)/shard_map/ppermute | solution.py:295
  (1 other events, 2.2 us)

commit v4 on v3

v4 whole, which is shorter than its diff:
```python
import jax
import jax.numpy as jnp
from jax import lax
from jax.experimental import pallas as pl
from jax.experimental.pallas import tpu as pltpu
from jax.sharding import Mesh, PartitionSpec as P

D = 7168
CAP = 8
ROWS = 128
FEAT = 896
WIDE = 1024
BOTH = WIDE + FEAT
HID = 256
EPSILON = 1e-06
PLACES = ((0, 1, 3, 2), (0, 3, 1, 2))

f32 = jnp.float32
bf16 = jnp.bfloat16
SMEM, VMEM, COPY, HBM = "smem", "vmem", "copy", "hbm"


def nn(a, b):
    return lax.dot_general(a, b, (((1,), (0,)), ((), ())), preferred_element_type=f32)


def nt(a, b):
    return lax.dot_general(a, b, (((1,), (1,)), ((), ())), preferred_element_type=f32)


def tn(a, b):
    return lax.dot_general(a, b, (((0,), (0,)), ((), ())), preferred_element_type=f32)


def local_call(kernel, inputs, outputs, mib, cost, scratch=()):
    in_specs, args = [], []
    for kind, value in inputs:
        space = {SMEM: pltpu.SMEM, HBM: pl.ANY}.get(kind, pltpu.VMEM)
        in_specs.append(pl.BlockSpec(memory_space=space))
        if kind != SMEM:
            value = pltpu.with_memory_space_constraint(value, pltpu.VMEM if kind == VMEM else pltpu.HBM)
        args.append(value)
    out_shape, out_specs = [], []
    for kind, shape, dtype in outputs:
        space = {VMEM: pltpu.VMEM, HBM: pltpu.HBM}.get(kind, jax.ShapeDtypeStruct)
        out_shape.append(space(shape, dtype))
        out_specs.append(pl.BlockSpec(memory_space=pl.ANY if kind == HBM else pltpu.VMEM))
    return pl.pallas_call(
        kernel,
        out_shape=out_shape,
        in_specs=in_specs,
        out_specs=out_specs,
        scratch_shapes=list(scratch),
        compiler_params=pltpu.CompilerParams(vmem_limit_bytes=mib * 2**20),
        cost_estimate=pl.CostEstimate(flops=cost[0], bytes_accessed=cost[1], transcendentals=0),
    )(*args)


def held(*values):
    return [(VMEM, value) for value in values]


def fetched(*values):
    return [(COPY, value) for value in values]


def split_two(value):
    high = value.astype(bf16)
    low = (value - high.astype(f32)).astype(bf16)
    return high, low


def slot_matches(ids, slots):
    live = (ids < 16) & (slots >= 0) & (slots < CAP)
    target = jnp.where(live, ids * CAP + slots, ROWS)
    slot = lax.broadcasted_iota(jnp.int32, (ROWS, ROWS), 0)
    return live, [slot == target[k : k + 1, :] for k in range(8)]


def pick_rows(matches, parent):
    pick = matches[0]
    for match in matches[1:]:
        pick = pick | match
    pick = jnp.where(pick, 1.0, 0.0).astype(bf16)
    row = lax.broadcasted_iota(jnp.int32, (ROWS, ROWS), 0)
    from_parent = jnp.where(row == parent, 1.0, 0.0).astype(bf16)
    return pick, nt(pick, from_parent).astype(bf16)


def mix_of(matches, gates):
    mix = jnp.zeros((ROWS, ROWS), f32)
    for k, match in enumerate(matches):
        mix = mix + jnp.where(match, gates[k : k + 1, :], 0.0)
    return mix


def prepare(hidden, gain, source, ids, slots, gates, cotangent, rows, kept):
    _, matches = slot_matches(ids[...], slots[...])
    pick, select = pick_rows(matches, source[...] & (ROWS - 1))
    gate = jnp.sum(mix_of(matches, gates[...]), axis=1, keepdims=True)
    beam = nn(select, hidden[...])
    rows[:, :FEAT] = (beam * gain[...][None, :]).astype(bf16)
    square = jnp.sum(beam * beam, axis=1, keepdims=True) * (1.0 / D)
    high, low = split_two(square)
    lane = lax.broadcasted_iota(jnp.int32, (ROWS, WIDE - FEAT), 1)
    tail = jnp.where(lane == 0, high.astype(f32), jnp.where(lane == 1, low.astype(f32), 0.0))
    rows[:, FEAT:WIDE] = tail.astype(bf16)
    rows[:, WIDE:] = (nn(pick, cotangent[...]) * gate).astype(bf16)
    kept[...] = hidden[...]


def turn_weights(gate, up, gate_t, up_t, wide, wide_t, sems):
    loads = [pltpu.make_async_copy(source, wide.at[i], sems.at[i]) for i, source in enumerate((gate, up))]
    stores = [pltpu.make_async_copy(wide_t.at[i], target, sems.at[2 + i]) for i, target in enumerate((gate_t, up_t))]
    for load in loads:
        load.start()
    for i in range(2):
        loads[i].wait()
        for head in range(8):
            part = slice(head * FEAT, (head + 1) * FEAT)
            wide_t[i, :, part] = wide[i, 0, part, :].T
        stores[i].start()
    for store in stores:
        store.wait()


def heads_here():
    y, core = lax.axis_index("y"), lax.axis_index("core")
    heads = []
    for side in (core, 1 - core):
        heads += [(y ^ jnp.where(side == 0, PLACES[0][i], PLACES[1][i])) * 2 + side for i in range(4)]
    return jnp.stack(heads).astype(jnp.int32)


def head_at(heads, place, side):
    return heads[4 * side + place]


def row_part(head):
    return pl.ds(pl.multiple_of(head * FEAT, FEAT), FEAT)


def column_part(head):
    return pl.ds(pl.multiple_of(head * FEAT, 128), FEAT)


def weight_copies(where, side, place, weights, targets, sems):
    head = head_at(where, place, side)
    w_gate, w_up, w_down = weights
    sources = (w_gate.at[0, row_part(head), :], w_up.at[0, row_part(head), :], w_down.at[0, :, column_part(head)])
    copies = [pltpu.make_async_copy(*pair, sems.at[j]) for j, pair in enumerate(zip(sources, targets))]
    for copy in copies:
        copy.start()
    return copies


def add_blocks(copies, blocks, parts, totals, squares):
    gate, up, hid = totals
    for n, block in enumerate(blocks):
        squares = squares + block[:, FEAT:WIDE].astype(f32)
        for copy in copies[n]:
            copy.wait()
        gate = gate + nn(block[:, :FEAT], parts[0][n])
        up = up + nn(block[:, :FEAT], parts[1][n])
        hid = hid + nt(block[:, WIDE:], parts[2][n])
    return (gate, up, hid), squares


def own_blocks(where, own, sibling, w_gate, w_up, w_down, *refs):
    gate, up, hid, mean, late_gate, late_up, late_down, *parts, late, sems = refs
    weights = (w_gate, w_up, w_down)
    copies = [weight_copies(where, side, 0, weights, [p.at[side] for p in parts], sems.at[side]) for side in range(2)]
    last = [
        weight_copies(where, side, 3, weights, (late_gate.at[side], late_up.at[side], late.at[side]), sems.at[2 + side])
        for side in range(2)
    ]
    zero = jnp.zeros((ROWS, HID), f32)
    squares = jnp.zeros((ROWS, WIDE - FEAT), f32)
    totals, squares = add_blocks(copies, (own, sibling), parts, (zero, zero, zero), squares)
    for side in range(2):
        for copy in last[side]:
            copy.wait()
        late_down[side] = late[side].T
    gate[...], up[...], hid[...] = totals
    mean[...] = squares


def near_blocks(where, *refs):
    blocks, weights, sums, results, (*parts, sems) = refs[:4], refs[4:7], refs[7:11], refs[11:15], refs[15:]
    places = ((0, 1), (0, 2), (1, 1), (1, 2))
    copies = [
        weight_copies(where, side, place, weights, [p.at[n] for p in parts], sems.at[n])
        for n, (side, place) in enumerate(places)
    ]
    totals, squares = add_blocks(copies, blocks, parts, [ref[...] for ref in sums[:3]], sums[3][...])
    results[0][...], results[1][...], results[2][...] = totals
    results[3][...] = squares


def expert_terms(where, act, d_gate, d_up, w_down, gate_t, up_t, side, results, tail):
    for i in (3, 1, 2, 0):
        columns = column_part(head_at(where, i, side))
        results[i][:, :FEAT] = nn(act, w_down[0, :, columns]).astype(bf16)
        term = nn(d_gate, gate_t[:, columns]) + nn(d_up, up_t[:, columns])
        results[i][:, FEAT : FEAT + FEAT] = term.astype(bf16)
        results[i][:, FEAT + FEAT :] = tail


def last_blocks(where, *refs):
    blocks, (late_gate, late_up, late_down) = refs[:2], refs[2:5]
    first_gate, first_up, first_hid, mean, w_down, gate_t, up_t = refs[5:12]
    act, grad_gate, grad_up, tail_out, *other = refs[12:]
    gate, up, hid = first_gate[...], first_up[...], first_hid[...]
    squares = mean[...]
    for side, block in enumerate(blocks):
        squares = squares + block[:, FEAT:WIDE].astype(f32)
        gate = gate + nn(block[:, :FEAT], late_gate[side])
        up = up + nn(block[:, :FEAT], late_up[side])
        hid = hid + nn(block[:, WIDE:], late_down[side])
    inverse = lax.rsqrt(jnp.sum(squares, axis=1, keepdims=True) + EPSILON)
    gate = gate * inverse
    up = up * inverse
    sigmoid = jax.nn.sigmoid(gate)
    hidden_act = (gate * sigmoid * up).astype(bf16)
    score = jnp.sum(hidden_act.astype(f32) * hid, axis=1, keepdims=True)
    scaled = hid * inverse
    d_gate = (scaled * up * sigmoid * (1.0 + gate * (1.0 - sigmoid))).astype(bf16)
    d_up = (scaled * gate * sigmoid).astype(bf16)
    act[...] = hidden_act
    grad_gate[...] = d_gate
    grad_up[...] = d_up
    dot = jnp.sum(d_gate.astype(f32) * gate + d_up.astype(f32) * up, axis=1, keepdims=True)
    dot = dot * inverse * (1.0 / D)
    lane = lax.broadcasted_iota(jnp.int32, (ROWS, WIDE - FEAT), 1)
    me = 2 * head_at(where, 0, 0)
    tail = jnp.zeros((ROWS, WIDE - FEAT), f32)
    for base, value in ((0, score), (64, dot)):
        high, low = split_two(value)
        tail = jnp.where(lane == base + me, high.astype(f32), tail)
        tail = jnp.where(lane == base + me + 1, low.astype(f32), tail)
    tail = tail.astype(bf16)
    tail_out[...] = tail
    expert_terms(where, hidden_act, d_gate, d_up, w_down, gate_t, up_t, 1, other, tail)


def own_terms(where, act, grad_gate, grad_up, tail, w_down, gate_t, up_t, *own):
    expert_terms(where, act[...], grad_gate[...], grad_up[...], w_down, gate_t, up_t, 0, own, tail[...])


def weight_grads(where, *refs):
    blocks, (act, grad_gate, grad_up, out_gate, out_up, out_down) = refs[:8], refs[8:14]
    held_rows, buf_gate, buf_up, buf_down, load_sems, store_sems = refs[14:]
    loads = [pltpu.make_async_copy(block, held_rows.at[n], load_sems.at[n]) for n, block in enumerate(blocks)]
    for load in loads:
        load.start()
    act_t = act[...].T
    stores = []
    for n in range(8):
        loads[n].wait()
        head = head_at(where, n % 4, n // 4)
        beam_t = held_rows[n, :, :FEAT].T
        for j, (left, right, buf, target) in enumerate(
            (
                (act_t, held_rows[n, :, WIDE:], buf_down, out_down.at[0, :, column_part(head)]),
                (beam_t, grad_gate[...], buf_gate, out_gate.at[0, row_part(head), :]),
                (beam_t, grad_up[...], buf_up, out_up.at[0, row_part(head), :]),
            )
        ):
            buf[n] = nn(left, right).astype(bf16)
            stores.append(pltpu.make_async_copy(buf.at[n], target, store_sems.at[n, j]))
            stores[-1].start()
    for store in stores:
        store.wait()


def route_tables(ids, slots, gates, source, gain, select, mix, targets, kept_gates, kept_gain):
    live, matches = slot_matches(ids[...], slots[...])
    select[...] = pick_rows(matches, source[...] & (ROWS - 1))[1]
    rest = mix_of(matches, gates[...])
    for i in range(3):
        mix[i] = rest.astype(bf16)
        rest = rest - mix[i].astype(f32)
    targets[...] = jnp.where(live, ids[...] * CAP + slots[...], ROWS)
    kept_gates[...] = gates[...]
    kept_gain[...] = gain[...][None, :]


def finish(home, hidden, select, mix, targets, gates, gain, moe, grad_hidden, grad_gates):
    rows = home[:, :FEAT]
    moe[...] = (tn(mix[0], rows) + (tn(mix[1], rows) + tn(mix[2], rows))).astype(bf16)
    tail = home[:, FEAT + FEAT :].astype(f32)
    lane = lax.broadcasted_iota(jnp.int32, tail.shape, 1)
    score = jnp.sum(jnp.where(lane < 64, tail, 0.0), axis=1, keepdims=True)
    dot = jnp.sum(jnp.where(lane < 64, 0.0, tail), axis=1, keepdims=True)
    slot = lax.broadcasted_iota(jnp.int32, (ROWS, ROWS), 0)
    found = [
        jnp.sum(jnp.where(slot == targets[k : k + 1, :], score, 0.0), axis=0, keepdims=True) for k in range(8)
    ]
    found = jnp.concatenate(found, axis=0)
    grad_gates[...] = jnp.where(targets[...] < ROWS, found / gates[...], 0.0)
    picks = select[...]
    back = tn(picks, home[:, FEAT : FEAT + FEAT]) * gain[...]
    dots = jnp.where(picks.astype(f32) > 0, dot, 0.0)
    per_parent = jnp.sum(dots.T, axis=1, keepdims=True)
    grad_hidden[...] = (back - hidden[...].astype(f32) * per_parent).astype(bf16)


def to_place(values, place):
    pairs = [(2 * y + core, 2 * (y ^ PLACES[core][place]) + core) for y in range(4) for core in range(2)]
    return lax.ppermute(values, ("y", "core"), pairs)


def to_sibling(values):
    return lax.ppermute(values, "core", [(0, 1), (1, 0)])


def sent_home(sums, beside):
    mine, first, second, across = sums
    passing, beside = lax.optimization_barrier((to_place(across, 2), beside))
    first = joined(first, passing)
    return joined(mine, to_place(first, 1), to_place(second, 2)), beside


def joined(*parts):
    total = parts[0].astype(f32)
    for part in parts[1:]:
        total = total + part.astype(f32)
    return total.astype(bf16)


def exchange(rows):
    width = rows.shape[1]
    pieces = rows.reshape(16, CAP, width)
    return lax.all_to_all(pieces, ("x", "z"), 0, 0, tiled=True).reshape(ROWS, width)


def on_device(
    hidden, norm_gain, beam_src, route_ids, route_slots, route_gates, w_gate, w_up, w_down, out_grad
):
    where = (SMEM, heads_here())
    gain = norm_gain
    source = beam_src.reshape(1, ROWS)
    ids, slots, gates = route_ids.T, route_slots.T, route_gates.T
    rows, kept = local_call(
        prepare,
        fetched(hidden, gain, source, ids, slots, gates, out_grad),
        [(VMEM, (ROWS, WIDE + FEAT), bf16), (VMEM, (ROWS, FEAT), bf16)],
        8,
        (0, 1000),
    )
    turned = local_call(
        turn_weights,
        [(HBM, w_gate), (HBM, w_up)],
        [(HBM, (HID, D), bf16), (HBM, (HID, D), bf16)],
        20,
        (0, 60 * 10**6),
        scratch=(
            pltpu.VMEM((2, 1, D, HID), bf16),
            pltpu.VMEM((2, HID, D), bf16),
            pltpu.SemaphoreType.DMA((4,)),
        ),
    )
    sent = exchange(rows)
    weights = [(HBM, w_gate), (HBM, w_up), (HBM, w_down)]
    sums = [*[(VMEM, (ROWS, HID), f32)] * 3, (VMEM, (ROWS, WIDE - FEAT), f32)]
    sibling = to_sibling(sent)
    *early, late_gate, late_up, late_down = local_call(
        own_blocks,
        [where, *held(sent, sibling), *weights],
        [*sums, *[(VMEM, (2, FEAT, HID), bf16)] * 3],
        8,
        (0, 1000),
        scratch=(
            pltpu.VMEM((2, FEAT, HID), bf16),
            pltpu.VMEM((2, FEAT, HID), bf16),
            pltpu.VMEM((2, HID, FEAT), bf16),
            pltpu.VMEM((2, HID, FEAT), bf16),
            pltpu.SemaphoreType.DMA((4, 3)),
        ),
    )
    first, second = to_place(sent, 1), to_place(sent, 2)
    first, second, gate_t, up_t, *early = lax.optimization_barrier((first, second, *turned, *early))
    across = to_place(first, 2)
    near = [sent, first, second]
    near_sibling = [sibling, to_sibling(first), to_sibling(second)]
    gate, up, hid, mean = local_call(
        near_blocks,
        [where, *held(*near[1:], *near_sibling[1:]), *weights, *held(*early)],
        sums,
        12,
        (10**10, 1000),
        scratch=(
            pltpu.VMEM((4, FEAT, HID), bf16),
            pltpu.VMEM((4, FEAT, HID), bf16),
            pltpu.VMEM((4, HID, FEAT), bf16),
            pltpu.SemaphoreType.DMA((4, 3)),
        ),
    )
    across, mean = lax.optimization_barrier((across, mean))
    across_sibling = to_sibling(across)
    act, d_gate, d_up, tail, *other = local_call(
        last_blocks,
        [where, *held(across, across_sibling, late_gate, late_up, late_down, gate, up, hid, mean, w_down, gate_t, up_t)],
        [
            *[(VMEM, (ROWS, HID), bf16)] * 3,
            (VMEM, (ROWS, WIDE - FEAT), bf16),
            *[(VMEM, (ROWS, BOTH), bf16)] * 4,
        ],
        4,
        (10**9, 1000),
    )
    theirs = [to_sibling(value) for value in other]
    own = local_call(
        own_terms,
        [where, *held(act, d_gate, d_up, tail, w_down, gate_t, up_t)],
        [(VMEM, (ROWS, BOTH), bf16)] * 4,
        4,
        (2 * 10**9, 1000),
    )
    blocks = [(HBM, block) for block in (*near, across, *near_sibling, across_sibling)]
    home_sums = [joined(mine, term) for mine, term in zip(own, theirs)]
    home_sums[3], late_gates = lax.optimization_barrier((home_sums[3], gates))
    tables = local_call(
        route_tables,
        fetched(ids, slots, late_gates, source, gain),
        [
            (VMEM, (ROWS, ROWS), bf16),
            (VMEM, (3, ROWS, ROWS), bf16),
            (VMEM, (8, ROWS), jnp.int32),
            (VMEM, (8, ROWS), f32),
            (VMEM, (1, FEAT), f32),
        ],
        4,
        (0, 1000),
    )
    home_sums, tables = sent_home(home_sums, tables)
    grads = local_call(
        weight_grads,
        [where, *blocks, *fetched(act, d_gate, d_up)],
        [(HBM, (1, D, HID), bf16), (HBM, (1, D, HID), bf16), (HBM, (1, HID, D), bf16)],
        20,
        (2 * 3 * 2 * ROWS * D * HID, 22 * 10**6),
        scratch=(
            pltpu.VMEM((8, ROWS, BOTH), bf16),
            pltpu.VMEM((8, FEAT, HID), bf16),
            pltpu.VMEM((8, FEAT, HID), bf16),
            pltpu.VMEM((8, HID, FEAT), bf16),
            pltpu.SemaphoreType.DMA((8,)),
            pltpu.SemaphoreType.DMA((8, 3)),
        ),
    )
    home_sums, *grads = lax.optimization_barrier((home_sums, *grads))
    home = exchange(home_sums)
    moe, grad_hidden, grad_gates = local_call(
        finish,
        held(home, kept, *tables),
        [(COPY, (ROWS, FEAT), bf16), (COPY, (ROWS, FEAT), bf16), (COPY, (8, ROWS), f32)],
        4,
        (0, 1000),
    )
    return (moe, grad_hidden, grad_gates.T, *grads)


def solution(mesh):
    split = Mesh(mesh.devices.reshape(4, 2, 4, 4), ("y", "core", "x", "z"))
    heads, seq = ("y", "core"), ("x", "z")
    return jax.shard_map(
        on_device,
        mesh=split,
        in_specs=(
            P(seq, heads),
            P(heads),
            P(seq),
            P(seq, None),
            P(seq, None),
            P(seq, None),
            P(seq, None, heads),
            P(seq, None, heads),
            P(seq, heads, None),
            P(seq, heads),
        ),
        out_specs=(
            P(seq, heads),
            P(seq, heads),
            P(seq, None),
            P(seq, None, heads),
            P(seq, None, heads),
            P(seq, heads, None),
        ),
        check_vma=False,
    )
```

time: 92.8 us -> 91.1 us (0.982)
  starting transfers between devices: 15.4 us -> 12.3 us
  blocking collectives: 32.4 us -> 34.6 us
  Pallas kernels: 29.5 us -> 28.4 us
    ppermute x8 -> x6, starting transfers between devices: 13.1 us -> 10.5 us  [to_place(): return lax.ppermute(values, ('y', 'core'), pairs)]
    all_to_all x2, blocking collectives: 32.4 us -> 34.6 us  [exchange(): lax.all_to_all(pieces, ('x', 'z'), 0, 0, tiled=True).reshape(ROWS, width)]
    pallas_call x7 -> x9, Pallas kernels: 29.5 us -> 28.4 us  [local_call(): pl.pallas_call(kernel, out_shape=out_shape, in_specs=in_specs, out_specs=...]
    ppermute x8 -> x6, waiting for transfers between devices: 11.7 us -> 11.1 us  [to_place(): return lax.ppermute(values, ('y', 'core'), pairs)]
    ppermute x9 -> x8, starting transfers between devices: 2.32 us -> 1.76 us  [to_sibling(): return lax.ppermute(values, 'core', [(0, 1), (1, 0)])]
    ppermute x9 -> x8, waiting for transfers between devices: 1.37 us -> 1.88 us  [to_sibling(): return lax.ppermute(values, 'core', [(0, 1), (1, 0)])]
  transfers between devices with their start and end apart: 17 -> 14, of which waited for: 6 -> 6; matrix products, arithmetic and copies ran while one was open for 1% -> 1% of each run, Pallas kernels for 25% -> 26%
where the time goes in v4:
time: 91.1 us; the launch traced here: 90 us
  blocking collectives  34.6 us (38%)
  Pallas kernels  28.4 us (31%)
  waiting for transfers between devices  13 us (14%)
  starting transfers between devices  12.3 us (14%)
    all_to_all x2, blocking collectives, exchange(): lax.all_to_all(pieces, ('x', 'z'), 0, 0, tiled=True).reshape(ROWS, width)  34.6 us
    pallas_call x9, Pallas kernels, local_call(): pl.pallas_call(kernel, out_shape=out_shape, in_specs=in_specs, out_specs=...  28.4 us
    ppermute x6, waiting for transfers between devices, to_place(): return lax.ppermute(values, ('y', 'core'), pairs)  11.1 us
    ppermute x6, starting transfers between devices, to_place(): return lax.ppermute(values, ('y', 'core'), pairs)  10.5 us
    ppermute x8, waiting for transfers between devices, to_sibling(): return lax.ppermute(values, 'core', [(0, 1), (1, 0)])  1.88 us
  transfers between devices with their start and end apart: 14, of which 6 were waited for; matrix products, arithmetic and copies ran while one was open for 1% of the time, Pallas kernels for 26%

profile of v4, /device:TPU:0, one launch (start us, length us, event | category | flops | bytes accessed | tf_op | source)
XLA Modules:
  0.0 90.0 jit_solution(17979493888083397967)
XLA Ops:
  0.6 1.6 %shard_map.145 = (bf16[128,1920]{1,0:T(8,128)(2,1)S(1)}, bf16[128,896]{1,0:T(8,128)(2,1)S(1)}) custom-call(bf16[128,896]{1,0:T(8,128)(2,1)} %hidden.1, f32[896]{0:T(1024)} %gain.3, s32[1,128]{1,0:T(1,128)} %bitcast.31, s32[8,128]{1,0:T(8,128)} %bitcast.25, s32[8,128]{1,0:T(8,128)} %bitcast.27, f32[8,128]{1,0:T(8,128)} %bitcast.29, bf16[128,896]{1,0:T(8,128)(2,1)} %cotangent.1), custom_call_target="tpu_custom_call" | custom-call | bytes 1000 | tf_op jit(solution)/shard_map/pallas_call | solution.py:48
  2.2 18.9 %all_to_all.10 = bf16[16,8,1920]{2,1,0:T(8,128)(2,1)S(1)} all-to-all(bf16[16,8,1920]{2,1,0:T(8,128)(2,1)S(1)} %bitcast.23), channel_id=1, replica_groups=mesh['y'=4,'core'=2,'x'=4,'z'=4] {'x','z'}, dimensions={0} | all-to-all | bytes 983040 | tf_op jit(solution)/shard_map/all_to_all | solution.py:334
  21.2 3.0 %collective-permute-start.1 = (bf16[128,1920]{1,0:T(8,128)(2,1)S(1)}, bf16[128,1920]{1,0:T(8,128)(2,1)S(1)}, u32[]{:S(2)}, u32[]{:S(2)}) collective-permute-start(bf16[128,1920]{1,0:T(8,128)(2,1)S(1)} %bitcast.18), channel_id=1, source_target_pairs={{0,96},{16,48},{32,64},{48,16},{64,32},{80,112},{96,0},{112,80},{1... | collective-permute-start | bytes 1474568 | tf_op jit(solution)/shard_map/ppermute | solution.py:310
  24.2 0.1 collective-permute-start
  24.3 6.2 %shard_map.146 = (bf16[256,7168]{1,0:T(8,128)(2,1)}, bf16[256,7168]{1,0:T(8,128)(2,1)}) custom-call(bf16[1,7168,256]{2,1,0:T(8,128)(2,1)} %refs_4_.1, bf16[1,7168,256]{2,1,0:T(8,128)(2,1)} %refs_5_.1), custom_call_target="tpu_custom_call" | custom-call | bytes 60000000 | tf_op jit(solution)/shard_map/pallas_call | solution.py:48
  30.6 3.4 %shard_map.147 = (f32[128,256]{1,0:T(8,128)S(1)}, f32[128,256]{1,0:T(8,128)S(1)}, f32[128,256]{1,0:T(8,128)S(1)}, f32[128,128]{1,0:T(8,128)S(1)}, bf16[2,896,256...) custom-call(s32[8]{0:T(128)S(1)} %stack.35.where, ...), custom_call_target="tpu_custom_call" | custom-call | bytes 1000 | tf_op jit(solution)/shard_map/pallas_call | solution.py:48
  34.1 1.7 %collective-permute-done.1.refs_1_.refs_2_ = bf16[128,1920]{1,0:T(8,128)(2,1)S(1)} collective-permute-done((bf16[128,1920]{1,0:T(8,128)(2,1)S(1)}, bf16[128,1920]{1,0:T(8,128)(2,1)S(1)}, u32[]{:S(2)}, u32[]{:S(2)}) %collective-permute-start.1) | collective-permute-done | bytes 491552 | tf_op jit(solution)/shard_map/ppermute | solution.py:310
  35.8 0.6 collective-permute-start.5
  36.4 0.1 collective-permute-start.4
  36.5 3.6 %collective-permute-start.3 = (bf16[128,1920]{1,0:T(8,128)(2,1)S(1)}, bf16[128,1920]{1,0:T(8,128)(2,1)S(1)}, u32[]{:S(2)}, u32[]{:S(2)}) collective-permute-start(bf16[128,1920]{1,0:T(8,128)(2,1)S(1)} %collective-permute-done.refs_0_.refs_1_), channel_id=1, source_target_pairs={{0,96},{16,48},{32,64},{48,16},{64,32},{80,112},{96,0},{112,80},{1... | collective-permute-start | bytes 1474568 | tf_op jit(solution)/shard_map/ppermute | solution.py:310
  40.1 3.9 %shard_map.148 = (f32[128,256]{1,0:T(8,128)S(1)}, f32[128,256]{1,0:T(8,128)S(1)}, f32[128,256]{1,0:T(8,128)S(1)}, f32[128,128]{1,0:T(8,128)S(1)}) custom-call(s32[8]{0:T(128)S(1)} %stack.35.where, bf16[128,1920]{1,0:T(8,128)(2,1)S(1)} %collective-permute-done.refs_0_.refs_1_, bf16[128,1920]{1,0:T(8,128)(2,1)S(1)} %collective-permute-done.1.refs_1_.refs_2_, ...), custom_call_target="tpu_custom_call" | custom-call | flops 10000000000 | bytes 1000 | tf_op jit(solution)/shard_map/pallas_call | solution.py:48
  44.1 2.8 %collective-permute-done.3.refs_0_.refs_3_ = bf16[128,1920]{1,0:T(8,128)(2,1)S(1)} collective-permute-done((bf16[128,1920]{1,0:T(8,128)(2,1)S(1)}, bf16[128,1920]{1,0:T(8,128)(2,1)S(1)}, u32[]{:S(2)}, u32[]{:S(2)}) %collective-permute-start.3) | collective-permute-done | bytes 491552 | tf_op jit(solution)/shard_map/ppermute | solution.py:310
  46.9 1.9 %collective-permute-done.6.refs_1_.refs_7_ = bf16[128,1920]{1,0:T(8,128)(2,1)S(1)} collective-permute-done((bf16[128,1920]{1,0:T(8,128)(2,1)S(1)}, bf16[128,1920]{1,0:T(8,128)(2,1)S(1)}, u32[]{:S(2)}, u32[]{:S(2)}) %collective-permute-start.6) | collective-permute-done | bytes 491552 | tf_op jit(solution)/shard_map/ppermute | solution.py:314
  48.8 2.3 %shard_map.149 = (bf16[128,256]{1,0:T(8,128)(2,1)S(1)}, bf16[128,256]{1,0:T(8,128)(2,1)S(1)}, bf16[128,256]{1,0:T(8,128)(2,1)S(1)}, bf16[128,128]{1,0:T(8,128)(2...) custom-call(s32[8]{0:T(128)S(1)} %stack.35.where, ...), custom_call_target="tpu_custom_call" | custom-call | flops 1000000000 | bytes 1000 | tf_op jit(solution)/shard_map/pallas_call | solution.py:48
  51.2 0.2 collective-permute-start.9
  51.4 0.4 collective-permute-start.12
  51.7 1.6 %shard_map.150 = (bf16[128,1920]{1,0:T(8,128)(2,1)S(1)}, bf16[128,1920]{1,0:T(8,128)(2,1)S(1)}, bf16[128,1920]{1,0:T(8,128)(2,1)S(1)}, bf16[128,1920]{1,0:T(8,128)(2,1)S(1)}) custom-call(s32[8]{0:T(128)S(1)} %stack.35.where, bf16[128,256]{1,0:T(8,128)(2,1)S(1)} %get-tuple-element.90.act.refs_8_, bf16[128,256]{1,0:T(8,128)(2,1)S(1)} %get-tuple-element.91.grad_gate.refs_9_, ...), custom_call_target="tpu_custom_call" | custom-call | flops 2000000000 | bytes 1000 | tf_op jit(solution)/shard_map/pallas_call | solution.py:48
  53.4 0.1 add_convert_fusion.3
  53.5 3.3 %collective-permute-start.10 = (bf16[128,1920]{1,0:T(8,128)(2,1)S(1)}, bf16[128,1920]{1,0:T(8,128)(2,1)S(1)}, u32[]{:S(2)}, u32[]{:S(2)}) collective-permute-start(bf16[128,1920]{1,0:T(8,128)(2,1)S(1)} %add_convert_fusion.3), channel_id=1, source_target_pairs={{0,96},{16,48},{32,64},{48,16},{64,32},{80,112},{96,0},{112,80},{1... | collective-permute-start | bytes 1474568 | tf_op jit(solution)/shard_map/ppermute | solution.py:310
  56.8 0.5 collective-permute-start.7
  57.3 1.0 %shard_map.151 = (bf16[128,128]{1,0:T(8,128)(2,1)S(1)}, bf16[3,128,128]{2,1,0:T(8,128)(2,1)S(1)}, s32[8,128]{1,0:T(8,128)S(1)}, f32[8,128]{1,0:T(8,128)S(1)}, f32[1,896]{1,0:T(1,128)S(1)}) custom-call(s32[8,128]{1,0:T(8,128)} %bitcast.26, s32[8,128]{1,0:T(8,128)} %bitcast.28, f32[8,128]{1,0:T(8,128)} %bitcast.30, s32[1,128]{1,0:T(1,128)} %bitcast.32, f32[896]{0:T(1024)} %gain.3), custom_call_target="tpu_custom_call" | custom-call | bytes 1000 | tf_op jit(solution)/shard_map/pallas_call | solution.py:48
  58.3 0.1 add_convert_fusion.1
  58.4 0.2 collective-permute-start.13
  58.6 5.0 %collective-permute-done.10 = bf16[128,1920]{1,0:T(8,128)(2,1)S(1)} collective-permute-done((bf16[128,1920]{1,0:T(8,128)(2,1)S(1)}, bf16[128,1920]{1,0:T(8,128)(2,1)S(1)}, u32[]{:S(2)}, u32[]{:S(2)}) %collective-permute-start.10) | collective-permute-done | bytes 491552 | tf_op jit(solution)/shard_map/ppermute | solution.py:310
  63.6 0.2 add_convert_fusion.2
  63.8 0.3 collective-permute-start.11
  64.1 7.3 %shard_map.152 = (bf16[1,7168,256]{2,1,0:T(8,128)(2,1)}, bf16[1,7168,256]{2,1,0:T(8,128)(2,1)}, bf16[1,256,7168]{2,1,0:T(8,128)(2,1)}) custom-call(s32[8]{0:T(128)S(1)} %stack.35.where, bf16[128,1920]{1,0:T(8,128)(2,1)} %bitcast.21, bf16[128,1920]{1,0:T(8,128)(2,1)} %copy-done.11, bf16[128,1920]{1,0:T(8,128)(2,1)} %copy-done.10, ...), custom_call_target="tpu_custom_call" | custom-call | flops 2818572288 | bytes 22000000 | tf_op jit(solution)/shard_map/pallas_call | solution.py:48
  71.4 0.1 collective-permute-done.13
  71.5 1.4 %collective-permute-done.11 = bf16[128,1920]{1,0:T(8,128)(2,1)S(1)} collective-permute-done((bf16[128,1920]{1,0:T(8,128)(2,1)S(1)}, bf16[128,1920]{1,0:T(8,128)(2,1)S(1)}, u32[]{:S(2)}, u32[]{:S(2)}) %collective-permute-start.11) | collective-permute-done | bytes 491552 | tf_op jit(solution)/shard_map/ppermute | solution.py:310
  72.9 0.2 add_convert_fusion
  73.1 15.7 %all_to_all.11 = bf16[16,8,1920]{2,1,0:T(8,128)(2,1)S(1)} all-to-all(bf16[16,8,1920]{2,1,0:T(8,128)(2,1)S(1)} %bitcast.24), channel_id=1, replica_groups=mesh['y'=4,'core'=2,'x'=4,'z'=4] {'x','z'}, dimensions={0} | all-to-all | bytes 983040 | tf_op jit(solution)/shard_map/all_to_all | solution.py:334
  88.8 1.2 %shard_map.153 = (bf16[128,896]{1,0:T(8,128)(2,1)}, bf16[128,896]{1,0:T(8,128)(2,1)}, f32[8,128]{1,0:T(8,128)}) custom-call(bf16[128,1920]{1,0:T(8,128)(2,1)S(1)} %bitcast.22, bf16[128,896]{1,0:T(8,128)(2,1)S(1)} %get-tuple-element.114.hidden, bf16[128,128]{1,0:T(8,128)(2,1)S(1)} %get-tuple-element.115.select, ...), custom_call_target="tpu_custom_call" | custom-call | bytes 1000 | tf_op jit(solution)/shard_map/pallas_call | solution.py:48
  (40 shorter events, 0.2 us)
Async XLA Ops:
  21.1 9.5 %copy-start.3 = (bf16[16,8,1920]{2,1,0:T(8,128)(2,1)}, bf16[16,8,1920]{2,1,0:T(8,128)(2,1)S(1)}, u32[]{:S(2)}) copy-start(bf16[16,8,1920]{2,1,0:T(8,128)(2,1)S(1)} %all_to_all.10) | copy-start | bytes 1474564
  21.1 9.4 %collective-permute-start.2 = (bf16[128,1920]{1,0:T(8,128)(2,1)S(1)}, bf16[128,1920]{1,0:T(8,128)(2,1)S(1)}, u32[]{:S(2)}, u32[]{:S(2)}) collective-permute-start(bf16[128,1920]{1,0:T(8,128)(2,1)S(1)} %bitcast.17), channel_id=1, source_target_pairs={{0,16},{16,0},{1,17},{17,1},{2,18},{18,2},{3,19},{19,3},{4,20},{20... | collective-permute-start | bytes 1474568 | tf_op jit(solution)/shard_map/ppermute | solution.py:314
  21.2 14.6 %collective-permute-start.1 = (bf16[128,1920]{1,0:T(8,128)(2,1)S(1)}, bf16[128,1920]{1,0:T(8,128)(2,1)S(1)}, u32[]{:S(2)}, u32[]{:S(2)}) collective-permute-start(bf16[128,1920]{1,0:T(8,128)(2,1)S(1)} %bitcast.18), channel_id=1, source_target_pairs={{0,96},{16,48},{32,64},{48,16},{64,32},{80,112},{96,0},{112,80},{1... | collective-permute-start | bytes 1474568 | tf_op jit(solution)/shard_map/ppermute | solution.py:310
  24.2 11.6 %collective-permute-start = (bf16[128,1920]{1,0:T(8,128)(2,1)S(1)}, bf16[128,1920]{1,0:T(8,128)(2,1)S(1)}, u32[]{:S(2)}, u32[]{:S(2)}) collective-permute-start(bf16[128,1920]{1,0:T(8,128)(2,1)S(1)} %bitcast.19), channel_id=1, source_target_pairs={{0,32},{16,112},{32,0},{48,80},{64,96},{80,48},{96,64},{112,16},{1... | collective-permute-start | bytes 1474568 | tf_op jit(solution)/shard_map/ppermute | solution.py:310
  30.6 3.5 %copy-start.4 = (bf16[128,1920]{1,0:T(8,128)(2,1)}, bf16[128,1920]{1,0:T(8,128)(2,1)S(1)}, u32[]{:S(2)}) copy-start(bf16[128,1920]{1,0:T(8,128)(2,1)S(1)} %collective-permute-done.2.sibling.refs_4_) | copy-start | bytes 1474564
  35.8 8.2 %copy-start.10 = (bf16[128,1920]{1,0:T(8,128)(2,1)}, bf16[128,1920]{1,0:T(8,128)(2,1)S(1)}, u32[]{:S(2)}) copy-start(bf16[128,1920]{1,0:T(8,128)(2,1)S(1)} %collective-permute-done.1.refs_1_.refs_2_) | copy-start | bytes 1474564
  35.8 8.3 %copy-start.11 = (bf16[128,1920]{1,0:T(8,128)(2,1)}, bf16[128,1920]{1,0:T(8,128)(2,1)S(1)}, u32[]{:S(2)}) copy-start(bf16[128,1920]{1,0:T(8,128)(2,1)S(1)} %collective-permute-done.refs_0_.refs_1_) | copy-start | bytes 1474564
  35.8 13.0 %copy-start = (bf16[1,256,7168]{2,1,0:T(8,128)(2,1)S(1)}, bf16[1,256,7168]{2,1,0:T(8,128)(2,1)}, u32[]{:S(2)}) copy-start(bf16[1,256,7168]{2,1,0:T(8,128)(2,1)} %w_down.3) | copy-start | bytes 11010052
  35.8 13.0 %copy-start.1 = (bf16[256,7168]{1,0:T(8,128)(2,1)S(1)}, bf16[256,7168]{1,0:T(8,128)(2,1)}, u32[]{:S(2)}) copy-start(bf16[256,7168]{1,0:T(8,128)(2,1)} %get-tuple-element.88.refs_10_.gate_t) | copy-start | bytes 11010052
  35.8 13.0 %copy-start.2 = (bf16[256,7168]{1,0:T(8,128)(2,1)S(1)}, bf16[256,7168]{1,0:T(8,128)(2,1)}, u32[]{:S(2)}) copy-start(bf16[256,7168]{1,0:T(8,128)(2,1)} %get-tuple-element.89.refs_11_.up_t) | copy-start | bytes 11010052
  35.8 4.3 %collective-permute-start.5 = (bf16[128,1920]{1,0:T(8,128)(2,1)S(1)}, bf16[128,1920]{1,0:T(8,128)(2,1)S(1)}, u32[]{:S(2)}, u32[]{:S(2)}) collective-permute-start(bf16[128,1920]{1,0:T(8,128)(2,1)S(1)} %collective-permute-done.1.refs_1_.refs_2_), channel_id=1, source_target_pairs={{0,16},{16,0},{1,17},{17,1},{2,18},{18,2},{3,19},{19,3},{4,20},{20... | collective-permute-start | bytes 1474568 | tf_op jit(solution)/shard_map/ppermute | solution.py:314
  36.4 3.7 %collective-permute-start.4 = (bf16[128,1920]{1,0:T(8,128)(2,1)S(1)}, bf16[128,1920]{1,0:T(8,128)(2,1)S(1)}, u32[]{:S(2)}, u32[]{:S(2)}) collective-permute-start(bf16[128,1920]{1,0:T(8,128)(2,1)S(1)} %collective-permute-done.refs_0_.refs_1_), channel_id=1, source_target_pairs={{0,16},{16,0},{1,17},{17,1},{2,18},{18,2},{3,19},{19,3},{4,20},{20... | collective-permute-start | bytes 1474568 | tf_op jit(solution)/shard_map/ppermute | solution.py:314
  36.5 10.4 %collective-permute-start.3 = (bf16[128,1920]{1,0:T(8,128)(2,1)S(1)}, bf16[128,1920]{1,0:T(8,128)(2,1)S(1)}, u32[]{:S(2)}, u32[]{:S(2)}) collective-permute-start(bf16[128,1920]{1,0:T(8,128)(2,1)S(1)} %collective-permute-done.refs_0_.refs_1_), channel_id=1, source_target_pairs={{0,96},{16,48},{32,64},{48,16},{64,32},{80,112},{96,0},{112,80},{1... | collective-permute-start | bytes 1474568 | tf_op jit(solution)/shard_map/ppermute | solution.py:310
  40.1 3.9 %copy-start.12 = (bf16[128,1920]{1,0:T(8,128)(2,1)}, bf16[128,1920]{1,0:T(8,128)(2,1)S(1)}, u32[]{:S(2)}) copy-start(bf16[128,1920]{1,0:T(8,128)(2,1)S(1)} %collective-permute-done.5.refs_3_.refs_6_) | copy-start | bytes 1474564
  40.1 3.9 %copy-start.13 = (bf16[128,1920]{1,0:T(8,128)(2,1)}, bf16[128,1920]{1,0:T(8,128)(2,1)S(1)}, u32[]{:S(2)}) copy-start(bf16[128,1920]{1,0:T(8,128)(2,1)S(1)} %collective-permute-done.4.refs_2_.refs_5_) | copy-start | bytes 1474564
  46.9 4.2 %copy-start.5 = (bf16[128,1920]{1,0:T(8,128)(2,1)}, bf16[128,1920]{1,0:T(8,128)(2,1)S(1)}, u32[]{:S(2)}) copy-start(bf16[128,1920]{1,0:T(8,128)(2,1)S(1)} %collective-permute-done.3.refs_0_.refs_3_) | copy-start | bytes 1474564
  46.9 1.9 %collective-permute-start.6 = (bf16[128,1920]{1,0:T(8,128)(2,1)S(1)}, bf16[128,1920]{1,0:T(8,128)(2,1)S(1)}, u32[]{:S(2)}, u32[]{:S(2)}) collective-permute-start(bf16[128,1920]{1,0:T(8,128)(2,1)S(1)} %collective-permute-done.3.refs_0_.refs_3_), channel_id=1, source_target_pairs={{0,16},{16,0},{1,17},{17,1},{2,18},{18,2},{3,19},{19,3},{4,20},{20... | collective-permute-start | bytes 1474568 | tf_op jit(solution)/shard_map/ppermute | solution.py:314
  48.8 2.3 %copy-start.6 = (bf16[128,1920]{1,0:T(8,128)(2,1)}, bf16[128,1920]{1,0:T(8,128)(2,1)S(1)}, u32[]{:S(2)}) copy-start(bf16[128,1920]{1,0:T(8,128)(2,1)S(1)} %collective-permute-done.6.refs_1_.refs_7_) | copy-start | bytes 1474564
  51.1 2.2 %copy-start.7 = (bf16[128,256]{1,0:T(8,128)(2,1)}, bf16[128,256]{1,0:T(8,128)(2,1)S(1)}, u32[]{:S(2)}) copy-start(bf16[128,256]{1,0:T(8,128)(2,1)S(1)} %get-tuple-element.90.act.refs_8_) | copy-start | bytes 196612
  51.1 2.2 %copy-start.8 = (bf16[128,256]{1,0:T(8,128)(2,1)}, bf16[128,256]{1,0:T(8,128)(2,1)S(1)}, u32[]{:S(2)}) copy-start(bf16[128,256]{1,0:T(8,128)(2,1)S(1)} %get-tuple-element.91.grad_gate.refs_9_) | copy-start | bytes 196612
  51.1 2.2 %copy-start.9 = (bf16[128,256]{1,0:T(8,128)(2,1)}, bf16[128,256]{1,0:T(8,128)(2,1)S(1)}, u32[]{:S(2)}) copy-start(bf16[128,256]{1,0:T(8,128)(2,1)S(1)} %get-tuple-element.92.grad_up.refs_10_) | copy-start | bytes 196612
  51.2 2.2 %collective-permute-start.9 = (bf16[128,1920]{1,0:T(8,128)(2,1)S(1)}, bf16[128,1920]{1,0:T(8,128)(2,1)S(1)}, u32[]{:S(2)}, u32[]{:S(2)}) collective-permute-start(bf16[128,1920]{1,0:T(8,128)(2,1)S(1)} %get-tuple-element.99), channel_id=1, source_target_pairs={{0,16},{16,0},{1,17},{17,1},{2,18},{18,2},{3,19},{19,3},{4,20},{20... | collective-permute-start | bytes 1474568 | tf_op jit(solution)/shard_map/ppermute | solution.py:314
  51.4 6.9 %collective-permute-start.12 = (bf16[128,1920]{1,0:T(8,128)(2,1)S(1)}, bf16[128,1920]{1,0:T(8,128)(2,1)S(1)}, u32[]{:S(2)}, u32[]{:S(2)}) collective-permute-start(bf16[128,1920]{1,0:T(8,128)(2,1)S(1)} %get-tuple-element.109), channel_id=1, source_target_pairs={{0,16},{16,0},{1,17},{17,1},{2,18},{18,2},{3,19},{19,3},{4,20},{20... | collective-permute-start | bytes 1474568 | tf_op jit(solution)/shard_map/ppermute | solution.py:314
  53.5 10.1 %collective-permute-start.10 = (bf16[128,1920]{1,0:T(8,128)(2,1)S(1)}, bf16[128,1920]{1,0:T(8,128)(2,1)S(1)}, u32[]{:S(2)}, u32[]{:S(2)}) collective-permute-start(bf16[128,1920]{1,0:T(8,128)(2,1)S(1)} %add_convert_fusion.3), channel_id=1, source_target_pairs={{0,96},{16,48},{32,64},{48,16},{64,32},{80,112},{96,0},{112,80},{1... | collective-permute-start | bytes 1474568 | tf_op jit(solution)/shard_map/ppermute | solution.py:310
  56.8 6.8 %collective-permute-start.8 = (bf16[128,1920]{1,0:T(8,128)(2,1)S(1)}, bf16[128,1920]{1,0:T(8,128)(2,1)S(1)}, u32[]{:S(2)}, u32[]{:S(2)}) collective-permute-start(bf16[128,1920]{1,0:T(8,128)(2,1)S(1)} %get-tuple-element.97), channel_id=1, source_target_pairs={{0,16},{16,0},{1,17},{17,1},{2,18},{18,2},{3,19},{19,3},{4,20},{20... | collective-permute-start | bytes 1474568 | tf_op jit(solution)/shard_map/ppermute | solution.py:314
  56.8 14.6 %collective-permute-start.7 = (bf16[128,1920]{1,0:T(8,128)(2,1)S(1)}, bf16[128,1920]{1,0:T(8,128)(2,1)S(1)}, u32[]{:S(2)}, u32[]{:S(2)}) collective-permute-start(bf16[128,1920]{1,0:T(8,128)(2,1)S(1)} %get-tuple-element.95), channel_id=1, source_target_pairs={{0,16},{16,0},{1,17},{17,1},{2,18},{18,2},{3,19},{19,3},{4,20},{20... | collective-permute-start | bytes 1474568 | tf_op jit(solution)/shard_map/ppermute | solution.py:314
  58.4 13.1 %collective-permute-start.13 = (bf16[128,1920]{1,0:T(8,128)(2,1)S(1)}, bf16[128,1920]{1,0:T(8,128)(2,1)S(1)}, u32[]{:S(2)}, u32[]{:S(2)}) collective-permute-start(bf16[128,1920]{1,0:T(8,128)(2,1)S(1)} %add_convert_fusion.1), channel_id=1, source_target_pairs={{0,96},{16,48},{32,64},{48,16},{64,32},{80,112},{96,0},{112,80},{1... | collective-permute-start | bytes 1474568 | tf_op jit(solution)/shard_map/ppermute | solution.py:310
  63.8 9.1 %collective-permute-start.11 = (bf16[128,1920]{1,0:T(8,128)(2,1)S(1)}, bf16[128,1920]{1,0:T(8,128)(2,1)S(1)}, u32[]{:S(2)}, u32[]{:S(2)}) collective-permute-start(bf16[128,1920]{1,0:T(8,128)(2,1)S(1)} %add_convert_fusion.2), channel_id=1, source_target_pairs={{0,32},{16,112},{32,0},{48,80},{64,96},{80,48},{96,64},{112,16},{1... | collective-permute-start | bytes 1474568 | tf_op jit(solution)/shard_map/ppermute | solution.py:310

commit v5 on v4

--- a/solution.py
+++ b/solution.py
@@ -109,21 +109,6 @@
     kept[...] = hidden[...]
 
 
-def turn_weights(gate, up, gate_t, up_t, wide, wide_t, sems):
-    loads = [pltpu.make_async_copy(source, wide.at[i], sems.at[i]) for i, source in enumerate((gate, up))]
-    stores = [pltpu.make_async_copy(wide_t.at[i], target, sems.at[2 + i]) for i, target in enumerate((gate_t, up_t))]
-    for load in loads:
-        load.start()
-    for i in range(2):
-        loads[i].wait()
-        for head in range(8):
-            part = slice(head * FEAT, (head + 1) * FEAT)
-            wide_t[i, :, part] = wide[i, 0, part, :].T
-        stores[i].start()
-    for store in stores:
-        store.wait()
-
-
 def heads_here():
     y, core = lax.axis_index("y"), lax.axis_index("core")
     heads = []
@@ -185,30 +170,45 @@
     mean[...] = squares
 
 
-def near_blocks(where, *refs):
-    blocks, weights, sums, results, (*parts, sems) = refs[:4], refs[4:7], refs[7:11], refs[11:15], refs[15:]
-    places = ((0, 1), (0, 2), (1, 1), (1, 2))
-    copies = [
-        weight_copies(where, side, place, weights, [p.at[n] for p in parts], sems.at[n])
-        for n, (side, place) in enumerate(places)
+def first_block(where, own, w_gate, w_up, w_down, *refs):
+    sums, results, next_parts, (*parts, sems) = refs[:4], refs[4:8], refs[8:11], refs[11:]
+    weights = (w_gate, w_up, w_down)
+    copies = [weight_copies(where, 0, 1, weights, [p.at[0] for p in parts], sems.at[0])]
+    following = [
+        weight_copies(where, side, place, weights, [p.at[n] for p in next_parts], sems.at[1 + n])
+        for n, (side, place) in enumerate(((1, 1), (0, 2), (1, 2)))
     ]
-    totals, squares = add_blocks(copies, blocks, parts, [ref[...] for ref in sums[:3]], sums[3][...])
+    totals, squares = add_blocks(copies, (own,), parts, [ref[...] for ref in sums[:3]], sums[3][...])
+    for copies in following:
+        for copy in copies:
+            copy.wait()
     results[0][...], results[1][...], results[2][...] = totals
     results[3][...] = squares
 
 
-def expert_terms(where, act, d_gate, d_up, w_down, gate_t, up_t, side, results, tail):
-    for i in (3, 1, 2, 0):
-        columns = column_part(head_at(where, i, side))
+def next_blocks(first_low, first_high, second, second_low, second_high, *refs):
+    sums, parts, results = refs[:4], refs[4:7], refs[7:]
+    first_sibling = jnp.concatenate([first_low[...], first_high[...]], axis=0)
+    second_sibling = jnp.concatenate([second_low[...], second_high[...]], axis=0)
+    blocks = (first_sibling, second, second_sibling)
+    totals, squares = add_blocks(((), (), ()), blocks, parts, [ref[...] for ref in sums[:3]], sums[3][...])
+    results[0][...], results[1][...], results[2][...] = totals
+    results[3][...] = squares
+
+
+def expert_terms(where, act, d_gate, d_up, w_down, w_gate, w_up, side, results, tail):
+    for i in results:
+        head = head_at(where, i, side)
+        rows, columns = row_part(head), column_part(head)
         results[i][:, :FEAT] = nn(act, w_down[0, :, columns]).astype(bf16)
-        term = nn(d_gate, gate_t[:, columns]) + nn(d_up, up_t[:, columns])
+        term = nt(d_gate, w_gate[0, rows, :]) + nt(d_up, w_up[0, rows, :])
         results[i][:, FEAT : FEAT + FEAT] = term.astype(bf16)
         results[i][:, FEAT + FEAT :] = tail
 
 
 def last_blocks(where, *refs):
     blocks, (late_gate, late_up, late_down) = refs[:2], refs[2:5]
-    first_gate, first_up, first_hid, mean, w_down, gate_t, up_t = refs[5:12]
+    first_gate, first_up, first_hid, mean, w_down, w_gate, w_up = refs[5:12]
     act, grad_gate, grad_up, tail_out, *other = refs[12:]
     gate, up, hid = first_gate[...], first_up[...], first_hid[...]
     squares = mean[...]
@@ -240,23 +240,33 @@
         tail = jnp.where(lane == base + me + 1, low.astype(f32), tail)
     tail = tail.astype(bf16)
     tail_out[...] = tail
-    expert_terms(where, hidden_act, d_gate, d_up, w_down, gate_t, up_t, 1, other, tail)
-
-
-def own_terms(where, act, grad_gate, grad_up, tail, w_down, gate_t, up_t, *own):
-    expert_terms(where, act[...], grad_gate[...], grad_up[...], w_down, gate_t, up_t, 0, own, tail[...])
+    expert_terms(where, hidden_act, d_gate, d_up, w_down, w_gate, w_up, 1, {3: other[3], 2: other[2], 1: other[1], 0: other[0]}, tail)
+
+
+def own_across(where, act, grad_gate, grad_up, tail, w_down, w_gate, w_up, across):
+    expert_terms(where, act[...], grad_gate[...], grad_up[...], w_down, w_gate, w_up, 0, {3: across}, tail[...])
+
+
+def own_terms(where, act, grad_gate, grad_up, tail, w_down, w_gate, w_up, mine, first, second):
+    results = {2: second, 1: first, 0: mine}
+    expert_terms(where, act[...], grad_gate[...], grad_up[...], w_down, w_gate, w_up, 0, results, tail[...])
 
 
 def weight_grads(where, *refs):
-    blocks, (act, grad_gate, grad_up, out_gate, out_up, out_down) = refs[:8], refs[8:14]
-    held_rows, buf_gate, buf_up, buf_down, load_sems, store_sems = refs[14:]
-    loads = [pltpu.make_async_copy(block, held_rows.at[n], load_sems.at[n]) for n, block in enumerate(blocks)]
-    for load in loads:
-        load.start()
+    blocks, (act, grad_gate, grad_up, out_gate, out_up, out_down) = refs[:10], refs[10:16]
+    held_rows, buf_gate, buf_up, buf_down, load_sems, store_sems = refs[16:]
+    loads = [[] for _ in range(8)]
+    for i, block in enumerate(blocks):
+        n = i if i < 5 else (i + 5) // 2 if i < 9 else 7
+        start = ROWS // 2 if i in (6, 8) else 0
+        rows = slice(start, start + block.shape[0])
+        loads[n].append(pltpu.make_async_copy(block, held_rows.at[n, rows, :], load_sems.at[i]))
+        loads[n][-1].start()
     act_t = act[...].T
     stores = []
     for n in range(8):
-        loads[n].wait()
+        for load in loads[n]:
+            load.wait()
         head = head_at(where, n % 4, n // 4)
         beam_t = held_rows[n, :, :FEAT].T
         for j, (left, right, buf, target) in enumerate(
@@ -348,18 +358,6 @@
         8,
         (0, 1000),
     )
-    turned = local_call(
-        turn_weights,
-        [(HBM, w_gate), (HBM, w_up)],
-        [(HBM, (HID, D), bf16), (HBM, (HID, D), bf16)],
-        20,
-        (0, 60 * 10**6),
-        scratch=(
-            pltpu.VMEM((2, 1, D, HID), bf16),
-            pltpu.VMEM((2, HID, D), bf16),
-            pltpu.SemaphoreType.DMA((4,)),
-        ),
-    )
     sent = exchange(rows)
     weights = [(HBM, w_gate), (HBM, w_up), (HBM, w_down)]
     sums = [*[(VMEM, (ROWS, HID), f32)] * 3, (VMEM, (ROWS, WIDE - FEAT), f32)]
@@ -378,29 +376,45 @@
             pltpu.SemaphoreType.DMA((4, 3)),
         ),
     )
-    first, second = to_place(sent, 1), to_place(sent, 2)
-    first, second, gate_t, up_t, *early = lax.optimization_barrier((first, second, *turned, *early))
+    later, *early = lax.optimization_barrier((sent, *early))
+    first, second = to_place(sent, 1), to_place(later, 2)
+    first, *early = lax.optimization_barrier((first, *early))
     across = to_place(first, 2)
-    near = [sent, first, second]
-    near_sibling = [sibling, to_sibling(first), to_sibling(second)]
-    gate, up, hid, mean = local_call(
-        near_blocks,
-        [where, *held(*near[1:], *near_sibling[1:]), *weights, *held(*early)],
-        sums,
-        12,
-        (10**10, 1000),
+    first_halves = [to_sibling(first[: ROWS // 2]), to_sibling(first[ROWS // 2 :])]
+    *early, next_gate, next_up, next_down = local_call(
+        first_block,
+        [where, *held(first), *weights, *held(*early)],
+        [
+            *sums,
+            (VMEM, (3, FEAT, HID), bf16),
+            (VMEM, (3, FEAT, HID), bf16),
+            (VMEM, (3, HID, FEAT), bf16),
+        ],
+        8,
+        (0, 1000),
         scratch=(
-            pltpu.VMEM((4, FEAT, HID), bf16),
-            pltpu.VMEM((4, FEAT, HID), bf16),
-            pltpu.VMEM((4, HID, FEAT), bf16),
+            pltpu.VMEM((1, FEAT, HID), bf16),
+            pltpu.VMEM((1, FEAT, HID), bf16),
+            pltpu.VMEM((1, HID, FEAT), bf16),
             pltpu.SemaphoreType.DMA((4, 3)),
         ),
+    )
+    second, *early = lax.optimization_barrier((second, *early))
+    second_halves = [to_sibling(second[: ROWS // 2]), to_sibling(second[ROWS // 2 :])]
+    near = [sent, first, second]
+    near_sibling = [sibling, *first_halves, *second_halves]
+    gate, up, hid, mean = local_call(
+        next_blocks,
+        held(*first_halves, second, *second_halves, *early, next_gate, next_up, next_down),
+        sums,
+        4,
+        (10**9, 1000),
     )
     across, mean = lax.optimization_barrier((across, mean))
     across_sibling = to_sibling(across)
     act, d_gate, d_up, tail, *other = local_call(
         last_blocks,
-        [where, *held(across, across_sibling, late_gate, late_up, late_down, gate, up, hid, mean, w_down, gate_t, up_t)],
+        [where, *held(across, across_sibling, late_gate, late_up, late_down, gate, up, hid, mean, w_down, w_gate, w_up)],
         [
             *[(VMEM, (ROWS, HID), bf16)] * 3,
             (VMEM, (ROWS, WIDE - FEAT), bf16),
@@ -410,15 +424,13 @@
         (10**9, 1000),
     )
     theirs = [to_sibling(value) for value in other]
-    own = local_call(
-        own_terms,
-        [where, *held(act, d_gate, d_up, tail, w_down, gate_t, up_t)],
-        [(VMEM, (ROWS, BOTH), bf16)] * 4,
-        4,
-        (2 * 10**9, 1000),
-    )
+    term_inputs = [where, *held(act, d_gate, d_up, tail, w_down, w_gate, w_up)]
+    (across_term,) = local_call(own_across, term_inputs, [(VMEM, (ROWS, BOTH), bf16)], 4, (0, 1000))
+    across_sum, later_tail = lax.optimization_barrier((joined(across_term, theirs[3]), tail))
+    term_inputs[4] = (VMEM, later_tail)
+    own = local_call(own_terms, term_inputs, [(VMEM, (ROWS, BOTH), bf16)] * 3, 4, (0, 1000))
     blocks = [(HBM, block) for block in (*near, across, *near_sibling, across_sibling)]
-    home_sums = [joined(mine, term) for mine, term in zip(own, theirs)]
+    home_sums = [joined(mine, term) for mine, term in zip(own, theirs)] + [across_sum]
     home_sums[3], late_gates = lax.optimization_barrier((home_sums[3], gates))
     tables = local_call(
         route_tables,
@@ -445,7 +457,7 @@
             pltpu.VMEM((8, FEAT, HID), bf16),
             pltpu.VMEM((8, FEAT, HID), bf16),
             pltpu.VMEM((8, HID, FEAT), bf16),
-            pltpu.SemaphoreType.DMA((8,)),
+            pltpu.SemaphoreType.DMA((10,)),
             pltpu.SemaphoreType.DMA((8, 3)),
         ),
     )

time: 91.1 us -> 87.3 us (0.958)
  Pallas kernels: 28.4 us -> 24.3 us
  starting transfers between devices: 12.3 us -> 14.3 us
  waiting for transfers between devices: 13 us -> 11.2 us
    pallas_call x9 -> x10, Pallas kernels: 28.4 us -> 24.3 us  [local_call(): pl.pallas_call(kernel, out_shape=out_shape, in_specs=in_specs, out_specs=...]
    ppermute x6, waiting for transfers between devices: 11.1 us -> 7.55 us  [to_place(): return lax.ppermute(values, ('y', 'core'), pairs)]
    ppermute x8 -> x10, waiting for transfers between devices: 1.88 us -> 3.7 us  [to_sibling(): return lax.ppermute(values, 'core', [(0, 1), (1, 0)])]
    ppermute x6, starting transfers between devices: 10.5 us -> 12 us  [to_place(): return lax.ppermute(values, ('y', 'core'), pairs)]
    ppermute x8 -> x10, starting transfers between devices: 1.76 us -> 2.28 us  [to_sibling(): return lax.ppermute(values, 'core', [(0, 1), (1, 0)])]
  transfers between devices with their start and end apart: 14 -> 16, of which waited for: 6 -> 9; matrix products, arithmetic and copies ran while one was open for 1% -> 1% of each run, Pallas kernels for 26% -> 22%
where the time goes in v5:
time: 87.3 us; the launch traced here: 86.2 us
  blocking collectives  34.6 us (40%)
  Pallas kernels  24.3 us (28%)
  starting transfers between devices  14.3 us (16%)
  waiting for transfers between devices  11.2 us (13%)
  between operations  0.94 us (1%)
    all_to_all x2, blocking collectives, exchange(): lax.all_to_all(pieces, ('x', 'z'), 0, 0, tiled=True).reshape(ROWS, width)  34.6 us
    pallas_call x10, Pallas kernels, local_call(): pl.pallas_call(kernel, out_shape=out_shape, in_specs=in_specs, out_specs=...  24.3 us
    ppermute x6, starting transfers between devices, to_place(): return lax.ppermute(values, ('y', 'core'), pairs)  12 us
    ppermute x6, waiting for transfers between devices, to_place(): return lax.ppermute(values, ('y', 'core'), pairs)  7.55 us
    ppermute x10, waiting for transfers between devices, to_sibling(): return lax.ppermute(values, 'core', [(0, 1), (1, 0)])  3.7 us
    ppermute x10, starting transfers between devices, to_sibling(): return lax.ppermute(values, 'core', [(0, 1), (1, 0)])  2.28 us
  transfers between devices with their start and end apart: 16, of which 9 were waited for; matrix products, arithmetic and copies ran while one was open for 1% of the time, Pallas kernels for 22%

profile of v5, /device:TPU:0, one launch (start us, length us, event | category | flops | bytes accessed | tf_op | source)
XLA Modules:
  0.0 86.2 jit_solution(13900349197686006370)
XLA Ops:
  0.6 1.6 %shard_map.145 = (bf16[128,1920]{1,0:T(8,128)(2,1)S(1)}, bf16[128,896]{1,0:T(8,128)(2,1)S(1)}) custom-call(bf16[128,896]{1,0:T(8,128)(2,1)} %hidden.1, f32[896]{0:T(1024)} %gain.3, s32[1,128]{1,0:T(1,128)} %bitcast.31, s32[8,128]{1,0:T(8,128)} %bitcast.25, s32[8,128]{1,0:T(8,128)} %bitcast.27, f32[8,128]{1,0:T(8,128)} %bitcast.29, bf16[128,896]{1,0:T(8,128)(2,1)} %cotangent.1), custom_call_target="tpu_custom_call" | custom-call | bytes 1000 | tf_op jit(solution)/shard_map/pallas_call | solution.py:48
  2.2 18.9 %all_to_all.10 = bf16[16,8,1920]{2,1,0:T(8,128)(2,1)S(1)} all-to-all(bf16[16,8,1920]{2,1,0:T(8,128)(2,1)S(1)} %bitcast.23), channel_id=1, replica_groups=mesh['y'=4,'core'=2,'x'=4,'z'=4] {'x','z'}, dimensions={0} | all-to-all | bytes 983040 | tf_op jit(solution)/shard_map/all_to_all | solution.py:344
  21.2 1.6 %collective-permute-start = (bf16[128,1920]{1,0:T(8,128)(2,1)S(1)}, bf16[128,1920]{1,0:T(8,128)(2,1)S(1)}, u32[]{:S(2)}, u32[]{:S(2)}) collective-permute-start(bf16[128,1920]{1,0:T(8,128)(2,1)S(1)} %bitcast.18), channel_id=1, source_target_pairs={{0,32},{16,112},{32,0},{48,80},{64,96},{80,48},{96,64},{112,16},{1... | collective-permute-start | bytes 1474568 | tf_op jit(solution)/shard_map/ppermute | solution.py:320
  23.0 3.4 %shard_map.146 = (f32[128,256]{1,0:T(8,128)S(1)}, f32[128,256]{1,0:T(8,128)S(1)}, f32[128,256]{1,0:T(8,128)S(1)}, f32[128,128]{1,0:T(8,128)S(1)}, bf16[2,896,256...) custom-call(s32[8]{0:T(128)S(1)} %stack.35.where, ...), custom_call_target="tpu_custom_call" | custom-call | bytes 1000 | tf_op jit(solution)/shard_map/pallas_call | solution.py:48
  26.5 3.1 %collective-permute-start.5 = (bf16[128,1920]{1,0:T(8,128)(2,1)S(1)}, bf16[128,1920]{1,0:T(8,128)(2,1)S(1)}, u32[]{:S(2)}, u32[]{:S(2)}) collective-permute-start(bf16[128,1920]{1,0:T(8,128)(2,1)S(1)} %bitcast.20), channel_id=1, source_target_pairs={{0,96},{16,48},{32,64},{48,16},{64,32},{80,112},{96,0},{112,80},{1... | collective-permute-start | bytes 1474568 | tf_op jit(solution)/shard_map/ppermute | solution.py:320
  29.6 0.4 collective-permute-done.own.refs_1_
  30.0 3.7 %collective-permute-start.2 = (bf16[128,1920]{1,0:T(8,128)(2,1)S(1)}, bf16[128,1920]{1,0:T(8,128)(2,1)S(1)}, u32[]{:S(2)}, u32[]{:S(2)}) collective-permute-start(bf16[128,1920]{1,0:T(8,128)(2,1)S(1)} %collective-permute-done.own.refs_1_), channel_id=1, source_target_pairs={{0,96},{16,48},{32,64},{48,16},{64,32},{80,112},{96,0},{112,80},{1... | collective-permute-start | bytes 1474568 | tf_op jit(solution)/shard_map/ppermute | solution.py:320
  33.8 0.5 collective-permute-start.3
  34.3 3.5 %shard_map.147 = (f32[128,256]{1,0:T(8,128)S(1)}, f32[128,256]{1,0:T(8,128)S(1)}, f32[128,256]{1,0:T(8,128)S(1)}, f32[128,128]{1,0:T(8,128)S(1)}, bf16[3,896,256...) custom-call(s32[8]{0:T(128)S(1)} %stack.35.where, ...), custom_call_target="tpu_custom_call" | custom-call | bytes 1000 | tf_op jit(solution)/shard_map/pallas_call | solution.py:48
  38.0 0.4 collective-permute-start.6
  38.5 1.0 %collective-permute-done.7.second_high.refs_8_ = bf16[64,1920]{1,0:T(8,128)(2,1)S(1)} collective-permute-done((bf16[64,1920]{1,0:T(8,128)(2,1)S(1)}, bf16[64,1920]{1,0:T(8,128)(2,1)S(1)}, u32[]{:S(2)}, u32[]{:S(2)}) %collective-permute-start.7) | collective-permute-done | bytes 245792 | tf_op jit(solution)/shard_map/ppermute | solution.py:324
  39.4 0.3 collective-permute-done.6.second_low.refs_7_
  39.8 1.0 %shard_map.148 = (f32[128,256]{1,0:T(8,128)S(1)}, f32[128,256]{1,0:T(8,128)S(1)}, f32[128,256]{1,0:T(8,128)S(1)}, f32[128,128]{1,0:T(8,128)S(1)}) custom-call(bf16[64,1920]{1,0:T(8,128)(2,1)S(1)} %collective-permute-done.3.first_low.refs_5_, bf16[64,1920]{1,0:T(8,128)(2,1)S(1)} %collective-permute-done.4.first_high.refs_6_, ...), custom_call_target="tpu_custom_call" | custom-call | flops 1000000000 | bytes 1000 | tf_op jit(solution)/shard_map/pallas_call | solution.py:48
  40.8 1.1 %collective-permute-done.2.refs_0_.refs_3_ = bf16[128,1920]{1,0:T(8,128)(2,1)S(1)} collective-permute-done((bf16[128,1920]{1,0:T(8,128)(2,1)S(1)}, bf16[128,1920]{1,0:T(8,128)(2,1)S(1)}, u32[]{:S(2)}, u32[]{:S(2)}) %collective-permute-start.2) | collective-permute-done | bytes 491552 | tf_op jit(solution)/shard_map/ppermute | solution.py:320
  41.9 1.9 %collective-permute-done.8.refs_1_.refs_9_ = bf16[128,1920]{1,0:T(8,128)(2,1)S(1)} collective-permute-done((bf16[128,1920]{1,0:T(8,128)(2,1)S(1)}, bf16[128,1920]{1,0:T(8,128)(2,1)S(1)}, u32[]{:S(2)}, u32[]{:S(2)}) %collective-permute-start.8) | collective-permute-done | bytes 491552 | tf_op jit(solution)/shard_map/ppermute | solution.py:324
  43.7 2.6 %shard_map.149 = (bf16[128,256]{1,0:T(8,128)(2,1)S(1)}, bf16[128,256]{1,0:T(8,128)(2,1)S(1)}, bf16[128,256]{1,0:T(8,128)(2,1)S(1)}, bf16[128,128]{1,0:T(8,128)(2...) custom-call(s32[8]{0:T(128)S(1)} %stack.35.where, ...), custom_call_target="tpu_custom_call" | custom-call | flops 1000000000 | bytes 1000 | tf_op jit(solution)/shard_map/pallas_call | solution.py:48
  46.5 0.2 collective-permute-start.9
  46.7 0.4 collective-permute-start.14
  47.0 1.0 %shard_map.150 = bf16[128,1920]{1,0:T(8,128)(2,1)S(1)} custom-call(s32[8]{0:T(128)S(1)} %stack.35.where, bf16[128,256]{1,0:T(8,128)(2,1)S(1)} %get-tuple-element.115.act.refs_10_, bf16[128,256]{1,0:T(8,128)(2,1)S(1)} %get-tuple-element.116.grad_gate.refs_11_, bf16[128,256]{1,0:T(8,128)(2,1)S(1)} %get-tuple-element.117.grad_up.refs_12_, ...), custom_call_target="tpu_custom_call" | custom-call | bytes 1000 | tf_op jit(solution)/shard_map/pallas_call | solution.py:48
  48.1 0.3 collective-permute-done.9
  48.5 3.1 %collective-permute-start.12 = (bf16[128,1920]{1,0:T(8,128)(2,1)S(1)}, bf16[128,1920]{1,0:T(8,128)(2,1)S(1)}, u32[]{:S(2)}, u32[]{:S(2)}) collective-permute-start(bf16[128,1920]{1,0:T(8,128)(2,1)S(1)} %add_convert_fusion.5), channel_id=1, source_target_pairs={{0,96},{16,48},{32,64},{48,16},{64,32},{80,112},{96,0},{112,80},{1... | collective-permute-start | bytes 1474568 | tf_op jit(solution)/shard_map/ppermute | solution.py:320
  51.6 0.5 collective-permute-start.10
  52.1 1.0 %shard_map.152 = (bf16[128,128]{1,0:T(8,128)(2,1)S(1)}, bf16[3,128,128]{2,1,0:T(8,128)(2,1)S(1)}, s32[8,128]{1,0:T(8,128)S(1)}, f32[8,128]{1,0:T(8,128)S(1)}, f32[1,896]{1,0:T(1,128)S(1)}) custom-call(s32[8,128]{1,0:T(8,128)} %bitcast.26, s32[8,128]{1,0:T(8,128)} %bitcast.28, f32[8,128]{1,0:T(8,128)} %bitcast.30, s32[1,128]{1,0:T(1,128)} %bitcast.32, f32[896]{0:T(1024)} %gain.3), custom_call_target="tpu_custom_call" | custom-call | bytes 1000 | tf_op jit(solution)/shard_map/pallas_call | solution.py:48
  53.1 1.7 %shard_map.151 = (bf16[128,1920]{1,0:T(8,128)(2,1)S(1)}, bf16[128,1920]{1,0:T(8,128)(2,1)S(1)}, bf16[128,1920]{1,0:T(8,128)(2,1)S(1)}) custom-call(s32[8]{0:T(128)S(1)} %stack.35.where, bf16[128,256]{1,0:T(8,128)(2,1)S(1)} %get-tuple-element.115.act.refs_10_, bf16[128,256]{1,0:T(8,128)(2,1)S(1)} %get-tuple-element.116.grad_gate.refs_11_, ...), custom_call_target="tpu_custom_call" | custom-call | bytes 1000 | tf_op jit(solution)/shard_map/pallas_call | solution.py:48
  55.0 0.3 collective-permute-start.15
  55.3 3.4 %collective-permute-done.12 = bf16[128,1920]{1,0:T(8,128)(2,1)S(1)} collective-permute-done((bf16[128,1920]{1,0:T(8,128)(2,1)S(1)}, bf16[128,1920]{1,0:T(8,128)(2,1)S(1)}, u32[]{:S(2)}, u32[]{:S(2)}) %collective-permute-start.12) | collective-permute-done | bytes 491552 | tf_op jit(solution)/shard_map/ppermute | solution.py:320
  58.8 0.3 collective-permute-start.13
  59.1 7.3 %shard_map.153 = (bf16[1,7168,256]{2,1,0:T(8,128)(2,1)}, bf16[1,7168,256]{2,1,0:T(8,128)(2,1)}, bf16[1,256,7168]{2,1,0:T(8,128)(2,1)}) custom-call(s32[8]{0:T(128)S(1)} %stack.35.where, bf16[128,1920]{1,0:T(8,128)(2,1)} %bitcast.21, bf16[128,1920]{1,0:T(8,128)(2,1)} %copy-done.4, bf16[128,1920]{1,0:T(8,128)(2,1)} %copy-done.5, bf16[128,1920]{1,0:T(8,128)(2,1)} %copy-done.7, ...), custom_call_target="tpu_custom_call" | custom-call | flops 2818572288 | bytes 22000000 | tf_op jit(solution)/shard_map/pallas_call | solution.py:48
  66.4 2.7 %collective-permute-done.15 = bf16[128,1920]{1,0:T(8,128)(2,1)S(1)} collective-permute-done((bf16[128,1920]{1,0:T(8,128)(2,1)S(1)}, bf16[128,1920]{1,0:T(8,128)(2,1)S(1)}, u32[]{:S(2)}, u32[]{:S(2)}) %collective-permute-start.15) | collective-permute-done | bytes 491552 | tf_op jit(solution)/shard_map/ppermute | solution.py:320
  69.1 0.2 add_convert_fusion
  69.4 15.7 %all_to_all.11 = bf16[16,8,1920]{2,1,0:T(8,128)(2,1)S(1)} all-to-all(bf16[16,8,1920]{2,1,0:T(8,128)(2,1)S(1)} %bitcast.24), channel_id=1, replica_groups=mesh['y'=4,'core'=2,'x'=4,'z'=4] {'x','z'}, dimensions={0} | all-to-all | bytes 983040 | tf_op jit(solution)/shard_map/all_to_all | solution.py:344
  85.0 1.2 %shard_map.154 = (bf16[128,896]{1,0:T(8,128)(2,1)}, bf16[128,896]{1,0:T(8,128)(2,1)}, f32[8,128]{1,0:T(8,128)}) custom-call(bf16[128,1920]{1,0:T(8,128)(2,1)S(1)} %bitcast.22, bf16[128,896]{1,0:T(8,128)(2,1)S(1)} %get-tuple-element.140.hidden, bf16[128,128]{1,0:T(8,128)(2,1)S(1)} %get-tuple-element.141.select, ...), custom_call_target="tpu_custom_call" | custom-call | bytes 1000 | tf_op jit(solution)/shard_map/pallas_call | solution.py:48
  (51 shorter events, 1.1 us)
Async XLA Ops:
  21.1 5.3 %copy-start.3 = (bf16[16,8,1920]{2,1,0:T(8,128)(2,1)}, bf16[16,8,1920]{2,1,0:T(8,128)(2,1)S(1)}, u32[]{:S(2)}) copy-start(bf16[16,8,1920]{2,1,0:T(8,128)(2,1)S(1)} %all_to_all.10) | copy-start | bytes 1474564
  21.1 1.9 %collective-permute-start.1 = (bf16[128,1920]{1,0:T(8,128)(2,1)S(1)}, bf16[128,1920]{1,0:T(8,128)(2,1)S(1)}, u32[]{:S(2)}, u32[]{:S(2)}) collective-permute-start(bf16[128,1920]{1,0:T(8,128)(2,1)S(1)} %bitcast.17), channel_id=1, source_target_pairs={{0,16},{16,0},{1,17},{17,1},{2,18},{18,2},{3,19},{19,3},{4,20},{20... | collective-permute-start | bytes 1474568 | tf_op jit(solution)/shard_map/ppermute | solution.py:324
  21.2 8.8 %collective-permute-start = (bf16[128,1920]{1,0:T(8,128)(2,1)S(1)}, bf16[128,1920]{1,0:T(8,128)(2,1)S(1)}, u32[]{:S(2)}, u32[]{:S(2)}) collective-permute-start(bf16[128,1920]{1,0:T(8,128)(2,1)S(1)} %bitcast.18), channel_id=1, source_target_pairs={{0,32},{16,112},{32,0},{48,80},{64,96},{80,48},{96,64},{112,16},{1... | collective-permute-start | bytes 1474568 | tf_op jit(solution)/shard_map/ppermute | solution.py:320
  23.0 3.4 %copy-start.6 = (bf16[128,1920]{1,0:T(8,128)(2,1)}, bf16[128,1920]{1,0:T(8,128)(2,1)S(1)}, u32[]{:S(2)}) copy-start(bf16[128,1920]{1,0:T(8,128)(2,1)S(1)} %collective-permute-done.1.sibling.refs_4_) | copy-start | bytes 1474564
  26.5 11.3 %collective-permute-start.5 = (bf16[128,1920]{1,0:T(8,128)(2,1)S(1)}, bf16[128,1920]{1,0:T(8,128)(2,1)S(1)}, u32[]{:S(2)}, u32[]{:S(2)}) collective-permute-start(bf16[128,1920]{1,0:T(8,128)(2,1)S(1)} %bitcast.20), channel_id=1, source_target_pairs={{0,96},{16,48},{32,64},{48,16},{64,32},{80,112},{96,0},{112,80},{1... | collective-permute-start | bytes 1474568 | tf_op jit(solution)/shard_map/ppermute | solution.py:320
  30.0 7.8 %copy-start.4 = (bf16[128,1920]{1,0:T(8,128)(2,1)}, bf16[128,1920]{1,0:T(8,128)(2,1)S(1)}, u32[]{:S(2)}) copy-start(bf16[128,1920]{1,0:T(8,128)(2,1)S(1)} %collective-permute-done.own.refs_1_) | copy-start | bytes 1474564
  30.0 11.9 %collective-permute-start.2 = (bf16[128,1920]{1,0:T(8,128)(2,1)S(1)}, bf16[128,1920]{1,0:T(8,128)(2,1)S(1)}, u32[]{:S(2)}, u32[]{:S(2)}) collective-permute-start(bf16[128,1920]{1,0:T(8,128)(2,1)S(1)} %collective-permute-done.own.refs_1_), channel_id=1, source_target_pairs={{0,96},{16,48},{32,64},{48,16},{64,32},{80,112},{96,0},{112,80},{1... | collective-permute-start | bytes 1474568 | tf_op jit(solution)/shard_map/ppermute | solution.py:320
  33.7 4.8 %collective-permute-start.4 = (bf16[64,1920]{1,0:T(8,128)(2,1)S(1)}, bf16[64,1920]{1,0:T(8,128)(2,1)S(1)}, u32[]{:S(2)}, u32[]{:S(2)}) collective-permute-start(bf16[64,1920]{1,0:T(8,128)(2,1)S(1)} %get-tuple-element.154), channel_id=1, source_target_pairs={{0,16},{16,0},{1,17},{17,1},{2,18},{18,2},{3,19},{19,3},{4,20},{20... | collective-permute-start | bytes 737288 | tf_op jit(solution)/shard_map/ppermute | solution.py:324
  33.8 4.7 %collective-permute-start.3 = (bf16[64,1920]{1,0:T(8,128)(2,1)S(1)}, bf16[64,1920]{1,0:T(8,128)(2,1)S(1)}, u32[]{:S(2)}, u32[]{:S(2)}) collective-permute-start(bf16[64,1920]{1,0:T(8,128)(2,1)S(1)} %get-tuple-element.155), channel_id=1, source_target_pairs={{0,16},{16,0},{1,17},{17,1},{2,18},{18,2},{3,19},{19,3},{4,20},{20... | collective-permute-start | bytes 737288 | tf_op jit(solution)/shard_map/ppermute | solution.py:324
  34.3 9.5 %copy-start.1 = (bf16[1,7168,256]{2,1,0:T(8,128)(2,1)S(1)}, bf16[1,7168,256]{2,1,0:T(8,128)(2,1)}, u32[]{:S(2)}) copy-start(bf16[1,7168,256]{2,1,0:T(8,128)(2,1)} %w_up.7) | copy-start | bytes 11010052
  34.3 9.5 %copy-start.2 = (bf16[1,256,7168]{2,1,0:T(8,128)(2,1)S(1)}, bf16[1,256,7168]{2,1,0:T(8,128)(2,1)}, u32[]{:S(2)}) copy-start(bf16[1,256,7168]{2,1,0:T(8,128)(2,1)} %w_down.7) | copy-start | bytes 11010052
  37.8 6.0 %copy-start = (bf16[1,7168,256]{2,1,0:T(8,128)(2,1)S(1)}, bf16[1,7168,256]{2,1,0:T(8,128)(2,1)}, u32[]{:S(2)}) copy-start(bf16[1,7168,256]{2,1,0:T(8,128)(2,1)} %w_gate.7) | copy-start | bytes 11010052
  37.8 8.6 %copy-start.5 = (bf16[128,1920]{1,0:T(8,128)(2,1)}, bf16[128,1920]{1,0:T(8,128)(2,1)S(1)}, u32[]{:S(2)}) copy-start(bf16[128,1920]{1,0:T(8,128)(2,1)S(1)} %collective-permute-done.5.second.refs_2_) | copy-start | bytes 1474564
  37.9 1.6 %collective-permute-start.7 = (bf16[64,1920]{1,0:T(8,128)(2,1)S(1)}, bf16[64,1920]{1,0:T(8,128)(2,1)S(1)}, u32[]{:S(2)}, u32[]{:S(2)}) collective-permute-start(bf16[64,1920]{1,0:T(8,128)(2,1)S(1)} %get-tuple-element.152), channel_id=1, source_target_pairs={{0,16},{16,0},{1,17},{17,1},{2,18},{18,2},{3,19},{19,3},{4,20},{20... | collective-permute-start | bytes 737288 | tf_op jit(solution)/shard_map/ppermute | solution.py:324
  38.0 1.8 %collective-permute-start.6 = (bf16[64,1920]{1,0:T(8,128)(2,1)S(1)}, bf16[64,1920]{1,0:T(8,128)(2,1)S(1)}, u32[]{:S(2)}, u32[]{:S(2)}) collective-permute-start(bf16[64,1920]{1,0:T(8,128)(2,1)S(1)} %get-tuple-element.153), channel_id=1, source_target_pairs={{0,16},{16,0},{1,17},{17,1},{2,18},{18,2},{3,19},{19,3},{4,20},{20... | collective-permute-start | bytes 737288 | tf_op jit(solution)/shard_map/ppermute | solution.py:324
  38.4 7.9 %copy-start.12 = (bf16[64,1920]{1,0:T(8,128)(2,1)}, bf16[64,1920]{1,0:T(8,128)(2,1)S(1)}, u32[]{:S(2)}) copy-start(bf16[64,1920]{1,0:T(8,128)(2,1)S(1)} %collective-permute-done.4.first_high.refs_6_) | copy-start | bytes 737284
  38.5 7.9 %copy-start.13 = (bf16[64,1920]{1,0:T(8,128)(2,1)}, bf16[64,1920]{1,0:T(8,128)(2,1)S(1)}, u32[]{:S(2)}) copy-start(bf16[64,1920]{1,0:T(8,128)(2,1)S(1)} %collective-permute-done.3.first_low.refs_5_) | copy-start | bytes 737284
  39.4 6.9 %copy-start.14 = (bf16[64,1920]{1,0:T(8,128)(2,1)}, bf16[64,1920]{1,0:T(8,128)(2,1)S(1)}, u32[]{:S(2)}) copy-start(bf16[64,1920]{1,0:T(8,128)(2,1)S(1)} %collective-permute-done.7.second_high.refs_8_) | copy-start | bytes 737284
  39.8 6.6 %copy-start.15 = (bf16[64,1920]{1,0:T(8,128)(2,1)}, bf16[64,1920]{1,0:T(8,128)(2,1)S(1)}, u32[]{:S(2)}) copy-start(bf16[64,1920]{1,0:T(8,128)(2,1)S(1)} %collective-permute-done.6.second_low.refs_7_) | copy-start | bytes 737284
  41.9 4.5 %copy-start.7 = (bf16[128,1920]{1,0:T(8,128)(2,1)}, bf16[128,1920]{1,0:T(8,128)(2,1)S(1)}, u32[]{:S(2)}) copy-start(bf16[128,1920]{1,0:T(8,128)(2,1)S(1)} %collective-permute-done.2.refs_0_.refs_3_) | copy-start | bytes 1474564
  41.9 1.9 %collective-permute-start.8 = (bf16[128,1920]{1,0:T(8,128)(2,1)S(1)}, bf16[128,1920]{1,0:T(8,128)(2,1)S(1)}, u32[]{:S(2)}, u32[]{:S(2)}) collective-permute-start(bf16[128,1920]{1,0:T(8,128)(2,1)S(1)} %collective-permute-done.2.refs_0_.refs_3_), channel_id=1, source_target_pairs={{0,16},{16,0},{1,17},{17,1},{2,18},{18,2},{3,19},{19,3},{4,20},{20... | collective-permute-start | bytes 1474568 | tf_op jit(solution)/shard_map/ppermute | solution.py:324
  43.7 2.7 %copy-start.8 = (bf16[128,1920]{1,0:T(8,128)(2,1)}, bf16[128,1920]{1,0:T(8,128)(2,1)S(1)}, u32[]{:S(2)}) copy-start(bf16[128,1920]{1,0:T(8,128)(2,1)S(1)} %collective-permute-done.8.refs_1_.refs_9_) | copy-start | bytes 1474564
  46.4 6.7 %copy-start.9 = (bf16[128,256]{1,0:T(8,128)(2,1)}, bf16[128,256]{1,0:T(8,128)(2,1)S(1)}, u32[]{:S(2)}) copy-start(bf16[128,256]{1,0:T(8,128)(2,1)S(1)} %get-tuple-element.115.act.refs_10_) | copy-start | bytes 196612
  46.4 6.7 %copy-start.10 = (bf16[128,256]{1,0:T(8,128)(2,1)}, bf16[128,256]{1,0:T(8,128)(2,1)S(1)}, u32[]{:S(2)}) copy-start(bf16[128,256]{1,0:T(8,128)(2,1)S(1)} %get-tuple-element.116.grad_gate.refs_11_) | copy-start | bytes 196612
  46.4 6.6 %copy-start.11 = (bf16[128,256]{1,0:T(8,128)(2,1)}, bf16[128,256]{1,0:T(8,128)(2,1)S(1)}, u32[]{:S(2)}) copy-start(bf16[128,256]{1,0:T(8,128)(2,1)S(1)} %get-tuple-element.117.grad_up.refs_12_) | copy-start | bytes 196612
  46.5 1.9 %collective-permute-start.9 = (bf16[128,1920]{1,0:T(8,128)(2,1)S(1)}, bf16[128,1920]{1,0:T(8,128)(2,1)S(1)}, u32[]{:S(2)}, u32[]{:S(2)}) collective-permute-start(bf16[128,1920]{1,0:T(8,128)(2,1)S(1)} %get-tuple-element.119), channel_id=1, source_target_pairs={{0,16},{16,0},{1,17},{17,1},{2,18},{18,2},{3,19},{19,3},{4,20},{20... | collective-permute-start | bytes 1474568 | tf_op jit(solution)/shard_map/ppermute | solution.py:324
  46.7 8.2 %collective-permute-start.14 = (bf16[128,1920]{1,0:T(8,128)(2,1)S(1)}, bf16[128,1920]{1,0:T(8,128)(2,1)S(1)}, u32[]{:S(2)}, u32[]{:S(2)}) collective-permute-start(bf16[128,1920]{1,0:T(8,128)(2,1)S(1)} %get-tuple-element.135), channel_id=1, source_target_pairs={{0,16},{16,0},{1,17},{17,1},{2,18},{18,2},{3,19},{19,3},{4,20},{20... | collective-permute-start | bytes 1474568 | tf_op jit(solution)/shard_map/ppermute | solution.py:324
  48.5 10.1 %collective-permute-start.12 = (bf16[128,1920]{1,0:T(8,128)(2,1)S(1)}, bf16[128,1920]{1,0:T(8,128)(2,1)S(1)}, u32[]{:S(2)}, u32[]{:S(2)}) collective-permute-start(bf16[128,1920]{1,0:T(8,128)(2,1)S(1)} %add_convert_fusion.5), channel_id=1, source_target_pairs={{0,96},{16,48},{32,64},{48,16},{64,32},{80,112},{96,0},{112,80},{1... | collective-permute-start | bytes 1474568 | tf_op jit(solution)/shard_map/ppermute | solution.py:320
  51.6 7.0 %collective-permute-start.11 = (bf16[128,1920]{1,0:T(8,128)(2,1)S(1)}, bf16[128,1920]{1,0:T(8,128)(2,1)S(1)}, u32[]{:S(2)}, u32[]{:S(2)}) collective-permute-start(bf16[128,1920]{1,0:T(8,128)(2,1)S(1)} %get-tuple-element.124), channel_id=1, source_target_pairs={{0,16},{16,0},{1,17},{17,1},{2,18},{18,2},{3,19},{19,3},{4,20},{20... | collective-permute-start | bytes 1474568 | tf_op jit(solution)/shard_map/ppermute | solution.py:324
  51.6 14.8 %collective-permute-start.10 = (bf16[128,1920]{1,0:T(8,128)(2,1)S(1)}, bf16[128,1920]{1,0:T(8,128)(2,1)S(1)}, u32[]{:S(2)}, u32[]{:S(2)}) collective-permute-start(bf16[128,1920]{1,0:T(8,128)(2,1)S(1)} %get-tuple-element.122), channel_id=1, source_target_pairs={{0,16},{16,0},{1,17},{17,1},{2,18},{18,2},{3,19},{19,3},{4,20},{20... | collective-permute-start | bytes 1474568 | tf_op jit(solution)/shard_map/ppermute | solution.py:324
  55.0 14.1 %collective-permute-start.15 = (bf16[128,1920]{1,0:T(8,128)(2,1)S(1)}, bf16[128,1920]{1,0:T(8,128)(2,1)S(1)}, u32[]{:S(2)}, u32[]{:S(2)}) collective-permute-start(bf16[128,1920]{1,0:T(8,128)(2,1)S(1)} %add_convert_fusion.1), channel_id=1, source_target_pairs={{0,96},{16,48},{32,64},{48,16},{64,32},{80,112},{96,0},{112,80},{1... | collective-permute-start | bytes 1474568 | tf_op jit(solution)/shard_map/ppermute | solution.py:320
  58.8 10.3 %collective-permute-start.13 = (bf16[128,1920]{1,0:T(8,128)(2,1)S(1)}, bf16[128,1920]{1,0:T(8,128)(2,1)S(1)}, u32[]{:S(2)}, u32[]{:S(2)}) collective-permute-start(bf16[128,1920]{1,0:T(8,128)(2,1)S(1)} %add_convert_fusion.2), channel_id=1, source_target_pairs={{0,32},{16,112},{32,0},{48,80},{64,96},{80,48},{96,64},{112,16},{1... | collective-permute-start | bytes 1474568 | tf_op jit(solution)/shard_map/ppermute | solution.py:320

commit v6 on v5

--- a/solution.py
+++ b/solution.py
@@ -1,3 +1,5 @@
+import functools
+
 import jax
 import jax.numpy as jnp
 from jax import lax
@@ -152,46 +154,34 @@
 
 
 def own_blocks(where, own, sibling, w_gate, w_up, w_down, *refs):
-    gate, up, hid, mean, late_gate, late_up, late_down, *parts, late, sems = refs
+    gate, up, hid, mean, *parts, sems = refs
     weights = (w_gate, w_up, w_down)
     copies = [weight_copies(where, side, 0, weights, [p.at[side] for p in parts], sems.at[side]) for side in range(2)]
-    last = [
-        weight_copies(where, side, 3, weights, (late_gate.at[side], late_up.at[side], late.at[side]), sems.at[2 + side])
-        for side in range(2)
-    ]
     zero = jnp.zeros((ROWS, HID), f32)
     squares = jnp.zeros((ROWS, WIDE - FEAT), f32)
     totals, squares = add_blocks(copies, (own, sibling), parts, (zero, zero, zero), squares)
-    for side in range(2):
-        for copy in last[side]:
-            copy.wait()
-        late_down[side] = late[side].T
     gate[...], up[...], hid[...] = totals
     mean[...] = squares
 
 
 def first_block(where, own, w_gate, w_up, w_down, *refs):
-    sums, results, next_parts, (*parts, sems) = refs[:4], refs[4:8], refs[8:11], refs[11:]
-    weights = (w_gate, w_up, w_down)
-    copies = [weight_copies(where, 0, 1, weights, [p.at[0] for p in parts], sems.at[0])]
-    following = [
-        weight_copies(where, side, place, weights, [p.at[n] for p in next_parts], sems.at[1 + n])
-        for n, (side, place) in enumerate(((1, 1), (0, 2), (1, 2)))
-    ]
+    sums, results, (*parts, sems) = refs[:4], refs[4:8], refs[8:]
+    copies = [weight_copies(where, 0, 1, (w_gate, w_up, w_down), [p.at[0] for p in parts], sems)]
     totals, squares = add_blocks(copies, (own,), parts, [ref[...] for ref in sums[:3]], sums[3][...])
-    for copies in following:
-        for copy in copies:
-            copy.wait()
     results[0][...], results[1][...], results[2][...] = totals
     results[3][...] = squares
 
 
-def next_blocks(first_low, first_high, second, second_low, second_high, *refs):
-    sums, parts, results = refs[:4], refs[4:7], refs[7:]
+def next_blocks(where, first_low, first_high, second, second_low, second_high, *refs):
+    sums, (w_gate, w_up, w_down), results = refs[:4], refs[4:7], refs[7:]
     first_sibling = jnp.concatenate([first_low[...], first_high[...]], axis=0)
     second_sibling = jnp.concatenate([second_low[...], second_high[...]], axis=0)
-    blocks = (first_sibling, second, second_sibling)
-    totals, squares = add_blocks(((), (), ()), blocks, parts, [ref[...] for ref in sums[:3]], sums[3][...])
+    totals, squares = [ref[...] for ref in sums[:3]], sums[3][...]
+    for place, side, block in ((1, 1, first_sibling), (2, 0, second), (2, 1, second_sibling)):
+        head = head_at(where, place, side)
+        rows, columns = row_part(head), column_part(head)
+        parts = ([w_gate[0, rows, :]], [w_up[0, rows, :]], [w_down[0, :, columns]])
+        totals, squares = add_blocks(((),), (block,), parts, totals, squares)
     results[0][...], results[1][...], results[2][...] = totals
     results[3][...] = squares
 
@@ -207,16 +197,17 @@
 
 
 def last_blocks(where, *refs):
-    blocks, (late_gate, late_up, late_down) = refs[:2], refs[2:5]
-    first_gate, first_up, first_hid, mean, w_down, w_gate, w_up = refs[5:12]
-    act, grad_gate, grad_up, tail_out, *other = refs[12:]
+    blocks, (first_gate, first_up, first_hid, mean), (w_down, w_gate, w_up) = refs[:2], refs[2:6], refs[6:9]
+    act, grad_gate, grad_up, tail_out, across_other = refs[9:]
     gate, up, hid = first_gate[...], first_up[...], first_hid[...]
     squares = mean[...]
     for side, block in enumerate(blocks):
         squares = squares + block[:, FEAT:WIDE].astype(f32)
-        gate = gate + nn(block[:, :FEAT], late_gate[side])
-        up = up + nn(block[:, :FEAT], late_up[side])
-        hid = hid + nn(block[:, WIDE:], late_down[side])
+        head = head_at(where, 3, side)
+        rows, columns = row_part(head), column_part(head)
+        gate = gate + nn(block[:, :FEAT], w_gate[0, rows, :])
+        up = up + nn(block[:, :FEAT], w_up[0, rows, :])
+        hid = hid + nt(block[:, WIDE:], w_down[0, :, columns])
     inverse = lax.rsqrt(jnp.sum(squares, axis=1, keepdims=True) + EPSILON)
     gate = gate * inverse
     up = up * inverse
@@ -240,16 +231,18 @@
         tail = jnp.where(lane == base + me + 1, low.astype(f32), tail)
     tail = tail.astype(bf16)
     tail_out[...] = tail
-    expert_terms(where, hidden_act, d_gate, d_up, w_down, w_gate, w_up, 1, {3: other[3], 2: other[2], 1: other[1], 0: other[0]}, tail)
-
-
-def own_across(where, act, grad_gate, grad_up, tail, w_down, w_gate, w_up, across):
-    expert_terms(where, act[...], grad_gate[...], grad_up[...], w_down, w_gate, w_up, 0, {3: across}, tail[...])
-
-
-def own_terms(where, act, grad_gate, grad_up, tail, w_down, w_gate, w_up, mine, first, second):
-    results = {2: second, 1: first, 0: mine}
-    expert_terms(where, act[...], grad_gate[...], grad_up[...], w_down, w_gate, w_up, 0, results, tail[...])
+    expert_terms(where, hidden_act, d_gate, d_up, w_down, w_gate, w_up, 1, {3: across_other}, tail)
+
+
+def own_across(where, act, grad_gate, grad_up, tail, w_down, w_gate, w_up, across, second_other):
+    terms = (where, act[...], grad_gate[...], grad_up[...], w_down, w_gate, w_up)
+    expert_terms(*terms, 0, {3: across}, tail[...])
+    expert_terms(*terms, 1, {2: second_other}, tail[...])
+
+
+def near_terms(side, where, act, grad_gate, grad_up, tail, w_down, w_gate, w_up, *terms):
+    results = {i: terms[i] for i in reversed(range(len(terms)))}
+    expert_terms(where, act[...], grad_gate[...], grad_up[...], w_down, w_gate, w_up, side, results, tail[...])
 
 
 def weight_grads(where, *refs):
@@ -362,18 +355,17 @@
     weights = [(HBM, w_gate), (HBM, w_up), (HBM, w_down)]
     sums = [*[(VMEM, (ROWS, HID), f32)] * 3, (VMEM, (ROWS, WIDE - FEAT), f32)]
     sibling = to_sibling(sent)
-    *early, late_gate, late_up, late_down = local_call(
+    early = local_call(
         own_blocks,
         [where, *held(sent, sibling), *weights],
-        [*sums, *[(VMEM, (2, FEAT, HID), bf16)] * 3],
+        sums,
         8,
         (0, 1000),
         scratch=(
             pltpu.VMEM((2, FEAT, HID), bf16),
             pltpu.VMEM((2, FEAT, HID), bf16),
             pltpu.VMEM((2, HID, FEAT), bf16),
-            pltpu.VMEM((2, HID, FEAT), bf16),
-            pltpu.SemaphoreType.DMA((4, 3)),
+            pltpu.SemaphoreType.DMA((2, 3)),
         ),
     )
     later, *early = lax.optimization_barrier((sent, *early))
@@ -381,22 +373,17 @@
     first, *early = lax.optimization_barrier((first, *early))
     across = to_place(first, 2)
     first_halves = [to_sibling(first[: ROWS // 2]), to_sibling(first[ROWS // 2 :])]
-    *early, next_gate, next_up, next_down = local_call(
+    early = local_call(
         first_block,
         [where, *held(first), *weights, *held(*early)],
-        [
-            *sums,
-            (VMEM, (3, FEAT, HID), bf16),
-            (VMEM, (3, FEAT, HID), bf16),
-            (VMEM, (3, HID, FEAT), bf16),
-        ],
+        sums,
         8,
         (0, 1000),
         scratch=(
             pltpu.VMEM((1, FEAT, HID), bf16),
             pltpu.VMEM((1, FEAT, HID), bf16),
             pltpu.VMEM((1, HID, FEAT), bf16),
-            pltpu.SemaphoreType.DMA((4, 3)),
+            pltpu.SemaphoreType.DMA((3,)),
         ),
     )
     second, *early = lax.optimization_barrier((second, *early))
@@ -405,30 +392,33 @@
     near_sibling = [sibling, *first_halves, *second_halves]
     gate, up, hid, mean = local_call(
         next_blocks,
-        held(*first_halves, second, *second_halves, *early, next_gate, next_up, next_down),
+        [where, *held(*first_halves, second, *second_halves, *early, w_gate, w_up, w_down)],
         sums,
         4,
         (10**9, 1000),
     )
     across, mean = lax.optimization_barrier((across, mean))
     across_sibling = to_sibling(across)
-    act, d_gate, d_up, tail, *other = local_call(
+    act, d_gate, d_up, tail, across_other = local_call(
         last_blocks,
-        [where, *held(across, across_sibling, late_gate, late_up, late_down, gate, up, hid, mean, w_down, w_gate, w_up)],
+        [where, *held(across, across_sibling, gate, up, hid, mean, w_down, w_gate, w_up)],
         [
             *[(VMEM, (ROWS, HID), bf16)] * 3,
             (VMEM, (ROWS, WIDE - FEAT), bf16),
-            *[(VMEM, (ROWS, BOTH), bf16)] * 4,
+            (VMEM, (ROWS, BOTH), bf16),
         ],
         4,
         (10**9, 1000),
     )
-    theirs = [to_sibling(value) for value in other]
     term_inputs = [where, *held(act, d_gate, d_up, tail, w_down, w_gate, w_up)]
-    (across_term,) = local_call(own_across, term_inputs, [(VMEM, (ROWS, BOTH), bf16)], 4, (0, 1000))
-    across_sum, later_tail = lax.optimization_barrier((joined(across_term, theirs[3]), tail))
+    across_own, second_other = local_call(own_across, term_inputs, [(VMEM, (ROWS, BOTH), bf16)] * 2, 4, (0, 1000))
+    across_sum, later_tail = lax.optimization_barrier((joined(across_own, to_sibling(across_other)), tail))
     term_inputs[4] = (VMEM, later_tail)
-    own = local_call(own_terms, term_inputs, [(VMEM, (ROWS, BOTH), bf16)] * 3, 4, (0, 1000))
+    other, own = [
+        local_call(functools.partial(near_terms, side), term_inputs, [(VMEM, (ROWS, BOTH), bf16)] * n, 4, (0, 1000))
+        for side, n in ((1, 2), (0, 3))
+    ]
+    theirs = [to_sibling(value) for value in (*other, second_other)]
     blocks = [(HBM, block) for block in (*near, across, *near_sibling, across_sibling)]
     home_sums = [joined(mine, term) for mine, term in zip(own, theirs)] + [across_sum]
     home_sums[3], late_gates = lax.optimization_barrier((home_sums[3], gates))

time: 87.3 us -> 86.7 us (level)
  blocking collectives: 34.6 us -> 33.3 us
    all_to_all x2, blocking collectives: 34.6 us -> 33.3 us  [exchange(): lax.all_to_all(pieces, ('x', 'z'), 0, 0, tiled=True).reshape(ROWS, width)]
    pallas_call x10 -> x11, Pallas kernels: 24.3 us -> 24.8 us  [local_call(): pl.pallas_call(kernel, out_shape=out_shape, in_specs=in_specs, out_specs=...]
  transfers between devices with their start and end apart: 16 -> 16, of which waited for: 9 -> 8; matrix products, arithmetic and copies ran while one was open for 1% -> 1% of each run, Pallas kernels for 22% -> 23%
where the time goes in v6:
time: 86.7 us; the launch traced here: 86.4 us
  blocking collectives  33.3 us (38%)
  Pallas kernels  24.8 us (29%)
  starting transfers between devices  14.8 us (17%)
  waiting for transfers between devices  11.6 us (13%)
  between operations  0.97 us (1%)
    all_to_all x2, blocking collectives, exchange(): lax.all_to_all(pieces, ('x', 'z'), 0, 0, tiled=True).reshape(ROWS, width)  33.3 us
    pallas_call x11, Pallas kernels, local_call(): pl.pallas_call(kernel, out_shape=out_shape, in_specs=in_specs, out_specs=...  24.8 us
    ppermute x6, starting transfers between devices, to_place(): return lax.ppermute(values, ('y', 'core'), pairs)  12.3 us
    ppermute x6, waiting for transfers between devices, to_place(): return lax.ppermute(values, ('y', 'core'), pairs)  8.22 us
    ppermute x10, waiting for transfers between devices, to_sibling(): return lax.ppermute(values, 'core', [(0, 1), (1, 0)])  3.4 us
    ppermute x10, starting transfers between devices, to_sibling(): return lax.ppermute(values, 'core', [(0, 1), (1, 0)])  2.43 us
  transfers between devices with their start and end apart: 16, of which 8 were waited for; matrix products, arithmetic and copies ran while one was open for 1% of the time, Pallas kernels for 23%

profile of v6, /device:TPU:0, one launch (start us, length us, event | category | flops | bytes accessed | tf_op | source)
XLA Modules:
  0.0 86.4 jit_solution(2117613180490901401)
XLA Ops:
  0.6 1.6 %shard_map.145 = (bf16[128,1920]{1,0:T(8,128)(2,1)S(1)}, bf16[128,896]{1,0:T(8,128)(2,1)S(1)}) custom-call(bf16[128,896]{1,0:T(8,128)(2,1)} %hidden.1, f32[896]{0:T(1024)} %gain.3, s32[1,128]{1,0:T(1,128)} %bitcast.31, s32[8,128]{1,0:T(8,128)} %bitcast.25, s32[8,128]{1,0:T(8,128)} %bitcast.27, f32[8,128]{1,0:T(8,128)} %bitcast.29, bf16[128,896]{1,0:T(8,128)(2,1)} %cotangent.1), custom_call_target="tpu_custom_call" | custom-call | bytes 1000 | tf_op jit(solution)/shard_map/pallas_call | solution.py:50
  2.2 18.9 %all_to_all.10 = bf16[16,8,1920]{2,1,0:T(8,128)(2,1)S(1)} all-to-all(bf16[16,8,1920]{2,1,0:T(8,128)(2,1)S(1)} %bitcast.23), channel_id=1, replica_groups=mesh['y'=4,'core'=2,'x'=4,'z'=4] {'x','z'}, dimensions={0} | all-to-all | bytes 983040 | tf_op jit(solution)/shard_map/all_to_all | solution.py:337
  21.2 1.6 %collective-permute-start = (bf16[128,1920]{1,0:T(8,128)(2,1)S(1)}, bf16[128,1920]{1,0:T(8,128)(2,1)S(1)}, u32[]{:S(2)}, u32[]{:S(2)}) collective-permute-start(bf16[128,1920]{1,0:T(8,128)(2,1)S(1)} %bitcast.18), channel_id=1, source_target_pairs={{0,32},{16,112},{32,0},{48,80},{64,96},{80,48},{96,64},{112,16},{1... | collective-permute-start | bytes 1474568 | tf_op jit(solution)/shard_map/ppermute | solution.py:313
  23.0 3.0 %shard_map.146 = (f32[128,256]{1,0:T(8,128)S(1)}, f32[128,256]{1,0:T(8,128)S(1)}, f32[128,256]{1,0:T(8,128)S(1)}, f32[128,128]{1,0:T(8,128)S(1)}) custom-call(s32[8]{0:T(128)S(1)} %stack.35.where, bf16[128,1920]{1,0:T(8,128)(2,1)S(1)} %bitcast.19, bf16[128,1920]{1,0:T(8,128)(2,1)S(1)} %collective-permute-done.1.sibling.refs_4_, ...), custom_call_target="tpu_custom_call" | custom-call | bytes 1000 | tf_op jit(solution)/shard_map/pallas_call | solution.py:50
  26.0 3.1 %collective-permute-start.5 = (bf16[128,1920]{1,0:T(8,128)(2,1)S(1)}, bf16[128,1920]{1,0:T(8,128)(2,1)S(1)}, u32[]{:S(2)}, u32[]{:S(2)}) collective-permute-start(bf16[128,1920]{1,0:T(8,128)(2,1)S(1)} %bitcast.20), channel_id=1, source_target_pairs={{0,96},{16,48},{32,64},{48,16},{64,32},{80,112},{96,0},{112,80},{1... | collective-permute-start | bytes 1474568 | tf_op jit(solution)/shard_map/ppermute | solution.py:313
  29.1 1.0 %collective-permute-done.own.refs_1_ = bf16[128,1920]{1,0:T(8,128)(2,1)S(1)} collective-permute-done((bf16[128,1920]{1,0:T(8,128)(2,1)S(1)}, bf16[128,1920]{1,0:T(8,128)(2,1)S(1)}, u32[]{:S(2)}, u32[]{:S(2)}) %collective-permute-start) | collective-permute-done | bytes 491552 | tf_op jit(solution)/shard_map/ppermute | solution.py:313
  30.1 4.0 %collective-permute-start.2 = (bf16[128,1920]{1,0:T(8,128)(2,1)S(1)}, bf16[128,1920]{1,0:T(8,128)(2,1)S(1)}, u32[]{:S(2)}, u32[]{:S(2)}) collective-permute-start(bf16[128,1920]{1,0:T(8,128)(2,1)S(1)} %collective-permute-done.own.refs_1_), channel_id=1, source_target_pairs={{0,96},{16,48},{32,64},{48,16},{64,32},{80,112},{96,0},{112,80},{1... | collective-permute-start | bytes 1474568 | tf_op jit(solution)/shard_map/ppermute | solution.py:313
  34.2 0.5 collective-permute-start.4
  34.7 2.8 %shard_map.147 = (f32[128,256]{1,0:T(8,128)S(1)}, f32[128,256]{1,0:T(8,128)S(1)}, f32[128,256]{1,0:T(8,128)S(1)}, f32[128,128]{1,0:T(8,128)S(1)}) custom-call(s32[8]{0:T(128)S(1)} %stack.35.where, bf16[128,1920]{1,0:T(8,128)(2,1)S(1)} %collective-permute-done.own.refs_1_, bf16[1,7168,256]{2,1,0:T(8,128)(2,1)} %w_gate.9, bf16[1,7168,256]{2,1,0:T(8,128)(2,1)} %w_up.9, ...), custom_call_target="tpu_custom_call" | custom-call | bytes 1000 | tf_op jit(solution)/shard_map/pallas_call | solution.py:50
  37.7 0.5 collective-permute-start.7
  38.2 1.0 %collective-permute-done.6.second_low.refs_7_ = bf16[64,1920]{1,0:T(8,128)(2,1)S(1)} collective-permute-done((bf16[64,1920]{1,0:T(8,128)(2,1)S(1)}, bf16[64,1920]{1,0:T(8,128)(2,1)S(1)}, u32[]{:S(2)}, u32[]{:S(2)}) %collective-permute-start.6) | collective-permute-done | bytes 245792 | tf_op jit(solution)/shard_map/ppermute | solution.py:317
  39.2 0.3 collective-permute-done.7.second_high.refs_8_
  39.6 1.5 %shard_map.148 = (f32[128,256]{1,0:T(8,128)S(1)}, f32[128,256]{1,0:T(8,128)S(1)}, f32[128,256]{1,0:T(8,128)S(1)}, f32[128,128]{1,0:T(8,128)S(1)}) custom-call(s32[8]{0:T(128)S(1)} %stack.35.where, bf16[64,1920]{1,0:T(8,128)(2,1)S(1)} %collective-permute-done.3.first_low.refs_5_, bf16[64,1920]{1,0:T(8,128)(2,1)S(1)} %collective-permute-done.4.first_high.refs_6_, ...), custom_call_target="tpu_custom_call" | custom-call | flops 1000000000 | bytes 1000 | tf_op jit(solution)/shard_map/pallas_call | solution.py:50
  41.1 0.3 collective-permute-done.2.refs_0_.refs_3_
  41.4 1.9 %collective-permute-done.8.refs_1_.refs_9_ = bf16[128,1920]{1,0:T(8,128)(2,1)S(1)} collective-permute-done((bf16[128,1920]{1,0:T(8,128)(2,1)S(1)}, bf16[128,1920]{1,0:T(8,128)(2,1)S(1)}, u32[]{:S(2)}, u32[]{:S(2)}) %collective-permute-start.8) | collective-permute-done | bytes 491552 | tf_op jit(solution)/shard_map/ppermute | solution.py:317
  43.3 2.0 %shard_map.149 = (bf16[128,256]{1,0:T(8,128)(2,1)S(1)}, bf16[128,256]{1,0:T(8,128)(2,1)S(1)}, bf16[128,256]{1,0:T(8,128)(2,1)S(1)}, bf16[128,128]{1,0:T(8,128)(2,1)S(1)}, bf16[128,1920]{1,0:T(8,128)(2,1)S(1)}) custom-call(s32[8]{0:T(128)S(1)} %stack.35.where, bf16[128,1920]{1,0:T(8,128)(2,1)S(1)} %collective-permute-done.2.refs_0_.refs_3_, ...), custom_call_target="tpu_custom_call" | custom-call | flops 1000000000 | bytes 1000 | tf_op jit(solution)/shard_map/pallas_call | solution.py:50
  45.4 0.2 collective-permute-start.9
  45.6 1.4 %shard_map.150 = (bf16[128,1920]{1,0:T(8,128)(2,1)S(1)}, bf16[128,1920]{1,0:T(8,128)(2,1)S(1)}) custom-call(s32[8]{0:T(128)S(1)} %stack.35.where, bf16[128,256]{1,0:T(8,128)(2,1)S(1)} %get-tuple-element.104.act.refs_10_, bf16[128,256]{1,0:T(8,128)(2,1)S(1)} %get-tuple-element.105.grad_gate.refs_11_, ...), custom_call_target="tpu_custom_call" | custom-call | bytes 1000 | tf_op jit(solution)/shard_map/pallas_call | solution.py:50
  47.0 0.5 collective-permute-start.14
  47.6 3.1 %collective-permute-start.12 = (bf16[128,1920]{1,0:T(8,128)(2,1)S(1)}, bf16[128,1920]{1,0:T(8,128)(2,1)S(1)}, u32[]{:S(2)}, u32[]{:S(2)}) collective-permute-start(bf16[128,1920]{1,0:T(8,128)(2,1)S(1)} %add_convert_fusion.5), channel_id=1, source_target_pairs={{0,96},{16,48},{32,64},{48,16},{64,32},{80,112},{96,0},{112,80},{1... | collective-permute-start | bytes 1474568 | tf_op jit(solution)/shard_map/ppermute | solution.py:313
  50.7 1.4 %shard_map.152 = (bf16[128,1920]{1,0:T(8,128)(2,1)S(1)}, bf16[128,1920]{1,0:T(8,128)(2,1)S(1)}) custom-call(s32[8]{0:T(128)S(1)} %stack.35.where, bf16[128,256]{1,0:T(8,128)(2,1)S(1)} %get-tuple-element.104.act.refs_10_, bf16[128,256]{1,0:T(8,128)(2,1)S(1)} %get-tuple-element.105.grad_gate.refs_11_, ...), custom_call_target="tpu_custom_call" | custom-call | bytes 1000 | tf_op jit(solution)/shard_map/pallas_call | solution.py:50
  52.2 1.7 %shard_map.151 = (bf16[128,1920]{1,0:T(8,128)(2,1)S(1)}, bf16[128,1920]{1,0:T(8,128)(2,1)S(1)}, bf16[128,1920]{1,0:T(8,128)(2,1)S(1)}) custom-call(s32[8]{0:T(128)S(1)} %stack.35.where, bf16[128,256]{1,0:T(8,128)(2,1)S(1)} %get-tuple-element.104.act.refs_10_, bf16[128,256]{1,0:T(8,128)(2,1)S(1)} %get-tuple-element.105.grad_gate.refs_11_, ...), custom_call_target="tpu_custom_call" | custom-call | bytes 1000 | tf_op jit(solution)/shard_map/pallas_call | solution.py:50
  53.9 1.0 %shard_map.153 = (bf16[128,128]{1,0:T(8,128)(2,1)S(1)}, bf16[3,128,128]{2,1,0:T(8,128)(2,1)S(1)}, s32[8,128]{1,0:T(8,128)S(1)}, f32[8,128]{1,0:T(8,128)S(1)}, f32[1,896]{1,0:T(1,128)S(1)}) custom-call(s32[8,128]{1,0:T(8,128)} %bitcast.26, s32[8,128]{1,0:T(8,128)} %bitcast.28, f32[8,128]{1,0:T(8,128)} %bitcast.30, s32[1,128]{1,0:T(1,128)} %bitcast.32, f32[896]{0:T(1024)} %gain.3), custom_call_target="tpu_custom_call" | custom-call | bytes 1000 | tf_op jit(solution)/shard_map/pallas_call | solution.py:50
  54.9 0.5 collective-permute-start.10
  55.6 0.3 collective-permute-start.15
  55.9 1.8 %collective-permute-done.12 = bf16[128,1920]{1,0:T(8,128)(2,1)S(1)} collective-permute-done((bf16[128,1920]{1,0:T(8,128)(2,1)S(1)}, bf16[128,1920]{1,0:T(8,128)(2,1)S(1)}, u32[]{:S(2)}, u32[]{:S(2)}) %collective-permute-start.12) | collective-permute-done | bytes 491552 | tf_op jit(solution)/shard_map/ppermute | solution.py:313
  57.9 0.3 collective-permute-start.13
  58.2 7.3 %shard_map.154 = (bf16[1,7168,256]{2,1,0:T(8,128)(2,1)}, bf16[1,7168,256]{2,1,0:T(8,128)(2,1)}, bf16[1,256,7168]{2,1,0:T(8,128)(2,1)}) custom-call(s32[8]{0:T(128)S(1)} %stack.35.where, bf16[128,1920]{1,0:T(8,128)(2,1)} %bitcast.21, bf16[128,1920]{1,0:T(8,128)(2,1)} %copy-done.4, bf16[128,1920]{1,0:T(8,128)(2,1)} %copy-done.5, bf16[128,1920]{1,0:T(8,128)(2,1)} %copy-done.10, ...), custom_call_target="tpu_custom_call" | custom-call | flops 2818572288 | bytes 22000000 | tf_op jit(solution)/shard_map/pallas_call | solution.py:50
  65.5 5.1 %collective-permute-done.15 = bf16[128,1920]{1,0:T(8,128)(2,1)S(1)} collective-permute-done((bf16[128,1920]{1,0:T(8,128)(2,1)S(1)}, bf16[128,1920]{1,0:T(8,128)(2,1)S(1)}, u32[]{:S(2)}, u32[]{:S(2)}) %collective-permute-start.15) | collective-permute-done | bytes 491552 | tf_op jit(solution)/shard_map/ppermute | solution.py:313
  70.6 0.2 add_convert_fusion
  70.9 14.4 %all_to_all.11 = bf16[16,8,1920]{2,1,0:T(8,128)(2,1)S(1)} all-to-all(bf16[16,8,1920]{2,1,0:T(8,128)(2,1)S(1)} %bitcast.24), channel_id=1, replica_groups=mesh['y'=4,'core'=2,'x'=4,'z'=4] {'x','z'}, dimensions={0} | all-to-all | bytes 983040 | tf_op jit(solution)/shard_map/all_to_all | solution.py:337
  85.2 1.2 %shard_map.155 = (bf16[128,896]{1,0:T(8,128)(2,1)}, bf16[128,896]{1,0:T(8,128)(2,1)}, f32[8,128]{1,0:T(8,128)}) custom-call(bf16[128,1920]{1,0:T(8,128)(2,1)S(1)} %bitcast.22, bf16[128,896]{1,0:T(8,128)(2,1)S(1)} %get-tuple-element.130.hidden, bf16[128,128]{1,0:T(8,128)(2,1)S(1)} %get-tuple-element.131.select, ...), custom_call_target="tpu_custom_call" | custom-call | bytes 1000 | tf_op jit(solution)/shard_map/pallas_call | solution.py:50
  (52 shorter events, 1.2 us)
Async XLA Ops:
  21.1 4.9 %copy-start.3 = (bf16[16,8,1920]{2,1,0:T(8,128)(2,1)}, bf16[16,8,1920]{2,1,0:T(8,128)(2,1)S(1)}, u32[]{:S(2)}) copy-start(bf16[16,8,1920]{2,1,0:T(8,128)(2,1)S(1)} %all_to_all.10) | copy-start | bytes 1474564
  21.1 1.9 %collective-permute-start.1 = (bf16[128,1920]{1,0:T(8,128)(2,1)S(1)}, bf16[128,1920]{1,0:T(8,128)(2,1)S(1)}, u32[]{:S(2)}, u32[]{:S(2)}) collective-permute-start(bf16[128,1920]{1,0:T(8,128)(2,1)S(1)} %bitcast.17), channel_id=1, source_target_pairs={{0,16},{16,0},{1,17},{17,1},{2,18},{18,2},{3,19},{19,3},{4,20},{20... | collective-permute-start | bytes 1474568 | tf_op jit(solution)/shard_map/ppermute | solution.py:317
  21.2 8.9 %collective-permute-start = (bf16[128,1920]{1,0:T(8,128)(2,1)S(1)}, bf16[128,1920]{1,0:T(8,128)(2,1)S(1)}, u32[]{:S(2)}, u32[]{:S(2)}) collective-permute-start(bf16[128,1920]{1,0:T(8,128)(2,1)S(1)} %bitcast.18), channel_id=1, source_target_pairs={{0,32},{16,112},{32,0},{48,80},{64,96},{80,48},{96,64},{112,16},{1... | collective-permute-start | bytes 1474568 | tf_op jit(solution)/shard_map/ppermute | solution.py:313
  23.0 3.0 %copy-start.9 = (bf16[128,1920]{1,0:T(8,128)(2,1)}, bf16[128,1920]{1,0:T(8,128)(2,1)S(1)}, u32[]{:S(2)}) copy-start(bf16[128,1920]{1,0:T(8,128)(2,1)S(1)} %collective-permute-done.1.sibling.refs_4_) | copy-start | bytes 1474564
  26.0 11.5 %collective-permute-start.5 = (bf16[128,1920]{1,0:T(8,128)(2,1)S(1)}, bf16[128,1920]{1,0:T(8,128)(2,1)S(1)}, u32[]{:S(2)}, u32[]{:S(2)}) collective-permute-start(bf16[128,1920]{1,0:T(8,128)(2,1)S(1)} %bitcast.20), channel_id=1, source_target_pairs={{0,96},{16,48},{32,64},{48,16},{64,32},{80,112},{96,0},{112,80},{1... | collective-permute-start | bytes 1474568 | tf_op jit(solution)/shard_map/ppermute | solution.py:313
  30.1 7.4 %copy-start.4 = (bf16[128,1920]{1,0:T(8,128)(2,1)}, bf16[128,1920]{1,0:T(8,128)(2,1)S(1)}, u32[]{:S(2)}) copy-start(bf16[128,1920]{1,0:T(8,128)(2,1)S(1)} %collective-permute-done.own.refs_1_) | copy-start | bytes 1474564
  30.1 11.3 %collective-permute-start.2 = (bf16[128,1920]{1,0:T(8,128)(2,1)S(1)}, bf16[128,1920]{1,0:T(8,128)(2,1)S(1)}, u32[]{:S(2)}, u32[]{:S(2)}) collective-permute-start(bf16[128,1920]{1,0:T(8,128)(2,1)S(1)} %collective-permute-done.own.refs_1_), channel_id=1, source_target_pairs={{0,96},{16,48},{32,64},{48,16},{64,32},{80,112},{96,0},{112,80},{1... | collective-permute-start | bytes 1474568 | tf_op jit(solution)/shard_map/ppermute | solution.py:313
  34.1 4.1 %collective-permute-start.3 = (bf16[64,1920]{1,0:T(8,128)(2,1)S(1)}, bf16[64,1920]{1,0:T(8,128)(2,1)S(1)}, u32[]{:S(2)}, u32[]{:S(2)}) collective-permute-start(bf16[64,1920]{1,0:T(8,128)(2,1)S(1)} %get-tuple-element.145), channel_id=1, source_target_pairs={{0,16},{16,0},{1,17},{17,1},{2,18},{18,2},{3,19},{19,3},{4,20},{20... | collective-permute-start | bytes 737288 | tf_op jit(solution)/shard_map/ppermute | solution.py:317
  34.2 5.3 %copy-start = (bf16[1,7168,256]{2,1,0:T(8,128)(2,1)S(1)}, bf16[1,7168,256]{2,1,0:T(8,128)(2,1)}, u32[]{:S(2)}) copy-start(bf16[1,7168,256]{2,1,0:T(8,128)(2,1)} %w_gate.9) | copy-start | bytes 11010052
  34.2 5.3 %copy-start.1 = (bf16[1,7168,256]{2,1,0:T(8,128)(2,1)S(1)}, bf16[1,7168,256]{2,1,0:T(8,128)(2,1)}, u32[]{:S(2)}) copy-start(bf16[1,7168,256]{2,1,0:T(8,128)(2,1)} %w_up.9) | copy-start | bytes 11010052
  34.2 5.3 %copy-start.2 = (bf16[1,256,7168]{2,1,0:T(8,128)(2,1)S(1)}, bf16[1,256,7168]{2,1,0:T(8,128)(2,1)}, u32[]{:S(2)}) copy-start(bf16[1,256,7168]{2,1,0:T(8,128)(2,1)} %w_down.9) | copy-start | bytes 11010052
  34.2 3.9 %collective-permute-start.4 = (bf16[64,1920]{1,0:T(8,128)(2,1)S(1)}, bf16[64,1920]{1,0:T(8,128)(2,1)S(1)}, u32[]{:S(2)}, u32[]{:S(2)}) collective-permute-start(bf16[64,1920]{1,0:T(8,128)(2,1)S(1)} %get-tuple-element.144), channel_id=1, source_target_pairs={{0,16},{16,0},{1,17},{17,1},{2,18},{18,2},{3,19},{19,3},{4,20},{20... | collective-permute-start | bytes 737288 | tf_op jit(solution)/shard_map/ppermute | solution.py:317
  37.5 3.6 %copy-start.5 = (bf16[128,1920]{1,0:T(8,128)(2,1)}, bf16[128,1920]{1,0:T(8,128)(2,1)S(1)}, u32[]{:S(2)}) copy-start(bf16[128,1920]{1,0:T(8,128)(2,1)S(1)} %collective-permute-done.5.second.refs_2_) | copy-start | bytes 1474564
  37.6 1.6 %collective-permute-start.6 = (bf16[64,1920]{1,0:T(8,128)(2,1)S(1)}, bf16[64,1920]{1,0:T(8,128)(2,1)S(1)}, u32[]{:S(2)}, u32[]{:S(2)}) collective-permute-start(bf16[64,1920]{1,0:T(8,128)(2,1)S(1)} %get-tuple-element.143), channel_id=1, source_target_pairs={{0,16},{16,0},{1,17},{17,1},{2,18},{18,2},{3,19},{19,3},{4,20},{20... | collective-permute-start | bytes 737288 | tf_op jit(solution)/shard_map/ppermute | solution.py:317
  37.7 1.9 %collective-permute-start.7 = (bf16[64,1920]{1,0:T(8,128)(2,1)S(1)}, bf16[64,1920]{1,0:T(8,128)(2,1)S(1)}, u32[]{:S(2)}, u32[]{:S(2)}) collective-permute-start(bf16[64,1920]{1,0:T(8,128)(2,1)S(1)} %get-tuple-element.142), channel_id=1, source_target_pairs={{0,16},{16,0},{1,17},{17,1},{2,18},{18,2},{3,19},{19,3},{4,20},{20... | collective-permute-start | bytes 737288 | tf_op jit(solution)/shard_map/ppermute | solution.py:317
  38.2 2.9 %copy-start.12 = (bf16[64,1920]{1,0:T(8,128)(2,1)}, bf16[64,1920]{1,0:T(8,128)(2,1)S(1)}, u32[]{:S(2)}) copy-start(bf16[64,1920]{1,0:T(8,128)(2,1)S(1)} %collective-permute-done.3.first_low.refs_5_) | copy-start | bytes 737284
  38.2 2.9 %copy-start.13 = (bf16[64,1920]{1,0:T(8,128)(2,1)}, bf16[64,1920]{1,0:T(8,128)(2,1)S(1)}, u32[]{:S(2)}) copy-start(bf16[64,1920]{1,0:T(8,128)(2,1)S(1)} %collective-permute-done.4.first_high.refs_6_) | copy-start | bytes 737284
  39.2 1.9 %copy-start.14 = (bf16[64,1920]{1,0:T(8,128)(2,1)}, bf16[64,1920]{1,0:T(8,128)(2,1)S(1)}, u32[]{:S(2)}) copy-start(bf16[64,1920]{1,0:T(8,128)(2,1)S(1)} %collective-permute-done.6.second_low.refs_7_) | copy-start | bytes 737284
  39.5 1.6 %copy-start.15 = (bf16[64,1920]{1,0:T(8,128)(2,1)}, bf16[64,1920]{1,0:T(8,128)(2,1)S(1)}, u32[]{:S(2)}) copy-start(bf16[64,1920]{1,0:T(8,128)(2,1)S(1)} %collective-permute-done.7.second_high.refs_8_) | copy-start | bytes 737284
  41.4 3.9 %copy-start.10 = (bf16[128,1920]{1,0:T(8,128)(2,1)}, bf16[128,1920]{1,0:T(8,128)(2,1)S(1)}, u32[]{:S(2)}) copy-start(bf16[128,1920]{1,0:T(8,128)(2,1)S(1)} %collective-permute-done.2.refs_0_.refs_3_) | copy-start | bytes 1474564
  41.4 1.9 %collective-permute-start.8 = (bf16[128,1920]{1,0:T(8,128)(2,1)S(1)}, bf16[128,1920]{1,0:T(8,128)(2,1)S(1)}, u32[]{:S(2)}, u32[]{:S(2)}) collective-permute-start(bf16[128,1920]{1,0:T(8,128)(2,1)S(1)} %collective-permute-done.2.refs_0_.refs_3_), channel_id=1, source_target_pairs={{0,16},{16,0},{1,17},{17,1},{2,18},{18,2},{3,19},{19,3},{4,20},{20... | collective-permute-start | bytes 1474568 | tf_op jit(solution)/shard_map/ppermute | solution.py:317
  43.3 2.0 %copy-start.11 = (bf16[128,1920]{1,0:T(8,128)(2,1)}, bf16[128,1920]{1,0:T(8,128)(2,1)S(1)}, u32[]{:S(2)}) copy-start(bf16[128,1920]{1,0:T(8,128)(2,1)S(1)} %collective-permute-done.8.refs_1_.refs_9_) | copy-start | bytes 1474564
  45.3 6.8 %copy-start.6 = (bf16[128,256]{1,0:T(8,128)(2,1)}, bf16[128,256]{1,0:T(8,128)(2,1)S(1)}, u32[]{:S(2)}) copy-start(bf16[128,256]{1,0:T(8,128)(2,1)S(1)} %get-tuple-element.104.act.refs_10_) | copy-start | bytes 196612
  45.3 6.8 %copy-start.7 = (bf16[128,256]{1,0:T(8,128)(2,1)}, bf16[128,256]{1,0:T(8,128)(2,1)S(1)}, u32[]{:S(2)}) copy-start(bf16[128,256]{1,0:T(8,128)(2,1)S(1)} %get-tuple-element.105.grad_gate.refs_11_) | copy-start | bytes 196612
  45.3 6.8 %copy-start.8 = (bf16[128,256]{1,0:T(8,128)(2,1)}, bf16[128,256]{1,0:T(8,128)(2,1)S(1)}, u32[]{:S(2)}) copy-start(bf16[128,256]{1,0:T(8,128)(2,1)S(1)} %get-tuple-element.106.grad_up.refs_12_) | copy-start | bytes 196612
  45.4 2.1 %collective-permute-start.9 = (bf16[128,1920]{1,0:T(8,128)(2,1)S(1)}, bf16[128,1920]{1,0:T(8,128)(2,1)S(1)}, u32[]{:S(2)}, u32[]{:S(2)}) collective-permute-start(bf16[128,1920]{1,0:T(8,128)(2,1)S(1)} %get-tuple-element.109), channel_id=1, source_target_pairs={{0,16},{16,0},{1,17},{17,1},{2,18},{18,2},{3,19},{19,3},{4,20},{20... | collective-permute-start | bytes 1474568 | tf_op jit(solution)/shard_map/ppermute | solution.py:317
  47.0 8.5 %collective-permute-start.14 = (bf16[128,1920]{1,0:T(8,128)(2,1)S(1)}, bf16[128,1920]{1,0:T(8,128)(2,1)S(1)}, u32[]{:S(2)}, u32[]{:S(2)}) collective-permute-start(bf16[128,1920]{1,0:T(8,128)(2,1)S(1)} %get-tuple-element.125), channel_id=1, source_target_pairs={{0,16},{16,0},{1,17},{17,1},{2,18},{18,2},{3,19},{19,3},{4,20},{20... | collective-permute-start | bytes 1474568 | tf_op jit(solution)/shard_map/ppermute | solution.py:317
  47.6 10.1 %collective-permute-start.12 = (bf16[128,1920]{1,0:T(8,128)(2,1)S(1)}, bf16[128,1920]{1,0:T(8,128)(2,1)S(1)}, u32[]{:S(2)}, u32[]{:S(2)}) collective-permute-start(bf16[128,1920]{1,0:T(8,128)(2,1)S(1)} %add_convert_fusion.5), channel_id=1, source_target_pairs={{0,96},{16,48},{32,64},{48,16},{64,32},{80,112},{96,0},{112,80},{1... | collective-permute-start | bytes 1474568 | tf_op jit(solution)/shard_map/ppermute | solution.py:313
  52.1 5.6 %collective-permute-start.11 = (bf16[128,1920]{1,0:T(8,128)(2,1)S(1)}, bf16[128,1920]{1,0:T(8,128)(2,1)S(1)}, u32[]{:S(2)}, u32[]{:S(2)}) collective-permute-start(bf16[128,1920]{1,0:T(8,128)(2,1)S(1)} %get-tuple-element.114), channel_id=1, source_target_pairs={{0,16},{16,0},{1,17},{17,1},{2,18},{18,2},{3,19},{19,3},{4,20},{20... | collective-permute-start | bytes 1474568 | tf_op jit(solution)/shard_map/ppermute | solution.py:317
  54.9 10.6 %collective-permute-start.10 = (bf16[128,1920]{1,0:T(8,128)(2,1)S(1)}, bf16[128,1920]{1,0:T(8,128)(2,1)S(1)}, u32[]{:S(2)}, u32[]{:S(2)}) collective-permute-start(bf16[128,1920]{1,0:T(8,128)(2,1)S(1)} %get-tuple-element.112), channel_id=1, source_target_pairs={{0,16},{16,0},{1,17},{17,1},{2,18},{18,2},{3,19},{19,3},{4,20},{20... | collective-permute-start | bytes 1474568 | tf_op jit(solution)/shard_map/ppermute | solution.py:317
  55.6 15.1 %collective-permute-start.15 = (bf16[128,1920]{1,0:T(8,128)(2,1)S(1)}, bf16[128,1920]{1,0:T(8,128)(2,1)S(1)}, u32[]{:S(2)}, u32[]{:S(2)}) collective-permute-start(bf16[128,1920]{1,0:T(8,128)(2,1)S(1)} %add_convert_fusion.1), channel_id=1, source_target_pairs={{0,96},{16,48},{32,64},{48,16},{64,32},{80,112},{96,0},{112,80},{1... | collective-permute-start | bytes 1474568 | tf_op jit(solution)/shard_map/ppermute | solution.py:313
  57.9 12.7 %collective-permute-start.13 = (bf16[128,1920]{1,0:T(8,128)(2,1)S(1)}, bf16[128,1920]{1,0:T(8,128)(2,1)S(1)}, u32[]{:S(2)}, u32[]{:S(2)}) collective-permute-start(bf16[128,1920]{1,0:T(8,128)(2,1)S(1)} %add_convert_fusion.2), channel_id=1, source_target_pairs={{0,32},{16,112},{32,0},{48,80},{64,96},{80,48},{96,64},{112,16},{1... | collective-permute-start | bytes 1474568 | tf_op jit(solution)/shard_map/ppermute | solution.py:313

commit v7 on v6

--- a/solution.py
+++ b/solution.py
@@ -96,19 +96,26 @@
     return mix
 
 
-def prepare(hidden, gain, source, ids, slots, gates, cotangent, rows, kept):
+def prepare(hidden, gain, source, ids, slots, gates, cotangent, rows, kept, held_cotangent, sems):
+    loads = [
+        pltpu.make_async_copy(hidden, kept, sems.at[0]),
+        pltpu.make_async_copy(cotangent, held_cotangent, sems.at[1]),
+    ]
+    for load in loads:
+        load.start()
     _, matches = slot_matches(ids[...], slots[...])
     pick, select = pick_rows(matches, source[...] & (ROWS - 1))
     gate = jnp.sum(mix_of(matches, gates[...]), axis=1, keepdims=True)
-    beam = nn(select, hidden[...])
+    loads[0].wait()
+    beam = nn(select, kept[...])
     rows[:, :FEAT] = (beam * gain[...][None, :]).astype(bf16)
     square = jnp.sum(beam * beam, axis=1, keepdims=True) * (1.0 / D)
     high, low = split_two(square)
     lane = lax.broadcasted_iota(jnp.int32, (ROWS, WIDE - FEAT), 1)
     tail = jnp.where(lane == 0, high.astype(f32), jnp.where(lane == 1, low.astype(f32), 0.0))
     rows[:, FEAT:WIDE] = tail.astype(bf16)
-    rows[:, WIDE:] = (nn(pick, cotangent[...]) * gate).astype(bf16)
-    kept[...] = hidden[...]
+    loads[1].wait()
+    rows[:, WIDE:] = (nn(pick, held_cotangent[...]) * gate).astype(bf16)
 
 
 def heads_here():
@@ -317,11 +324,10 @@
     return lax.ppermute(values, "core", [(0, 1), (1, 0)])
 
 
-def sent_home(sums, beside):
+def sent_home(sums, later):
     mine, first, second, across = sums
-    passing, beside = lax.optimization_barrier((to_place(across, 2), beside))
-    first = joined(first, passing)
-    return joined(mine, to_place(first, 1), to_place(second, 2)), beside
+    first, later = lax.optimization_barrier((joined(first, to_place(across, 2)), later))
+    return joined(mine, to_place(first, 1), to_place(second, 2)), later
 
 
 def joined(*parts):
@@ -346,10 +352,11 @@
     ids, slots, gates = route_ids.T, route_slots.T, route_gates.T
     rows, kept = local_call(
         prepare,
-        fetched(hidden, gain, source, ids, slots, gates, out_grad),
+        [(HBM, hidden), *fetched(gain, source, ids, slots, gates), (HBM, out_grad)],
         [(VMEM, (ROWS, WIDE + FEAT), bf16), (VMEM, (ROWS, FEAT), bf16)],
         8,
         (0, 1000),
+        scratch=(pltpu.VMEM((ROWS, FEAT), bf16), pltpu.SemaphoreType.DMA((2,))),
     )
     sent = exchange(rows)
     weights = [(HBM, w_gate), (HBM, w_up), (HBM, w_down)]
@@ -421,7 +428,7 @@
     theirs = [to_sibling(value) for value in (*other, second_other)]
     blocks = [(HBM, block) for block in (*near, across, *near_sibling, across_sibling)]
     home_sums = [joined(mine, term) for mine, term in zip(own, theirs)] + [across_sum]
-    home_sums[3], late_gates = lax.optimization_barrier((home_sums[3], gates))
+    home_sums, late_gates = sent_home(home_sums, gates)
     tables = local_call(
         route_tables,
         fetched(ids, slots, late_gates, source, gain),
@@ -435,7 +442,6 @@
         4,
         (0, 1000),
     )
-    home_sums, tables = sent_home(home_sums, tables)
     grads = local_call(
         weight_grads,
         [where, *blocks, *fetched(act, d_gate, d_up)],
@@ -451,7 +457,7 @@
             pltpu.SemaphoreType.DMA((8, 3)),
         ),
     )
-    home_sums, *grads = lax.optimization_barrier((home_sums, *grads))
+    home_sums, tables, grads = lax.optimization_barrier((home_sums, tables, grads))
     home = exchange(home_sums)
     moe, grad_hidden, grad_gates = local_call(
         finish,

time: 86.7 us -> 87.4 us (level)
  waiting for transfers between devices: 11.6 us -> 9.79 us
  blocking collectives: 33.3 us -> 34.6 us
    ppermute x6, waiting for transfers between devices: 8.22 us -> 6.38 us  [to_place(): return lax.ppermute(values, ('y', 'core'), pairs)]
    all_to_all x2, blocking collectives: 33.3 us -> 34.6 us  [exchange(): lax.all_to_all(pieces, ('x', 'z'), 0, 0, tiled=True).reshape(ROWS, width)]
where the time goes in v7:
time: 87.4 us; the launch traced here: 86.2 us
  blocking collectives  34.6 us (40%)
  Pallas kernels  25.5 us (29%)
  starting transfers between devices  14.5 us (17%)
  waiting for transfers between devices  9.79 us (11%)
  between operations  0.96 us (1%)
    all_to_all x2, blocking collectives, exchange(): lax.all_to_all(pieces, ('x', 'z'), 0, 0, tiled=True).reshape(ROWS, width)  34.6 us
    pallas_call x11, Pallas kernels, local_call(): pl.pallas_call(kernel, out_shape=out_shape, in_specs=in_specs, out_specs=...  25.5 us
    ppermute x6, starting transfers between devices, to_place(): return lax.ppermute(values, ('y', 'core'), pairs)  12.4 us
    ppermute x6, waiting for transfers between devices, to_place(): return lax.ppermute(values, ('y', 'core'), pairs)  6.38 us
    ppermute x10, waiting for transfers between devices, to_sibling(): return lax.ppermute(values, 'core', [(0, 1), (1, 0)])  3.4 us
    ppermute x10, starting transfers between devices, to_sibling(): return lax.ppermute(values, 'core', [(0, 1), (1, 0)])  2.1 us
  transfers between devices with their start and end apart: 16, of which 8 were waited for; matrix products, arithmetic and copies ran while one was open for 1% of the time, Pallas kernels for 23%

profile of v7, /device:TPU:0, one launch (start us, length us, event | category | flops | bytes accessed | tf_op | source)
XLA Modules:
  0.0 86.2 jit_solution(3163600962572164768)
XLA Ops:
  0.6 2.2 %shard_map.145 = (bf16[128,1920]{1,0:T(8,128)(2,1)S(1)}, bf16[128,896]{1,0:T(8,128)(2,1)S(1)}) custom-call(bf16[128,896]{1,0:T(8,128)(2,1)} %hidden.1, f32[896]{0:T(1024)} %gain.3, s32[1,128]{1,0:T(1,128)} %bitcast.31, s32[8,128]{1,0:T(8,128)} %bitcast.25, s32[8,128]{1,0:T(8,128)} %bitcast.27, f32[8,128]{1,0:T(8,128)} %bitcast.29, bf16[128,896]{1,0:T(8,128)(2,1)} %cotangent.1), custom_call_target="tpu_custom_call" | custom-call | bytes 1000 | tf_op jit(solution)/shard_map/pallas_call | solution.py:50
  2.9 18.9 %all_to_all.10 = bf16[16,8,1920]{2,1,0:T(8,128)(2,1)S(1)} all-to-all(bf16[16,8,1920]{2,1,0:T(8,128)(2,1)S(1)} %bitcast.23), channel_id=1, replica_groups=mesh['y'=4,'core'=2,'x'=4,'z'=4] {'x','z'}, dimensions={0} | all-to-all | bytes 983040 | tf_op jit(solution)/shard_map/all_to_all | solution.py:343
  21.8 1.6 %collective-permute-start = (bf16[128,1920]{1,0:T(8,128)(2,1)S(1)}, bf16[128,1920]{1,0:T(8,128)(2,1)S(1)}, u32[]{:S(2)}, u32[]{:S(2)}) collective-permute-start(bf16[128,1920]{1,0:T(8,128)(2,1)S(1)} %bitcast.18), channel_id=1, source_target_pairs={{0,32},{16,112},{32,0},{48,80},{64,96},{80,48},{96,64},{112,16},{1... | collective-permute-start | bytes 1474568 | tf_op jit(solution)/shard_map/ppermute | solution.py:320
  23.4 0.2 collective-permute-done.1.sibling.refs_4_
  23.6 3.0 %shard_map.146 = (f32[128,256]{1,0:T(8,128)S(1)}, f32[128,256]{1,0:T(8,128)S(1)}, f32[128,256]{1,0:T(8,128)S(1)}, f32[128,128]{1,0:T(8,128)S(1)}) custom-call(s32[8]{0:T(128)S(1)} %stack.35.where, bf16[128,1920]{1,0:T(8,128)(2,1)S(1)} %bitcast.19, bf16[128,1920]{1,0:T(8,128)(2,1)S(1)} %collective-permute-done.1.sibling.refs_4_, ...), custom_call_target="tpu_custom_call" | custom-call | bytes 1000 | tf_op jit(solution)/shard_map/pallas_call | solution.py:50
  26.7 3.1 %collective-permute-start.5 = (bf16[128,1920]{1,0:T(8,128)(2,1)S(1)}, bf16[128,1920]{1,0:T(8,128)(2,1)S(1)}, u32[]{:S(2)}, u32[]{:S(2)}) collective-permute-start(bf16[128,1920]{1,0:T(8,128)(2,1)S(1)} %bitcast.20), channel_id=1, source_target_pairs={{0,96},{16,48},{32,64},{48,16},{64,32},{80,112},{96,0},{112,80},{1... | collective-permute-start | bytes 1474568 | tf_op jit(solution)/shard_map/ppermute | solution.py:320
  29.8 1.0 %collective-permute-done.own.refs_1_ = bf16[128,1920]{1,0:T(8,128)(2,1)S(1)} collective-permute-done((bf16[128,1920]{1,0:T(8,128)(2,1)S(1)}, bf16[128,1920]{1,0:T(8,128)(2,1)S(1)}, u32[]{:S(2)}, u32[]{:S(2)}) %collective-permute-start) | collective-permute-done | bytes 491552 | tf_op jit(solution)/shard_map/ppermute | solution.py:320
  30.7 4.0 %collective-permute-start.2 = (bf16[128,1920]{1,0:T(8,128)(2,1)S(1)}, bf16[128,1920]{1,0:T(8,128)(2,1)S(1)}, u32[]{:S(2)}, u32[]{:S(2)}) collective-permute-start(bf16[128,1920]{1,0:T(8,128)(2,1)S(1)} %collective-permute-done.own.refs_1_), channel_id=1, source_target_pairs={{0,96},{16,48},{32,64},{48,16},{64,32},{80,112},{96,0},{112,80},{1... | collective-permute-start | bytes 1474568 | tf_op jit(solution)/shard_map/ppermute | solution.py:320
  34.9 0.5 collective-permute-start.4
  35.3 2.8 %shard_map.147 = (f32[128,256]{1,0:T(8,128)S(1)}, f32[128,256]{1,0:T(8,128)S(1)}, f32[128,256]{1,0:T(8,128)S(1)}, f32[128,128]{1,0:T(8,128)S(1)}) custom-call(s32[8]{0:T(128)S(1)} %stack.35.where, bf16[128,1920]{1,0:T(8,128)(2,1)S(1)} %collective-permute-done.own.refs_1_, bf16[1,7168,256]{2,1,0:T(8,128)(2,1)} %w_gate.9, bf16[1,7168,256]{2,1,0:T(8,128)(2,1)} %w_up.9, ...), custom_call_target="tpu_custom_call" | custom-call | bytes 1000 | tf_op jit(solution)/shard_map/pallas_call | solution.py:50
  38.3 0.5 collective-permute-start.7
  38.8 1.0 %collective-permute-done.6.second_low.refs_7_ = bf16[64,1920]{1,0:T(8,128)(2,1)S(1)} collective-permute-done((bf16[64,1920]{1,0:T(8,128)(2,1)S(1)}, bf16[64,1920]{1,0:T(8,128)(2,1)S(1)}, u32[]{:S(2)}, u32[]{:S(2)}) %collective-permute-start.6) | collective-permute-done | bytes 245792 | tf_op jit(solution)/shard_map/ppermute | solution.py:324
  39.8 0.3 collective-permute-done.7.second_high.refs_8_
  40.2 1.5 %shard_map.148 = (f32[128,256]{1,0:T(8,128)S(1)}, f32[128,256]{1,0:T(8,128)S(1)}, f32[128,256]{1,0:T(8,128)S(1)}, f32[128,128]{1,0:T(8,128)S(1)}) custom-call(s32[8]{0:T(128)S(1)} %stack.35.where, bf16[64,1920]{1,0:T(8,128)(2,1)S(1)} %collective-permute-done.3.first_low.refs_5_, bf16[64,1920]{1,0:T(8,128)(2,1)S(1)} %collective-permute-done.4.first_high.refs_6_, ...), custom_call_target="tpu_custom_call" | custom-call | flops 1000000000 | bytes 1000 | tf_op jit(solution)/shard_map/pallas_call | solution.py:50
  41.8 0.3 collective-permute-done.2.refs_0_.refs_3_
  42.1 1.9 %collective-permute-done.8.refs_1_.refs_9_ = bf16[128,1920]{1,0:T(8,128)(2,1)S(1)} collective-permute-done((bf16[128,1920]{1,0:T(8,128)(2,1)S(1)}, bf16[128,1920]{1,0:T(8,128)(2,1)S(1)}, u32[]{:S(2)}, u32[]{:S(2)}) %collective-permute-start.8) | collective-permute-done | bytes 491552 | tf_op jit(solution)/shard_map/ppermute | solution.py:324
  43.9 2.0 %shard_map.149 = (bf16[128,256]{1,0:T(8,128)(2,1)S(1)}, bf16[128,256]{1,0:T(8,128)(2,1)S(1)}, bf16[128,256]{1,0:T(8,128)(2,1)S(1)}, bf16[128,128]{1,0:T(8,128)(2,1)S(1)}, bf16[128,1920]{1,0:T(8,128)(2,1)S(1)}) custom-call(s32[8]{0:T(128)S(1)} %stack.35.where, bf16[128,1920]{1,0:T(8,128)(2,1)S(1)} %collective-permute-done.2.refs_0_.refs_3_, ...), custom_call_target="tpu_custom_call" | custom-call | flops 1000000000 | bytes 1000 | tf_op jit(solution)/shard_map/pallas_call | solution.py:50
  46.0 0.2 collective-permute-start.9
  46.2 1.4 %shard_map.150 = (bf16[128,1920]{1,0:T(8,128)(2,1)S(1)}, bf16[128,1920]{1,0:T(8,128)(2,1)S(1)}) custom-call(s32[8]{0:T(128)S(1)} %stack.35.where, bf16[128,256]{1,0:T(8,128)(2,1)S(1)} %get-tuple-element.103.act.refs_10_, bf16[128,256]{1,0:T(8,128)(2,1)S(1)} %get-tuple-element.104.grad_gate.refs_11_, ...), custom_call_target="tpu_custom_call" | custom-call | bytes 1000 | tf_op jit(solution)/shard_map/pallas_call | solution.py:50
  47.6 0.5 collective-permute-start.14
  48.2 1.4 %shard_map.152 = (bf16[128,1920]{1,0:T(8,128)(2,1)S(1)}, bf16[128,1920]{1,0:T(8,128)(2,1)S(1)}) custom-call(s32[8]{0:T(128)S(1)} %stack.35.where, bf16[128,256]{1,0:T(8,128)(2,1)S(1)} %get-tuple-element.103.act.refs_10_, bf16[128,256]{1,0:T(8,128)(2,1)S(1)} %get-tuple-element.104.grad_gate.refs_11_, ...), custom_call_target="tpu_custom_call" | custom-call | bytes 1000 | tf_op jit(solution)/shard_map/pallas_call | solution.py:50
  49.8 3.0 %collective-permute-start.12 = (bf16[128,1920]{1,0:T(8,128)(2,1)S(1)}, bf16[128,1920]{1,0:T(8,128)(2,1)S(1)}, u32[]{:S(2)}, u32[]{:S(2)}) collective-permute-start(bf16[128,1920]{1,0:T(8,128)(2,1)S(1)} %add_convert_fusion.5), channel_id=1, source_target_pairs={{0,96},{16,48},{32,64},{48,16},{64,32},{80,112},{96,0},{112,80},{1... | collective-permute-start | bytes 1474568 | tf_op jit(solution)/shard_map/ppermute | solution.py:320
  52.8 1.7 %shard_map.151 = (bf16[128,1920]{1,0:T(8,128)(2,1)S(1)}, bf16[128,1920]{1,0:T(8,128)(2,1)S(1)}, bf16[128,1920]{1,0:T(8,128)(2,1)S(1)}) custom-call(s32[8]{0:T(128)S(1)} %stack.35.where, bf16[128,256]{1,0:T(8,128)(2,1)S(1)} %get-tuple-element.103.act.refs_10_, bf16[128,256]{1,0:T(8,128)(2,1)S(1)} %get-tuple-element.104.grad_gate.refs_11_, ...), custom_call_target="tpu_custom_call" | custom-call | bytes 1000 | tf_op jit(solution)/shard_map/pallas_call | solution.py:50
  54.8 0.4 collective-permute-start.15
  55.2 4.6 %collective-permute-done.12 = bf16[128,1920]{1,0:T(8,128)(2,1)S(1)} collective-permute-done((bf16[128,1920]{1,0:T(8,128)(2,1)S(1)}, bf16[128,1920]{1,0:T(8,128)(2,1)S(1)}, u32[]{:S(2)}, u32[]{:S(2)}) %collective-permute-start.12) | collective-permute-done | bytes 491552 | tf_op jit(solution)/shard_map/ppermute | solution.py:320
  60.0 0.3 collective-permute-start.13
  60.3 7.3 %shard_map.154 = (bf16[1,7168,256]{2,1,0:T(8,128)(2,1)}, bf16[1,7168,256]{2,1,0:T(8,128)(2,1)}, bf16[1,256,7168]{2,1,0:T(8,128)(2,1)}) custom-call(s32[8]{0:T(128)S(1)} %stack.35.where, bf16[128,1920]{1,0:T(8,128)(2,1)} %bitcast.21, bf16[128,1920]{1,0:T(8,128)(2,1)} %copy-done.4, bf16[128,1920]{1,0:T(8,128)(2,1)} %copy-done.5, bf16[128,1920]{1,0:T(8,128)(2,1)} %copy-done.10, ...), custom_call_target="tpu_custom_call" | custom-call | flops 2818572288 | bytes 22000000 | tf_op jit(solution)/shard_map/pallas_call | solution.py:50
  67.6 1.0 %shard_map.153 = (bf16[128,128]{1,0:T(8,128)(2,1)S(1)}, bf16[3,128,128]{2,1,0:T(8,128)(2,1)S(1)}, s32[8,128]{1,0:T(8,128)S(1)}, f32[8,128]{1,0:T(8,128)S(1)}, f32[1,896]{1,0:T(1,128)S(1)}) custom-call(s32[8,128]{1,0:T(8,128)} %bitcast.26, s32[8,128]{1,0:T(8,128)} %bitcast.28, f32[8,128]{1,0:T(8,128)} %bitcast.30, s32[1,128]{1,0:T(1,128)} %bitcast.32, f32[896]{0:T(1024)} %gain.3), custom_call_target="tpu_custom_call" | custom-call | bytes 1000 | tf_op jit(solution)/shard_map/pallas_call | solution.py:50
  68.6 0.5 collective-permute-done.13
  69.1 0.3 add_convert_fusion
  69.4 15.7 %all_to_all.11 = bf16[16,8,1920]{2,1,0:T(8,128)(2,1)S(1)} all-to-all(bf16[16,8,1920]{2,1,0:T(8,128)(2,1)S(1)} %bitcast.24), channel_id=1, replica_groups=mesh['y'=4,'core'=2,'x'=4,'z'=4] {'x','z'}, dimensions={0} | all-to-all | bytes 983040 | tf_op jit(solution)/shard_map/all_to_all | solution.py:343
  85.1 1.2 %shard_map.155 = (bf16[128,896]{1,0:T(8,128)(2,1)}, bf16[128,896]{1,0:T(8,128)(2,1)}, f32[8,128]{1,0:T(8,128)}) custom-call(bf16[128,1920]{1,0:T(8,128)(2,1)S(1)} %bitcast.22, bf16[128,896]{1,0:T(8,128)(2,1)S(1)} %get-tuple-element.128.hidden, bf16[128,128]{1,0:T(8,128)(2,1)S(1)} %get-tuple-element.129.select, ...), custom_call_target="tpu_custom_call" | custom-call | bytes 1000 | tf_op jit(solution)/shard_map/pallas_call | solution.py:50
  (52 shorter events, 1.2 us)
Async XLA Ops:
  21.8 4.9 %copy-start.3 = (bf16[16,8,1920]{2,1,0:T(8,128)(2,1)}, bf16[16,8,1920]{2,1,0:T(8,128)(2,1)S(1)}, u32[]{:S(2)}) copy-start(bf16[16,8,1920]{2,1,0:T(8,128)(2,1)S(1)} %all_to_all.10) | copy-start | bytes 1474564
  21.8 1.9 %collective-permute-start.1 = (bf16[128,1920]{1,0:T(8,128)(2,1)S(1)}, bf16[128,1920]{1,0:T(8,128)(2,1)S(1)}, u32[]{:S(2)}, u32[]{:S(2)}) collective-permute-start(bf16[128,1920]{1,0:T(8,128)(2,1)S(1)} %bitcast.17), channel_id=1, source_target_pairs={{0,16},{16,0},{1,17},{17,1},{2,18},{18,2},{3,19},{19,3},{4,20},{20... | collective-permute-start | bytes 1474568 | tf_op jit(solution)/shard_map/ppermute | solution.py:324
  21.8 8.9 %collective-permute-start = (bf16[128,1920]{1,0:T(8,128)(2,1)S(1)}, bf16[128,1920]{1,0:T(8,128)(2,1)S(1)}, u32[]{:S(2)}, u32[]{:S(2)}) collective-permute-start(bf16[128,1920]{1,0:T(8,128)(2,1)S(1)} %bitcast.18), channel_id=1, source_target_pairs={{0,32},{16,112},{32,0},{48,80},{64,96},{80,48},{96,64},{112,16},{1... | collective-permute-start | bytes 1474568 | tf_op jit(solution)/shard_map/ppermute | solution.py:320
  23.6 3.0 %copy-start.9 = (bf16[128,1920]{1,0:T(8,128)(2,1)}, bf16[128,1920]{1,0:T(8,128)(2,1)S(1)}, u32[]{:S(2)}) copy-start(bf16[128,1920]{1,0:T(8,128)(2,1)S(1)} %collective-permute-done.1.sibling.refs_4_) | copy-start | bytes 1474564
  26.7 11.5 %collective-permute-start.5 = (bf16[128,1920]{1,0:T(8,128)(2,1)S(1)}, bf16[128,1920]{1,0:T(8,128)(2,1)S(1)}, u32[]{:S(2)}, u32[]{:S(2)}) collective-permute-start(bf16[128,1920]{1,0:T(8,128)(2,1)S(1)} %bitcast.20), channel_id=1, source_target_pairs={{0,96},{16,48},{32,64},{48,16},{64,32},{80,112},{96,0},{112,80},{1... | collective-permute-start | bytes 1474568 | tf_op jit(solution)/shard_map/ppermute | solution.py:320
  30.7 7.4 %copy-start.4 = (bf16[128,1920]{1,0:T(8,128)(2,1)}, bf16[128,1920]{1,0:T(8,128)(2,1)S(1)}, u32[]{:S(2)}) copy-start(bf16[128,1920]{1,0:T(8,128)(2,1)S(1)} %collective-permute-done.own.refs_1_) | copy-start | bytes 1474564
  30.7 11.3 %collective-permute-start.2 = (bf16[128,1920]{1,0:T(8,128)(2,1)S(1)}, bf16[128,1920]{1,0:T(8,128)(2,1)S(1)}, u32[]{:S(2)}, u32[]{:S(2)}) collective-permute-start(bf16[128,1920]{1,0:T(8,128)(2,1)S(1)} %collective-permute-done.own.refs_1_), channel_id=1, source_target_pairs={{0,96},{16,48},{32,64},{48,16},{64,32},{80,112},{96,0},{112,80},{1... | collective-permute-start | bytes 1474568 | tf_op jit(solution)/shard_map/ppermute | solution.py:320
  34.7 4.1 %collective-permute-start.3 = (bf16[64,1920]{1,0:T(8,128)(2,1)S(1)}, bf16[64,1920]{1,0:T(8,128)(2,1)S(1)}, u32[]{:S(2)}, u32[]{:S(2)}) collective-permute-start(bf16[64,1920]{1,0:T(8,128)(2,1)S(1)} %get-tuple-element.143), channel_id=1, source_target_pairs={{0,16},{16,0},{1,17},{17,1},{2,18},{18,2},{3,19},{19,3},{4,20},{20... | collective-permute-start | bytes 737288 | tf_op jit(solution)/shard_map/ppermute | solution.py:324
  34.8 5.3 %copy-start = (bf16[1,7168,256]{2,1,0:T(8,128)(2,1)S(1)}, bf16[1,7168,256]{2,1,0:T(8,128)(2,1)}, u32[]{:S(2)}) copy-start(bf16[1,7168,256]{2,1,0:T(8,128)(2,1)} %w_gate.9) | copy-start | bytes 11010052
  34.8 5.3 %copy-start.1 = (bf16[1,7168,256]{2,1,0:T(8,128)(2,1)S(1)}, bf16[1,7168,256]{2,1,0:T(8,128)(2,1)}, u32[]{:S(2)}) copy-start(bf16[1,7168,256]{2,1,0:T(8,128)(2,1)} %w_up.9) | copy-start | bytes 11010052
  34.9 5.3 %copy-start.2 = (bf16[1,256,7168]{2,1,0:T(8,128)(2,1)S(1)}, bf16[1,256,7168]{2,1,0:T(8,128)(2,1)}, u32[]{:S(2)}) copy-start(bf16[1,256,7168]{2,1,0:T(8,128)(2,1)} %w_down.9) | copy-start | bytes 11010052
  34.9 3.9 %collective-permute-start.4 = (bf16[64,1920]{1,0:T(8,128)(2,1)S(1)}, bf16[64,1920]{1,0:T(8,128)(2,1)S(1)}, u32[]{:S(2)}, u32[]{:S(2)}) collective-permute-start(bf16[64,1920]{1,0:T(8,128)(2,1)S(1)} %get-tuple-element.142), channel_id=1, source_target_pairs={{0,16},{16,0},{1,17},{17,1},{2,18},{18,2},{3,19},{19,3},{4,20},{20... | collective-permute-start | bytes 737288 | tf_op jit(solution)/shard_map/ppermute | solution.py:324
  38.2 3.6 %copy-start.5 = (bf16[128,1920]{1,0:T(8,128)(2,1)}, bf16[128,1920]{1,0:T(8,128)(2,1)S(1)}, u32[]{:S(2)}) copy-start(bf16[128,1920]{1,0:T(8,128)(2,1)S(1)} %collective-permute-done.5.second.refs_2_) | copy-start | bytes 1474564
  38.2 1.6 %collective-permute-start.6 = (bf16[64,1920]{1,0:T(8,128)(2,1)S(1)}, bf16[64,1920]{1,0:T(8,128)(2,1)S(1)}, u32[]{:S(2)}, u32[]{:S(2)}) collective-permute-start(bf16[64,1920]{1,0:T(8,128)(2,1)S(1)} %get-tuple-element.141), channel_id=1, source_target_pairs={{0,16},{16,0},{1,17},{17,1},{2,18},{18,2},{3,19},{19,3},{4,20},{20... | collective-permute-start | bytes 737288 | tf_op jit(solution)/shard_map/ppermute | solution.py:324
  38.3 1.9 %collective-permute-start.7 = (bf16[64,1920]{1,0:T(8,128)(2,1)S(1)}, bf16[64,1920]{1,0:T(8,128)(2,1)S(1)}, u32[]{:S(2)}, u32[]{:S(2)}) collective-permute-start(bf16[64,1920]{1,0:T(8,128)(2,1)S(1)} %get-tuple-element.140), channel_id=1, source_target_pairs={{0,16},{16,0},{1,17},{17,1},{2,18},{18,2},{3,19},{19,3},{4,20},{20... | collective-permute-start | bytes 737288 | tf_op jit(solution)/shard_map/ppermute | solution.py:324
  38.8 2.9 %copy-start.12 = (bf16[64,1920]{1,0:T(8,128)(2,1)}, bf16[64,1920]{1,0:T(8,128)(2,1)S(1)}, u32[]{:S(2)}) copy-start(bf16[64,1920]{1,0:T(8,128)(2,1)S(1)} %collective-permute-done.3.first_low.refs_5_) | copy-start | bytes 737284
  38.8 2.9 %copy-start.13 = (bf16[64,1920]{1,0:T(8,128)(2,1)}, bf16[64,1920]{1,0:T(8,128)(2,1)S(1)}, u32[]{:S(2)}) copy-start(bf16[64,1920]{1,0:T(8,128)(2,1)S(1)} %collective-permute-done.4.first_high.refs_6_) | copy-start | bytes 737284
  39.8 1.9 %copy-start.14 = (bf16[64,1920]{1,0:T(8,128)(2,1)}, bf16[64,1920]{1,0:T(8,128)(2,1)S(1)}, u32[]{:S(2)}) copy-start(bf16[64,1920]{1,0:T(8,128)(2,1)S(1)} %collective-permute-done.6.second_low.refs_7_) | copy-start | bytes 737284
  40.2 1.6 %copy-start.15 = (bf16[64,1920]{1,0:T(8,128)(2,1)}, bf16[64,1920]{1,0:T(8,128)(2,1)S(1)}, u32[]{:S(2)}) copy-start(bf16[64,1920]{1,0:T(8,128)(2,1)S(1)} %collective-permute-done.7.second_high.refs_8_) | copy-start | bytes 737284
  42.0 3.9 %copy-start.10 = (bf16[128,1920]{1,0:T(8,128)(2,1)}, bf16[128,1920]{1,0:T(8,128)(2,1)S(1)}, u32[]{:S(2)}) copy-start(bf16[128,1920]{1,0:T(8,128)(2,1)S(1)} %collective-permute-done.2.refs_0_.refs_3_) | copy-start | bytes 1474564
  42.0 1.9 %collective-permute-start.8 = (bf16[128,1920]{1,0:T(8,128)(2,1)S(1)}, bf16[128,1920]{1,0:T(8,128)(2,1)S(1)}, u32[]{:S(2)}, u32[]{:S(2)}) collective-permute-start(bf16[128,1920]{1,0:T(8,128)(2,1)S(1)} %collective-permute-done.2.refs_0_.refs_3_), channel_id=1, source_target_pairs={{0,16},{16,0},{1,17},{17,1},{2,18},{18,2},{3,19},{19,3},{4,20},{20... | collective-permute-start | bytes 1474568 | tf_op jit(solution)/shard_map/ppermute | solution.py:324
  43.9 2.0 %copy-start.11 = (bf16[128,1920]{1,0:T(8,128)(2,1)}, bf16[128,1920]{1,0:T(8,128)(2,1)S(1)}, u32[]{:S(2)}) copy-start(bf16[128,1920]{1,0:T(8,128)(2,1)S(1)} %collective-permute-done.8.refs_1_.refs_9_) | copy-start | bytes 1474564
  46.0 6.9 %copy-start.6 = (bf16[128,256]{1,0:T(8,128)(2,1)}, bf16[128,256]{1,0:T(8,128)(2,1)S(1)}, u32[]{:S(2)}) copy-start(bf16[128,256]{1,0:T(8,128)(2,1)S(1)} %get-tuple-element.103.act.refs_10_) | copy-start | bytes 196612
  46.0 6.9 %copy-start.7 = (bf16[128,256]{1,0:T(8,128)(2,1)}, bf16[128,256]{1,0:T(8,128)(2,1)S(1)}, u32[]{:S(2)}) copy-start(bf16[128,256]{1,0:T(8,128)(2,1)S(1)} %get-tuple-element.104.grad_gate.refs_11_) | copy-start | bytes 196612
  46.0 6.9 %copy-start.8 = (bf16[128,256]{1,0:T(8,128)(2,1)}, bf16[128,256]{1,0:T(8,128)(2,1)S(1)}, u32[]{:S(2)}) copy-start(bf16[128,256]{1,0:T(8,128)(2,1)S(1)} %get-tuple-element.105.grad_up.refs_12_) | copy-start | bytes 196612
  46.0 2.1 %collective-permute-start.9 = (bf16[128,1920]{1,0:T(8,128)(2,1)S(1)}, bf16[128,1920]{1,0:T(8,128)(2,1)S(1)}, u32[]{:S(2)}, u32[]{:S(2)}) collective-permute-start(bf16[128,1920]{1,0:T(8,128)(2,1)S(1)} %get-tuple-element.108), channel_id=1, source_target_pairs={{0,16},{16,0},{1,17},{17,1},{2,18},{18,2},{3,19},{19,3},{4,20},{20... | collective-permute-start | bytes 1474568 | tf_op jit(solution)/shard_map/ppermute | solution.py:324
  47.6 7.1 %collective-permute-start.14 = (bf16[128,1920]{1,0:T(8,128)(2,1)S(1)}, bf16[128,1920]{1,0:T(8,128)(2,1)S(1)}, u32[]{:S(2)}, u32[]{:S(2)}) collective-permute-start(bf16[128,1920]{1,0:T(8,128)(2,1)S(1)} %get-tuple-element.117), channel_id=1, source_target_pairs={{0,16},{16,0},{1,17},{17,1},{2,18},{18,2},{3,19},{19,3},{4,20},{20... | collective-permute-start | bytes 1474568 | tf_op jit(solution)/shard_map/ppermute | solution.py:324
  49.6 5.6 %collective-permute-start.11 = (bf16[128,1920]{1,0:T(8,128)(2,1)S(1)}, bf16[128,1920]{1,0:T(8,128)(2,1)S(1)}, u32[]{:S(2)}, u32[]{:S(2)}) collective-permute-start(bf16[128,1920]{1,0:T(8,128)(2,1)S(1)} %get-tuple-element.113), channel_id=1, source_target_pairs={{0,16},{16,0},{1,17},{17,1},{2,18},{18,2},{3,19},{19,3},{4,20},{20... | collective-permute-start | bytes 1474568 | tf_op jit(solution)/shard_map/ppermute | solution.py:324
  49.8 10.0 %collective-permute-start.12 = (bf16[128,1920]{1,0:T(8,128)(2,1)S(1)}, bf16[128,1920]{1,0:T(8,128)(2,1)S(1)}, u32[]{:S(2)}, u32[]{:S(2)}) collective-permute-start(bf16[128,1920]{1,0:T(8,128)(2,1)S(1)} %add_convert_fusion.5), channel_id=1, source_target_pairs={{0,96},{16,48},{32,64},{48,16},{64,32},{80,112},{96,0},{112,80},{1... | collective-permute-start | bytes 1474568 | tf_op jit(solution)/shard_map/ppermute | solution.py:320
  54.6 14.0 %collective-permute-start.10 = (bf16[128,1920]{1,0:T(8,128)(2,1)S(1)}, bf16[128,1920]{1,0:T(8,128)(2,1)S(1)}, u32[]{:S(2)}, u32[]{:S(2)}) collective-permute-start(bf16[128,1920]{1,0:T(8,128)(2,1)S(1)} %get-tuple-element.111), channel_id=1, source_target_pairs={{0,16},{16,0},{1,17},{17,1},{2,18},{18,2},{3,19},{19,3},{4,20},{20... | collective-permute-start | bytes 1474568 | tf_op jit(solution)/shard_map/ppermute | solution.py:324
  54.8 13.8 %collective-permute-start.15 = (bf16[128,1920]{1,0:T(8,128)(2,1)S(1)}, bf16[128,1920]{1,0:T(8,128)(2,1)S(1)}, u32[]{:S(2)}, u32[]{:S(2)}) collective-permute-start(bf16[128,1920]{1,0:T(8,128)(2,1)S(1)} %add_convert_fusion.1), channel_id=1, source_target_pairs={{0,96},{16,48},{32,64},{48,16},{64,32},{80,112},{96,0},{112,80},{1... | collective-permute-start | bytes 1474568 | tf_op jit(solution)/shard_map/ppermute | solution.py:320
  60.0 9.1 %collective-permute-start.13 = (bf16[128,1920]{1,0:T(8,128)(2,1)S(1)}, bf16[128,1920]{1,0:T(8,128)(2,1)S(1)}, u32[]{:S(2)}, u32[]{:S(2)}) collective-permute-start(bf16[128,1920]{1,0:T(8,128)(2,1)S(1)} %add_convert_fusion.2), channel_id=1, source_target_pairs={{0,32},{16,112},{32,0},{48,80},{64,96},{80,48},{96,64},{112,16},{1... | collective-permute-start | bytes 1474568 | tf_op jit(solution)/shard_map/ppermute | solution.py:320

commit v8 on v6

--- a/solution.py
+++ b/solution.py
@@ -421,7 +421,7 @@
     theirs = [to_sibling(value) for value in (*other, second_other)]
     blocks = [(HBM, block) for block in (*near, across, *near_sibling, across_sibling)]
     home_sums = [joined(mine, term) for mine, term in zip(own, theirs)] + [across_sum]
-    home_sums[3], late_gates = lax.optimization_barrier((home_sums[3], gates))
+    home_sums[2], late_gates = lax.optimization_barrier((home_sums[2], gates))
     tables = local_call(
         route_tables,
         fetched(ids, slots, late_gates, source, gain),

time: 86.7 us -> 86.8 us (level)
  no operation moved by 1% of the time
where the time goes in v8:
time: 86.8 us; the launch traced here: 86.5 us
  blocking collectives  33.4 us (38%)
  Pallas kernels  24.8 us (29%)
  starting transfers between devices  14.7 us (17%)
  waiting for transfers between devices  11.7 us (13%)
  between operations  0.98 us (1%)
    all_to_all x2, blocking collectives, exchange(): lax.all_to_all(pieces, ('x', 'z'), 0, 0, tiled=True).reshape(ROWS, width)  33.4 us
    pallas_call x11, Pallas kernels, local_call(): pl.pallas_call(kernel, out_shape=out_shape, in_specs=in_specs, out_specs=...  24.8 us
    ppermute x6, starting transfers between devices, to_place(): return lax.ppermute(values, ('y', 'core'), pairs)  12.2 us
    ppermute x6, waiting for transfers between devices, to_place(): return lax.ppermute(values, ('y', 'core'), pairs)  8.32 us
    ppermute x10, waiting for transfers between devices, to_sibling(): return lax.ppermute(values, 'core', [(0, 1), (1, 0)])  3.4 us
    ppermute x10, starting transfers between devices, to_sibling(): return lax.ppermute(values, 'core', [(0, 1), (1, 0)])  2.44 us
  transfers between devices with their start and end apart: 16, of which 8 were waited for; matrix products, arithmetic and copies ran while one was open for 1% of the time, Pallas kernels for 23%

profile of v8, /device:TPU:0, one launch (start us, length us, event | category | flops | bytes accessed | tf_op | source)
XLA Modules:
  0.0 86.5 jit_solution(12547430743600946974)
XLA Ops:
  0.6 1.6 %shard_map.145 = (bf16[128,1920]{1,0:T(8,128)(2,1)S(1)}, bf16[128,896]{1,0:T(8,128)(2,1)S(1)}) custom-call(bf16[128,896]{1,0:T(8,128)(2,1)} %hidden.1, f32[896]{0:T(1024)} %gain.3, s32[1,128]{1,0:T(1,128)} %bitcast.31, s32[8,128]{1,0:T(8,128)} %bitcast.25, s32[8,128]{1,0:T(8,128)} %bitcast.27, f32[8,128]{1,0:T(8,128)} %bitcast.29, bf16[128,896]{1,0:T(8,128)(2,1)} %cotangent.1), custom_call_target="tpu_custom_call" | custom-call | bytes 1000 | tf_op jit(solution)/shard_map/pallas_call | solution.py:50
  2.2 18.9 %all_to_all.10 = bf16[16,8,1920]{2,1,0:T(8,128)(2,1)S(1)} all-to-all(bf16[16,8,1920]{2,1,0:T(8,128)(2,1)S(1)} %bitcast.23), channel_id=1, replica_groups=mesh['y'=4,'core'=2,'x'=4,'z'=4] {'x','z'}, dimensions={0} | all-to-all | bytes 983040 | tf_op jit(solution)/shard_map/all_to_all | solution.py:337
  21.2 1.6 %collective-permute-start = (bf16[128,1920]{1,0:T(8,128)(2,1)S(1)}, bf16[128,1920]{1,0:T(8,128)(2,1)S(1)}, u32[]{:S(2)}, u32[]{:S(2)}) collective-permute-start(bf16[128,1920]{1,0:T(8,128)(2,1)S(1)} %bitcast.18), channel_id=1, source_target_pairs={{0,32},{16,112},{32,0},{48,80},{64,96},{80,48},{96,64},{112,16},{1... | collective-permute-start | bytes 1474568 | tf_op jit(solution)/shard_map/ppermute | solution.py:313
  23.0 3.0 %shard_map.146 = (f32[128,256]{1,0:T(8,128)S(1)}, f32[128,256]{1,0:T(8,128)S(1)}, f32[128,256]{1,0:T(8,128)S(1)}, f32[128,128]{1,0:T(8,128)S(1)}) custom-call(s32[8]{0:T(128)S(1)} %stack.35.where, bf16[128,1920]{1,0:T(8,128)(2,1)S(1)} %bitcast.19, bf16[128,1920]{1,0:T(8,128)(2,1)S(1)} %collective-permute-done.1.sibling.refs_4_, ...), custom_call_target="tpu_custom_call" | custom-call | bytes 1000 | tf_op jit(solution)/shard_map/pallas_call | solution.py:50
  26.0 3.1 %collective-permute-start.5 = (bf16[128,1920]{1,0:T(8,128)(2,1)S(1)}, bf16[128,1920]{1,0:T(8,128)(2,1)S(1)}, u32[]{:S(2)}, u32[]{:S(2)}) collective-permute-start(bf16[128,1920]{1,0:T(8,128)(2,1)S(1)} %bitcast.20), channel_id=1, source_target_pairs={{0,96},{16,48},{32,64},{48,16},{64,32},{80,112},{96,0},{112,80},{1... | collective-permute-start | bytes 1474568 | tf_op jit(solution)/shard_map/ppermute | solution.py:313
  29.1 1.0 %collective-permute-done.own.refs_1_ = bf16[128,1920]{1,0:T(8,128)(2,1)S(1)} collective-permute-done((bf16[128,1920]{1,0:T(8,128)(2,1)S(1)}, bf16[128,1920]{1,0:T(8,128)(2,1)S(1)}, u32[]{:S(2)}, u32[]{:S(2)}) %collective-permute-start) | collective-permute-done | bytes 491552 | tf_op jit(solution)/shard_map/ppermute | solution.py:313
  30.1 4.0 %collective-permute-start.2 = (bf16[128,1920]{1,0:T(8,128)(2,1)S(1)}, bf16[128,1920]{1,0:T(8,128)(2,1)S(1)}, u32[]{:S(2)}, u32[]{:S(2)}) collective-permute-start(bf16[128,1920]{1,0:T(8,128)(2,1)S(1)} %collective-permute-done.own.refs_1_), channel_id=1, source_target_pairs={{0,96},{16,48},{32,64},{48,16},{64,32},{80,112},{96,0},{112,80},{1... | collective-permute-start | bytes 1474568 | tf_op jit(solution)/shard_map/ppermute | solution.py:313
  34.2 0.5 collective-permute-start.4
  34.7 2.8 %shard_map.147 = (f32[128,256]{1,0:T(8,128)S(1)}, f32[128,256]{1,0:T(8,128)S(1)}, f32[128,256]{1,0:T(8,128)S(1)}, f32[128,128]{1,0:T(8,128)S(1)}) custom-call(s32[8]{0:T(128)S(1)} %stack.35.where, bf16[128,1920]{1,0:T(8,128)(2,1)S(1)} %collective-permute-done.own.refs_1_, bf16[1,7168,256]{2,1,0:T(8,128)(2,1)} %w_gate.9, bf16[1,7168,256]{2,1,0:T(8,128)(2,1)} %w_up.9, ...), custom_call_target="tpu_custom_call" | custom-call | bytes 1000 | tf_op jit(solution)/shard_map/pallas_call | solution.py:50
  37.7 0.5 collective-permute-start.7
  38.2 1.0 %collective-permute-done.6.second_low.refs_7_ = bf16[64,1920]{1,0:T(8,128)(2,1)S(1)} collective-permute-done((bf16[64,1920]{1,0:T(8,128)(2,1)S(1)}, bf16[64,1920]{1,0:T(8,128)(2,1)S(1)}, u32[]{:S(2)}, u32[]{:S(2)}) %collective-permute-start.6) | collective-permute-done | bytes 245792 | tf_op jit(solution)/shard_map/ppermute | solution.py:317
  39.2 0.3 collective-permute-done.7.second_high.refs_8_
  39.6 1.5 %shard_map.148 = (f32[128,256]{1,0:T(8,128)S(1)}, f32[128,256]{1,0:T(8,128)S(1)}, f32[128,256]{1,0:T(8,128)S(1)}, f32[128,128]{1,0:T(8,128)S(1)}) custom-call(s32[8]{0:T(128)S(1)} %stack.35.where, bf16[64,1920]{1,0:T(8,128)(2,1)S(1)} %collective-permute-done.3.first_low.refs_5_, bf16[64,1920]{1,0:T(8,128)(2,1)S(1)} %collective-permute-done.4.first_high.refs_6_, ...), custom_call_target="tpu_custom_call" | custom-call | flops 1000000000 | bytes 1000 | tf_op jit(solution)/shard_map/pallas_call | solution.py:50
  41.1 0.3 collective-permute-done.2.refs_0_.refs_3_
  41.4 1.9 %collective-permute-done.8.refs_1_.refs_9_ = bf16[128,1920]{1,0:T(8,128)(2,1)S(1)} collective-permute-done((bf16[128,1920]{1,0:T(8,128)(2,1)S(1)}, bf16[128,1920]{1,0:T(8,128)(2,1)S(1)}, u32[]{:S(2)}, u32[]{:S(2)}) %collective-permute-start.8) | collective-permute-done | bytes 491552 | tf_op jit(solution)/shard_map/ppermute | solution.py:317
  43.3 2.0 %shard_map.149 = (bf16[128,256]{1,0:T(8,128)(2,1)S(1)}, bf16[128,256]{1,0:T(8,128)(2,1)S(1)}, bf16[128,256]{1,0:T(8,128)(2,1)S(1)}, bf16[128,128]{1,0:T(8,128)(2,1)S(1)}, bf16[128,1920]{1,0:T(8,128)(2,1)S(1)}) custom-call(s32[8]{0:T(128)S(1)} %stack.35.where, bf16[128,1920]{1,0:T(8,128)(2,1)S(1)} %collective-permute-done.2.refs_0_.refs_3_, ...), custom_call_target="tpu_custom_call" | custom-call | flops 1000000000 | bytes 1000 | tf_op jit(solution)/shard_map/pallas_call | solution.py:50
  45.4 0.2 collective-permute-start.9
  45.6 1.4 %shard_map.150 = (bf16[128,1920]{1,0:T(8,128)(2,1)S(1)}, bf16[128,1920]{1,0:T(8,128)(2,1)S(1)}) custom-call(s32[8]{0:T(128)S(1)} %stack.35.where, bf16[128,256]{1,0:T(8,128)(2,1)S(1)} %get-tuple-element.104.act.refs_10_, bf16[128,256]{1,0:T(8,128)(2,1)S(1)} %get-tuple-element.105.grad_gate.refs_11_, ...), custom_call_target="tpu_custom_call" | custom-call | bytes 1000 | tf_op jit(solution)/shard_map/pallas_call | solution.py:50
  47.0 0.5 collective-permute-start.13
  47.5 3.1 %collective-permute-start.12 = (bf16[128,1920]{1,0:T(8,128)(2,1)S(1)}, bf16[128,1920]{1,0:T(8,128)(2,1)S(1)}, u32[]{:S(2)}, u32[]{:S(2)}) collective-permute-start(bf16[128,1920]{1,0:T(8,128)(2,1)S(1)} %add_convert_fusion.5), channel_id=1, source_target_pairs={{0,96},{16,48},{32,64},{48,16},{64,32},{80,112},{96,0},{112,80},{1... | collective-permute-start | bytes 1474568 | tf_op jit(solution)/shard_map/ppermute | solution.py:313
  50.6 1.4 %shard_map.152 = (bf16[128,1920]{1,0:T(8,128)(2,1)S(1)}, bf16[128,1920]{1,0:T(8,128)(2,1)S(1)}) custom-call(s32[8]{0:T(128)S(1)} %stack.35.where, bf16[128,256]{1,0:T(8,128)(2,1)S(1)} %get-tuple-element.104.act.refs_10_, bf16[128,256]{1,0:T(8,128)(2,1)S(1)} %get-tuple-element.105.grad_gate.refs_11_, ...), custom_call_target="tpu_custom_call" | custom-call | bytes 1000 | tf_op jit(solution)/shard_map/pallas_call | solution.py:50
  52.2 1.7 %shard_map.151 = (bf16[128,1920]{1,0:T(8,128)(2,1)S(1)}, bf16[128,1920]{1,0:T(8,128)(2,1)S(1)}, bf16[128,1920]{1,0:T(8,128)(2,1)S(1)}) custom-call(s32[8]{0:T(128)S(1)} %stack.35.where, bf16[128,256]{1,0:T(8,128)(2,1)S(1)} %get-tuple-element.104.act.refs_10_, bf16[128,256]{1,0:T(8,128)(2,1)S(1)} %get-tuple-element.105.grad_gate.refs_11_, ...), custom_call_target="tpu_custom_call" | custom-call | bytes 1000 | tf_op jit(solution)/shard_map/pallas_call | solution.py:50
  54.0 1.0 %shard_map.153 = (bf16[128,128]{1,0:T(8,128)(2,1)S(1)}, bf16[3,128,128]{2,1,0:T(8,128)(2,1)S(1)}, s32[8,128]{1,0:T(8,128)S(1)}, f32[8,128]{1,0:T(8,128)S(1)}, f32[1,896]{1,0:T(1,128)S(1)}) custom-call(s32[8,128]{1,0:T(8,128)} %bitcast.26, s32[8,128]{1,0:T(8,128)} %bitcast.28, f32[8,128]{1,0:T(8,128)} %bitcast.30, s32[1,128]{1,0:T(1,128)} %bitcast.32, f32[896]{0:T(1024)} %gain.3), custom_call_target="tpu_custom_call" | custom-call | bytes 1000 | tf_op jit(solution)/shard_map/pallas_call | solution.py:50
  55.0 0.5 collective-permute-start.10
  55.5 0.2 collective-permute-start.15
  55.7 1.9 %collective-permute-done.12 = bf16[128,1920]{1,0:T(8,128)(2,1)S(1)} collective-permute-done((bf16[128,1920]{1,0:T(8,128)(2,1)S(1)}, bf16[128,1920]{1,0:T(8,128)(2,1)S(1)}, u32[]{:S(2)}, u32[]{:S(2)}) %collective-permute-start.12) | collective-permute-done | bytes 491552 | tf_op jit(solution)/shard_map/ppermute | solution.py:313
  57.8 0.3 collective-permute-start.14
  58.1 7.3 %shard_map.154 = (bf16[1,7168,256]{2,1,0:T(8,128)(2,1)}, bf16[1,7168,256]{2,1,0:T(8,128)(2,1)}, bf16[1,256,7168]{2,1,0:T(8,128)(2,1)}) custom-call(s32[8]{0:T(128)S(1)} %stack.35.where, bf16[128,1920]{1,0:T(8,128)(2,1)} %bitcast.21, bf16[128,1920]{1,0:T(8,128)(2,1)} %copy-done.4, bf16[128,1920]{1,0:T(8,128)(2,1)} %copy-done.5, bf16[128,1920]{1,0:T(8,128)(2,1)} %copy-done.10, ...), custom_call_target="tpu_custom_call" | custom-call | flops 2818572288 | bytes 22000000 | tf_op jit(solution)/shard_map/pallas_call | solution.py:50
  65.5 5.1 %collective-permute-done.15 = bf16[128,1920]{1,0:T(8,128)(2,1)S(1)} collective-permute-done((bf16[128,1920]{1,0:T(8,128)(2,1)S(1)}, bf16[128,1920]{1,0:T(8,128)(2,1)S(1)}, u32[]{:S(2)}, u32[]{:S(2)}) %collective-permute-start.15) | collective-permute-done | bytes 491552 | tf_op jit(solution)/shard_map/ppermute | solution.py:313
  70.6 0.2 add_convert_fusion
  70.8 14.5 %all_to_all.11 = bf16[16,8,1920]{2,1,0:T(8,128)(2,1)S(1)} all-to-all(bf16[16,8,1920]{2,1,0:T(8,128)(2,1)S(1)} %bitcast.24), channel_id=1, replica_groups=mesh['y'=4,'core'=2,'x'=4,'z'=4] {'x','z'}, dimensions={0} | all-to-all | bytes 983040 | tf_op jit(solution)/shard_map/all_to_all | solution.py:337
  85.3 1.2 %shard_map.155 = (bf16[128,896]{1,0:T(8,128)(2,1)}, bf16[128,896]{1,0:T(8,128)(2,1)}, f32[8,128]{1,0:T(8,128)}) custom-call(bf16[128,1920]{1,0:T(8,128)(2,1)S(1)} %bitcast.22, bf16[128,896]{1,0:T(8,128)(2,1)S(1)} %get-tuple-element.130.hidden, bf16[128,128]{1,0:T(8,128)(2,1)S(1)} %get-tuple-element.131.select, ...), custom_call_target="tpu_custom_call" | custom-call | bytes 1000 | tf_op jit(solution)/shard_map/pallas_call | solution.py:50
  (52 shorter events, 1.1 us)
Async XLA Ops:
  21.1 4.9 %copy-start.3 = (bf16[16,8,1920]{2,1,0:T(8,128)(2,1)}, bf16[16,8,1920]{2,1,0:T(8,128)(2,1)S(1)}, u32[]{:S(2)}) copy-start(bf16[16,8,1920]{2,1,0:T(8,128)(2,1)S(1)} %all_to_all.10) | copy-start | bytes 1474564
  21.1 1.9 %collective-permute-start.1 = (bf16[128,1920]{1,0:T(8,128)(2,1)S(1)}, bf16[128,1920]{1,0:T(8,128)(2,1)S(1)}, u32[]{:S(2)}, u32[]{:S(2)}) collective-permute-start(bf16[128,1920]{1,0:T(8,128)(2,1)S(1)} %bitcast.17), channel_id=1, source_target_pairs={{0,16},{16,0},{1,17},{17,1},{2,18},{18,2},{3,19},{19,3},{4,20},{20... | collective-permute-start | bytes 1474568 | tf_op jit(solution)/shard_map/ppermute | solution.py:317
  21.2 8.9 %collective-permute-start = (bf16[128,1920]{1,0:T(8,128)(2,1)S(1)}, bf16[128,1920]{1,0:T(8,128)(2,1)S(1)}, u32[]{:S(2)}, u32[]{:S(2)}) collective-permute-start(bf16[128,1920]{1,0:T(8,128)(2,1)S(1)} %bitcast.18), channel_id=1, source_target_pairs={{0,32},{16,112},{32,0},{48,80},{64,96},{80,48},{96,64},{112,16},{1... | collective-permute-start | bytes 1474568 | tf_op jit(solution)/shard_map/ppermute | solution.py:313
  23.0 3.0 %copy-start.9 = (bf16[128,1920]{1,0:T(8,128)(2,1)}, bf16[128,1920]{1,0:T(8,128)(2,1)S(1)}, u32[]{:S(2)}) copy-start(bf16[128,1920]{1,0:T(8,128)(2,1)S(1)} %collective-permute-done.1.sibling.refs_4_) | copy-start | bytes 1474564
  26.0 11.5 %collective-permute-start.5 = (bf16[128,1920]{1,0:T(8,128)(2,1)S(1)}, bf16[128,1920]{1,0:T(8,128)(2,1)S(1)}, u32[]{:S(2)}, u32[]{:S(2)}) collective-permute-start(bf16[128,1920]{1,0:T(8,128)(2,1)S(1)} %bitcast.20), channel_id=1, source_target_pairs={{0,96},{16,48},{32,64},{48,16},{64,32},{80,112},{96,0},{112,80},{1... | collective-permute-start | bytes 1474568 | tf_op jit(solution)/shard_map/ppermute | solution.py:313
  30.1 7.4 %copy-start.4 = (bf16[128,1920]{1,0:T(8,128)(2,1)}, bf16[128,1920]{1,0:T(8,128)(2,1)S(1)}, u32[]{:S(2)}) copy-start(bf16[128,1920]{1,0:T(8,128)(2,1)S(1)} %collective-permute-done.own.refs_1_) | copy-start | bytes 1474564
  30.1 11.3 %collective-permute-start.2 = (bf16[128,1920]{1,0:T(8,128)(2,1)S(1)}, bf16[128,1920]{1,0:T(8,128)(2,1)S(1)}, u32[]{:S(2)}, u32[]{:S(2)}) collective-permute-start(bf16[128,1920]{1,0:T(8,128)(2,1)S(1)} %collective-permute-done.own.refs_1_), channel_id=1, source_target_pairs={{0,96},{16,48},{32,64},{48,16},{64,32},{80,112},{96,0},{112,80},{1... | collective-permute-start | bytes 1474568 | tf_op jit(solution)/shard_map/ppermute | solution.py:313
  34.1 4.1 %collective-permute-start.3 = (bf16[64,1920]{1,0:T(8,128)(2,1)S(1)}, bf16[64,1920]{1,0:T(8,128)(2,1)S(1)}, u32[]{:S(2)}, u32[]{:S(2)}) collective-permute-start(bf16[64,1920]{1,0:T(8,128)(2,1)S(1)} %get-tuple-element.145), channel_id=1, source_target_pairs={{0,16},{16,0},{1,17},{17,1},{2,18},{18,2},{3,19},{19,3},{4,20},{20... | collective-permute-start | bytes 737288 | tf_op jit(solution)/shard_map/ppermute | solution.py:317
  34.2 5.3 %copy-start = (bf16[1,7168,256]{2,1,0:T(8,128)(2,1)S(1)}, bf16[1,7168,256]{2,1,0:T(8,128)(2,1)}, u32[]{:S(2)}) copy-start(bf16[1,7168,256]{2,1,0:T(8,128)(2,1)} %w_gate.9) | copy-start | bytes 11010052
  34.2 5.3 %copy-start.1 = (bf16[1,7168,256]{2,1,0:T(8,128)(2,1)S(1)}, bf16[1,7168,256]{2,1,0:T(8,128)(2,1)}, u32[]{:S(2)}) copy-start(bf16[1,7168,256]{2,1,0:T(8,128)(2,1)} %w_up.9) | copy-start | bytes 11010052
  34.2 5.3 %copy-start.2 = (bf16[1,256,7168]{2,1,0:T(8,128)(2,1)S(1)}, bf16[1,256,7168]{2,1,0:T(8,128)(2,1)}, u32[]{:S(2)}) copy-start(bf16[1,256,7168]{2,1,0:T(8,128)(2,1)} %w_down.9) | copy-start | bytes 11010052
  34.2 3.9 %collective-permute-start.4 = (bf16[64,1920]{1,0:T(8,128)(2,1)S(1)}, bf16[64,1920]{1,0:T(8,128)(2,1)S(1)}, u32[]{:S(2)}, u32[]{:S(2)}) collective-permute-start(bf16[64,1920]{1,0:T(8,128)(2,1)S(1)} %get-tuple-element.144), channel_id=1, source_target_pairs={{0,16},{16,0},{1,17},{17,1},{2,18},{18,2},{3,19},{19,3},{4,20},{20... | collective-permute-start | bytes 737288 | tf_op jit(solution)/shard_map/ppermute | solution.py:317
  37.5 3.6 %copy-start.5 = (bf16[128,1920]{1,0:T(8,128)(2,1)}, bf16[128,1920]{1,0:T(8,128)(2,1)S(1)}, u32[]{:S(2)}) copy-start(bf16[128,1920]{1,0:T(8,128)(2,1)S(1)} %collective-permute-done.5.second.refs_2_) | copy-start | bytes 1474564
  37.6 1.6 %collective-permute-start.6 = (bf16[64,1920]{1,0:T(8,128)(2,1)S(1)}, bf16[64,1920]{1,0:T(8,128)(2,1)S(1)}, u32[]{:S(2)}, u32[]{:S(2)}) collective-permute-start(bf16[64,1920]{1,0:T(8,128)(2,1)S(1)} %get-tuple-element.143), channel_id=1, source_target_pairs={{0,16},{16,0},{1,17},{17,1},{2,18},{18,2},{3,19},{19,3},{4,20},{20... | collective-permute-start | bytes 737288 | tf_op jit(solution)/shard_map/ppermute | solution.py:317
  37.7 1.9 %collective-permute-start.7 = (bf16[64,1920]{1,0:T(8,128)(2,1)S(1)}, bf16[64,1920]{1,0:T(8,128)(2,1)S(1)}, u32[]{:S(2)}, u32[]{:S(2)}) collective-permute-start(bf16[64,1920]{1,0:T(8,128)(2,1)S(1)} %get-tuple-element.142), channel_id=1, source_target_pairs={{0,16},{16,0},{1,17},{17,1},{2,18},{18,2},{3,19},{19,3},{4,20},{20... | collective-permute-start | bytes 737288 | tf_op jit(solution)/shard_map/ppermute | solution.py:317
  38.2 2.9 %copy-start.12 = (bf16[64,1920]{1,0:T(8,128)(2,1)}, bf16[64,1920]{1,0:T(8,128)(2,1)S(1)}, u32[]{:S(2)}) copy-start(bf16[64,1920]{1,0:T(8,128)(2,1)S(1)} %collective-permute-done.3.first_low.refs_5_) | copy-start | bytes 737284
  38.2 2.9 %copy-start.13 = (bf16[64,1920]{1,0:T(8,128)(2,1)}, bf16[64,1920]{1,0:T(8,128)(2,1)S(1)}, u32[]{:S(2)}) copy-start(bf16[64,1920]{1,0:T(8,128)(2,1)S(1)} %collective-permute-done.4.first_high.refs_6_) | copy-start | bytes 737284
  39.2 1.9 %copy-start.14 = (bf16[64,1920]{1,0:T(8,128)(2,1)}, bf16[64,1920]{1,0:T(8,128)(2,1)S(1)}, u32[]{:S(2)}) copy-start(bf16[64,1920]{1,0:T(8,128)(2,1)S(1)} %collective-permute-done.6.second_low.refs_7_) | copy-start | bytes 737284
  39.5 1.6 %copy-start.15 = (bf16[64,1920]{1,0:T(8,128)(2,1)}, bf16[64,1920]{1,0:T(8,128)(2,1)S(1)}, u32[]{:S(2)}) copy-start(bf16[64,1920]{1,0:T(8,128)(2,1)S(1)} %collective-permute-done.7.second_high.refs_8_) | copy-start | bytes 737284
  41.4 3.9 %copy-start.10 = (bf16[128,1920]{1,0:T(8,128)(2,1)}, bf16[128,1920]{1,0:T(8,128)(2,1)S(1)}, u32[]{:S(2)}) copy-start(bf16[128,1920]{1,0:T(8,128)(2,1)S(1)} %collective-permute-done.2.refs_0_.refs_3_) | copy-start | bytes 1474564
  41.4 1.9 %collective-permute-start.8 = (bf16[128,1920]{1,0:T(8,128)(2,1)S(1)}, bf16[128,1920]{1,0:T(8,128)(2,1)S(1)}, u32[]{:S(2)}, u32[]{:S(2)}) collective-permute-start(bf16[128,1920]{1,0:T(8,128)(2,1)S(1)} %collective-permute-done.2.refs_0_.refs_3_), channel_id=1, source_target_pairs={{0,16},{16,0},{1,17},{17,1},{2,18},{18,2},{3,19},{19,3},{4,20},{20... | collective-permute-start | bytes 1474568 | tf_op jit(solution)/shard_map/ppermute | solution.py:317
  43.3 2.0 %copy-start.11 = (bf16[128,1920]{1,0:T(8,128)(2,1)}, bf16[128,1920]{1,0:T(8,128)(2,1)S(1)}, u32[]{:S(2)}) copy-start(bf16[128,1920]{1,0:T(8,128)(2,1)S(1)} %collective-permute-done.8.refs_1_.refs_9_) | copy-start | bytes 1474564
  45.3 6.8 %copy-start.6 = (bf16[128,256]{1,0:T(8,128)(2,1)}, bf16[128,256]{1,0:T(8,128)(2,1)S(1)}, u32[]{:S(2)}) copy-start(bf16[128,256]{1,0:T(8,128)(2,1)S(1)} %get-tuple-element.104.act.refs_10_) | copy-start | bytes 196612
  45.3 6.8 %copy-start.7 = (bf16[128,256]{1,0:T(8,128)(2,1)}, bf16[128,256]{1,0:T(8,128)(2,1)S(1)}, u32[]{:S(2)}) copy-start(bf16[128,256]{1,0:T(8,128)(2,1)S(1)} %get-tuple-element.105.grad_gate.refs_11_) | copy-start | bytes 196612
  45.3 6.8 %copy-start.8 = (bf16[128,256]{1,0:T(8,128)(2,1)}, bf16[128,256]{1,0:T(8,128)(2,1)S(1)}, u32[]{:S(2)}) copy-start(bf16[128,256]{1,0:T(8,128)(2,1)S(1)} %get-tuple-element.106.grad_up.refs_12_) | copy-start | bytes 196612
  45.4 2.1 %collective-permute-start.9 = (bf16[128,1920]{1,0:T(8,128)(2,1)S(1)}, bf16[128,1920]{1,0:T(8,128)(2,1)S(1)}, u32[]{:S(2)}, u32[]{:S(2)}) collective-permute-start(bf16[128,1920]{1,0:T(8,128)(2,1)S(1)} %get-tuple-element.109), channel_id=1, source_target_pairs={{0,16},{16,0},{1,17},{17,1},{2,18},{18,2},{3,19},{19,3},{4,20},{20... | collective-permute-start | bytes 1474568 | tf_op jit(solution)/shard_map/ppermute | solution.py:317
  47.0 6.9 %collective-permute-start.13 = (bf16[128,1920]{1,0:T(8,128)(2,1)S(1)}, bf16[128,1920]{1,0:T(8,128)(2,1)S(1)}, u32[]{:S(2)}, u32[]{:S(2)}) collective-permute-start(bf16[128,1920]{1,0:T(8,128)(2,1)S(1)} %get-tuple-element.117), channel_id=1, source_target_pairs={{0,16},{16,0},{1,17},{17,1},{2,18},{18,2},{3,19},{19,3},{4,20},{20... | collective-permute-start | bytes 1474568 | tf_op jit(solution)/shard_map/ppermute | solution.py:317
  47.5 10.1 %collective-permute-start.12 = (bf16[128,1920]{1,0:T(8,128)(2,1)S(1)}, bf16[128,1920]{1,0:T(8,128)(2,1)S(1)}, u32[]{:S(2)}, u32[]{:S(2)}) collective-permute-start(bf16[128,1920]{1,0:T(8,128)(2,1)S(1)} %add_convert_fusion.5), channel_id=1, source_target_pairs={{0,96},{16,48},{32,64},{48,16},{64,32},{80,112},{96,0},{112,80},{1... | collective-permute-start | bytes 1474568 | tf_op jit(solution)/shard_map/ppermute | solution.py:313
  52.0 5.6 %collective-permute-start.11 = (bf16[128,1920]{1,0:T(8,128)(2,1)S(1)}, bf16[128,1920]{1,0:T(8,128)(2,1)S(1)}, u32[]{:S(2)}, u32[]{:S(2)}) collective-permute-start(bf16[128,1920]{1,0:T(8,128)(2,1)S(1)} %get-tuple-element.114), channel_id=1, source_target_pairs={{0,16},{16,0},{1,17},{17,1},{2,18},{18,2},{3,19},{19,3},{4,20},{20... | collective-permute-start | bytes 1474568 | tf_op jit(solution)/shard_map/ppermute | solution.py:317
  55.0 10.5 %collective-permute-start.10 = (bf16[128,1920]{1,0:T(8,128)(2,1)S(1)}, bf16[128,1920]{1,0:T(8,128)(2,1)S(1)}, u32[]{:S(2)}, u32[]{:S(2)}) collective-permute-start(bf16[128,1920]{1,0:T(8,128)(2,1)S(1)} %get-tuple-element.112), channel_id=1, source_target_pairs={{0,16},{16,0},{1,17},{17,1},{2,18},{18,2},{3,19},{19,3},{4,20},{20... | collective-permute-start | bytes 1474568 | tf_op jit(solution)/shard_map/ppermute | solution.py:317
  55.5 15.1 %collective-permute-start.15 = (bf16[128,1920]{1,0:T(8,128)(2,1)S(1)}, bf16[128,1920]{1,0:T(8,128)(2,1)S(1)}, u32[]{:S(2)}, u32[]{:S(2)}) collective-permute-start(bf16[128,1920]{1,0:T(8,128)(2,1)S(1)} %add_convert_fusion.2), channel_id=1, source_target_pairs={{0,96},{16,48},{32,64},{48,16},{64,32},{80,112},{96,0},{112,80},{1... | collective-permute-start | bytes 1474568 | tf_op jit(solution)/shard_map/ppermute | solution.py:313
  57.8 12.7 %collective-permute-start.14 = (bf16[128,1920]{1,0:T(8,128)(2,1)S(1)}, bf16[128,1920]{1,0:T(8,128)(2,1)S(1)}, u32[]{:S(2)}, u32[]{:S(2)}) collective-permute-start(bf16[128,1920]{1,0:T(8,128)(2,1)S(1)} %add_convert_fusion.1), channel_id=1, source_target_pairs={{0,32},{16,112},{32,0},{48,80},{64,96},{80,48},{96,64},{112,16},{1... | collective-permute-start | bytes 1474568 | tf_op jit(solution)/shard_map/ppermute | solution.py:313
